TPU v7x, 32 devices: a whole 2x2x4 slice. The times are simulated.
32 devices in a mesh: groups: 2 (over y), pool: 4 (over z), tensor: 4 (over x, core).
Axes of the slice: x: 2, y: 2, z: 4, core: 2. Of those that a mesh axis runs over, the one named last changes fastest.
Arguments:
- hidden: bfloat16 [128, 2, 8192], P(('groups', 'pool')), parts along dimension 0, may hold values from -6 to 6
- queries: bfloat16 [128, 2, 64, 128], P(('groups', 'pool'), None, 'tensor'), parts along dimension 0, may hold values from -110 to 110
- cache: bfloat16 [128, 256, 8, 256], P(('groups', 'pool'), None, 'tensor'), parts along dimension 0, may hold values from -4 to 4
- key_value_weight: bfloat16 [8192, 8, 256], P('pool', 'tensor'), may hold values from -0.0625 to 0.0625
- adapter_down_weight: bfloat16 [24, 8192, 128], P('tensor', 'pool'), may hold values from -0.0625 to 0.0625
- adapter_up_key: bfloat16 [24, 64, 8, 128], P('pool', None, 'tensor'), may hold values from -0.75 to 0.75
- adapter_up_value: bfloat16 [24, 64, 8, 128], P('pool', None, 'tensor'), may hold values from -0.75 to 0.75
- request_adapter: int32 [128], P(('groups', 'pool')), parts along dimension 0, may hold values from 0 to 23
- adapter_storage: int32 [24], replicated, may hold values from 0 to 23, each once
- lengths: int32 [128], P(('groups', 'pool')), parts along dimension 0, may hold values from 1 to 256, 10240 in all
Outputs:
- attended: bfloat16 [128, 2, 8192], P(('groups', 'pool'), None, 'tensor'), parts along dimension 0
- fresh_key_value: bfloat16 [128, 2, 8, 256], P(('groups', 'pool'), None, 'tensor'), parts along dimension 0
There are 2 independent parts, one for each index of `groups`. A program takes and returns all parts, laid end to end along the dimension named above; an argument that names none is the same for every part. Nothing has to cross between parts.
Inputs may be any that keep to these rules, and one draw needn't show every extreme that they name: `adapter_storage`: each slot from 0 to 23 holds exactly one adapter.
All inputs are finite; a program needn't handle non-finite values. No bound on the sum of `lengths` on one device may be relied on, other than what follows from the above.
Results may differ from a plain program's by a relative error of at most 0.0052.
Values may be sent and summed in bfloat16 or wider, within the bound.
No kernel may reach another device: no remote copies, remote signals or barrier semaphores. Data moves between devices by JAX's collectives and lax.ppermute only.
A program may use at most 64 MiB of HBM per device.

v0:
```python
import jax
import jax.numpy as jnp
from jax import lax
from jax.sharding import PartitionSpec as P

ADAPTER_SCALE = 0.5


def attend(queries, cache, fresh_key_value, lengths):
    rows, steps_new, heads, head_dim = queries.shape
    kv_count = cache.shape[2]
    depth = cache.shape[1]
    group = heads // kv_count
    keys = jnp.concatenate([cache[..., :head_dim], fresh_key_value[..., :head_dim]], axis=1)
    values = jnp.concatenate([cache[..., head_dim:], fresh_key_value[..., head_dim:]], axis=1)
    grouped = queries.reshape(rows, steps_new, kv_count, group, head_dim)
    scores = jnp.einsum(
        "rnkgd,rpkd->rnkgp", grouped, keys, preferred_element_type=jnp.float32
    ) * head_dim ** (-0.5)
    places = jnp.arange(depth + steps_new, dtype=jnp.int32)
    turns = jnp.arange(steps_new, dtype=jnp.int32)
    valid = jnp.where(
        places[None, None, :] < depth,
        places[None, None, :] < lengths[:, None, None],
        places[None, None, :] - depth <= turns[None, :, None],
    )
    scores = jnp.where(valid[:, :, None, None, :], scores, -1e30)
    weights = jax.nn.softmax(scores, axis=-1).astype(jnp.bfloat16)
    mixed = jnp.einsum("rnkgp,rpke->rnkge", weights, values, preferred_element_type=jnp.float32)
    return mixed.reshape(rows, steps_new, heads * head_dim).astype(jnp.bfloat16)


def expanded_update(reduced_input, owner_select, key_up_matrix, value_up_matrix):
    count = reduced_input.shape[0]
    holders, rank, kv_local, head_dim = key_up_matrix.shape
    spread_key = (owner_select[:, :, None] * reduced_input[:, None, :rank]).reshape(
        count, holders * rank
    )
    spread_value = (owner_select[:, :, None] * reduced_input[:, None, rank:]).reshape(
        count, holders * rank
    )
    delta_key = jnp.dot(
        spread_key,
        key_up_matrix.reshape(holders * rank, kv_local * head_dim),
        preferred_element_type=jnp.float32,
    )
    delta_value = jnp.dot(
        spread_value,
        value_up_matrix.reshape(holders * rank, kv_local * head_dim),
        preferred_element_type=jnp.float32,
    )
    joined = jnp.concatenate(
        [
            delta_key.reshape(count, kv_local, head_dim),
            delta_value.reshape(count, kv_local, head_dim),
        ],
        axis=2,
    )
    return joined.reshape(count, kv_local * 2 * head_dim)


def owned_reduced(flattened_rows, adapter_down_weight, owned_down):
    down_by_storage, owned_width, paired_rank = adapter_down_weight.shape
    group_key = jnp.where(
        (owned_down >= 0) & (owned_down < down_by_storage), owned_down, down_by_storage
    )
    order = jnp.argsort(group_key, stable=True)
    inverse = jnp.argsort(order, stable=True)
    sorted_rows = flattened_rows[order]
    group_sizes = jnp.sum(
        (group_key[:, None] == jnp.arange(down_by_storage + 1, dtype=jnp.int32)[None, :]).astype(
            jnp.int32
        ),
        axis=0,
    )
    padded_down = jnp.concatenate(
        [adapter_down_weight, jnp.zeros((1, owned_width, paired_rank), adapter_down_weight.dtype)],
        axis=0,
    )
    sorted_out = lax.ragged_dot(
        sorted_rows, padded_down, group_sizes, preferred_element_type=jnp.float32
    )
    return sorted_out[inverse]


def body(
    hidden,
    queries,
    cache,
    key_value_weight,
    adapter_down_weight,
    adapter_up_key,
    adapter_up_value,
    request_adapter,
    adapter_storage,
    lengths,
):
    rows_dev, steps_new, width = hidden.shape
    total_rows = rows_dev * lax.axis_size("pool")
    down_by_storage = adapter_down_weight.shape[0]
    up_by_storage = adapter_up_key.shape[0]
    kv_local = key_value_weight.shape[1]
    pair_width = key_value_weight.shape[2]
    table_size = adapter_storage.shape[0]
    table_index = jnp.arange(table_size, dtype=jnp.int32)
    slot_own = jnp.sum(
        jnp.where(request_adapter[:, None] == table_index[None, :], adapter_storage[None, :], 0),
        axis=1,
    )
    all_slots = lax.all_gather(slot_own, "pool", axis=0, tiled=True)
    spread = lax.all_to_all(hidden, "pool", split_axis=2, concat_axis=0, tiled=True)
    flattened_rows = spread.reshape(total_rows * steps_new, spread.shape[2])
    base_part = jnp.dot(
        flattened_rows,
        key_value_weight.reshape(spread.shape[2], kv_local * pair_width),
        preferred_element_type=jnp.float32,
    )
    owned_down = jnp.repeat(all_slots - lax.axis_index("tensor") * down_by_storage, steps_new)
    reduced_portion = owned_reduced(flattened_rows, adapter_down_weight, owned_down)
    reduced_input = lax.psum(reduced_portion, ("pool", "tensor")).astype(jnp.bfloat16)
    local_up = jnp.repeat(all_slots - lax.axis_index("pool") * up_by_storage, steps_new)
    owner_select = (
        local_up[:, None] == jnp.arange(up_by_storage, dtype=jnp.int32)[None, :]
    ).astype(jnp.bfloat16)
    adapter_update = expanded_update(reduced_input, owner_select, adapter_up_key, adapter_up_value)
    base_owned = lax.psum_scatter(base_part, "pool", scatter_dimension=0, tiled=True)
    update_owned = lax.psum_scatter(adapter_update, "pool", scatter_dimension=0, tiled=True)
    combined_output = base_owned + ADAPTER_SCALE * update_owned
    fresh_key_value = combined_output.astype(jnp.bfloat16).reshape(
        rows_dev, steps_new, kv_local, pair_width
    )
    attended = attend(queries, cache, fresh_key_value, lengths)
    return (attended, fresh_key_value)


def solution(mesh):
    return jax.shard_map(
        body,
        mesh=mesh,
        in_specs=(
            P(("groups", "pool"), None, None),
            P(("groups", "pool"), None, "tensor", None),
            P(("groups", "pool"), None, "tensor", None),
            P("pool", "tensor", None),
            P("tensor", "pool", None),
            P("pool", None, "tensor", None),
            P("pool", None, "tensor", None),
            P(("groups", "pool")),
            P(),
            P(("groups", "pool")),
        ),
        out_specs=(
            P(("groups", "pool"), None, "tensor"),
            P(("groups", "pool"), None, "tensor", None),
        ),
        check_vma=False,
    )
```

profile of v0, /device:TPU:0, one launch (start us, length us, event | category | flops | bytes accessed | tf_op | source)
XLA Modules:
  0.0 197.8 jit_solution(8604177634980358357)
XLA Ops:
  7.2 9.0 %copy.69 = bf16[16,2,8192]{0,1,2:T(2,128)(2,1)} copy(bf16[16,2,8192]{2,1,0:T(2,128)(2,1)} %param.10) | data formatting | bytes 1048576 | tf_op args[0]
  16.2 6.6 %reshape.198 = bf16[4,2,32768]{2,1,0:T(2,128)(2,1)} reshape(bf16[8192,2,16]{2,1,0:T(2,128)(2,1)} %bitcast.84) | data formatting | bytes 1048576
  22.8 6.3 %all-to-all-start = ((bf16[4,2,32768]{2,1,0:T(2,128)(2,1)}), bf16[4,2,32768]{2,1,0:T(2,128)(2,1)}, u32[]{:S(2)}, u32[]{:S(2)}) async-start(bf16[4,2,32768]{2,1,0:T(2,128)(2,1)} %reshape.198), calls=%async_computation | async-start | bytes 1048576 | tf_op jit(solution)/shard_map/all_to_all | solution.py:111
  30.8 13.2 %all-reduce.1 = s32[64]{0:T(128)S(1)} all-reduce(s32[64]{0:T(128)S(1)} %dynamic-update-slice), channel_id=1, replica_groups=mesh['groups'=2,'pool'=4,'tensor'=4] {'pool'}, use_global_device_ids=true, to_apply=%add.1 | all-reduce | flops 64 | bytes 512
  44.9 1.4 ragged-dot-metadata
  46.4 2.5 %sort.31 = (s32[128]{0:T(128)}, s32[128]{0:T(128)S(1)}) sort(s32[128]{0:T(128)S(1)} %and_select_fusion, s32[128]{0:T(128)S(1)} %iota.44), dimensions={0}, to_apply=%region_2.3 | sort | flops 896 | bytes 2048 | tf_op jit(solution)/shard_map/jit(argsort)/sort | solution.py:67
  49.0 2.5 %sort.32 = (s32[128]{0:T(128)}, s32[128]{0:T(128)S(1)}) sort(s32[128]{0:T(128)S(1)} %get-tuple-element.4, s32[128]{0:T(128)S(1)} %iota.45), dimensions={0}, to_apply=%region_4.5 | sort | flops 896 | bytes 2048 | tf_op jit(solution)/shard_map/jit(argsort)/sort | solution.py:68
  51.7 1.0 copy.111
  55.3 2.1 %concatenate.12 = bf16[7,2048,128]{2,1,0:T(8,128)(2,1)} pad(bf16[6,2048,128]{2,1,0:T(8,128)(2,1)S(1)} %copy-done.3, bf16[]{:T(256)} %constant.7.clone.1), padding=0_1x0_0x0_0 | pad | bytes 6815746 | tf_op jit(solution)/shard_map/concatenate | solution.py:76
  57.4 1.4 copy-done.2
  58.8 3.8 %fusion.28 = (bf16[16,256,2,128]{3,2,1,0:T(2,128)(2,1)}, bf16[16,256,2,128]{3,2,1,0:T(2,128)(2,1)S(1)}) fusion(bf16[16,256,2,256]{3,2,1,0:T(2,128)(2,1)S(1)} %copy-done.2), kind=kLoop, calls=%fused_computation.51 | loop fusion | bytes 8388608 | tf_op jit(solution)/shard_map/slice | solution.py:14
  62.6 5.4 %reshape.199 = bf16[8192,2,16]{2,1,0:T(2,128)(2,1)} reshape(bf16[4,2,32768]{2,1,0:T(2,128)(2,1)} %all-to-all-done) | data formatting | bytes 1048576
  68.0 9.6 %copy.70 = bf16[16,2,4,2048]{3,1,0,2:T(2,128)(2,1)S(1)} copy(bf16[16,2,4,2048]{0,1,3,2:T(2,128)(2,1)} %bitcast.83) | data formatting | bytes 1048576 | tf_op jit(solution)/shard_map/all_to_all | solution.py:111
  77.8 1.7 gather_fusion
  79.5 7.3 %ragged-dot-none = f32[128,128]{1,0:T(8,128)} custom-call(s32[1]{0:T(128)} %get-tuple-element.6, s32[8]{0:T(128)} %get-tuple-element.7, s32[7]{0:T(128)} %get-tuple-element.8, s32[7]{0:T(128)} %get-tuple-element.9, s32[1]{0:T(128)} %get-tuple-element.6, bf16[128,2048]{1,0:T(8,128)(2,1)} %gather_fusion, bf16[7,2048,128]{2,1,0:T(8,128)(2,1)} %concatenate.12), custom_call_target="tpu_custom_call" | custom-call | flops 67108864 | bytes 4259868 | tf_op jit(solution)/shard_map/ragged_dot_general/ragged-dot-none
  86.8 1.5 gather_fusion.1
  88.3 57.7 %psum.7 = bf16[128,128]{1,0:T(8,128)(2,1)S(1)} all-reduce(f32[128,128]{1,0:T(8,128)S(1)} %gather_fusion.1), channel_id=1, replica_groups=mesh['groups'=2,'pool'=4,'tensor'=4] {'pool','tensor'}, use_global_device_ids=true, to_apply=%region_5.6 | all-reduce | flops 16384 | bytes 98304 | tf_op jit(solution)/shard_map/psum | solution.py:120
  147.7 2.2 %copy.97 = bf16[256,8,2,256]{3,1,2,0:T(8,128)(2,1)S(1)} copy(bf16[256,8,2,256]{3,2,1,0:T(2,128)(2,1)} %bitcast.87) | data formatting | bytes 4194304
  149.9 1.8 copy.95
  151.7 1.9 copy.93
  153.5 1.2 fusion.34
  154.9 10.7 %reduce-scatter.5.cloned.1.call-done = f32[32,512]{1,0:T(8,128)} async-done(((f32[128,512]{1,0:T(8,128)}), f32[32,512]{1,0:T(8,128)}) %reduce-scatter.5.cloned.1.call-update) | async-done | bytes 65552 | tf_op jit(solution)/shard_map/reduce_scatter | solution.py:127
  165.6 20.4 %reduce-scatter.3.cloned.1.call-done = f32[32,512]{1,0:T(8,128)} async-done(((f32[128,512]{1,0:T(8,128)}), f32[32,512]{1,0:T(8,128)}) %reduce-scatter.3.cloned.1.call-update) | async-done | bytes 65552 | tf_op jit(solution)/shard_map/reduce_scatter | solution.py:126
  187.0 2.6 %fusion.31 = (f32[16,2,2,8]{3,1,2,0:T(2,128)S(1)}, f32[16,2,2,8,258]{4,3,1,2,0:T(8,128)S(1)}) fusion(bf16[16,2,2,128]{3,1,2,0:T(2,128)(2,1)S(1)} %copy.96, bf16[16,256,2,128]{3,1,2,0:T(8,128)(2,1)} %copy.95, pred[16,2,258]{2,1,0:T(4,128)(4,1)S(1)} %broadcast_select_fusion, bf16[16,2,16,128]{3,2,1,0:T(8,128)(2,1)S(1)} %copy-done), kind=kOutput, calls=%fused_computation.54 | convolution fusion | flops 38572288 | bytes 2783296 | tf_op jit(solution)/shard_map/sub | solution.py:28
  (71 shorter events, 8.9 us)
Async XLA Ops:
  7.2 179.8 %copy-start = (bf16[16,2,16,128]{3,2,1,0:T(8,128)(2,1)S(1)}, bf16[16,2,16,128]{3,2,1,0:T(8,128)(2,1)}, u32[]{:S(2)}) copy-start(bf16[16,2,16,128]{3,2,1,0:T(8,128)(2,1)} %param.11) | copy-start | bytes 393220
  16.2 12.9 %copy-start.11 = (u32[32]{0:T(128)S(1)}, u32[32]{0:T(128)}, u32[]{:S(2)}) copy-start(u32[32]{0:T(128)} %constant.41) | copy-start | bytes 388
  16.2 14.2 %copy-start.9 = (s32[24]{0:T(128)S(1)}, s32[24]{0:T(128)}, u32[]{:S(2)}) copy-start(s32[24]{0:T(128)} %param.18) | copy-start | bytes 292
  16.2 14.2 %copy-start.10 = (s32[16]{0:T(128)S(1)}, s32[16]{0:T(128)}, u32[]{:S(2)}) copy-start(s32[16]{0:T(128)} %param.17) | copy-start | bytes 196
  16.2 39.1 %copy-start.3 = (bf16[6,2048,128]{2,1,0:T(8,128)(2,1)S(1)}, bf16[6,2048,128]{2,1,0:T(8,128)(2,1)}, u32[]{:S(2)}) copy-start(bf16[6,2048,128]{2,1,0:T(8,128)(2,1)} %param.14) | copy-start | bytes 9437188
  22.8 39.8 %all-to-all-start = ((bf16[4,2,32768]{2,1,0:T(2,128)(2,1)}), bf16[4,2,32768]{2,1,0:T(2,128)(2,1)}, u32[]{:S(2)}, u32[]{:S(2)}) async-start(bf16[4,2,32768]{2,1,0:T(2,128)(2,1)} %reshape.198), calls=%async_computation | async-start | bytes 1048576 | tf_op jit(solution)/shard_map/all_to_all | solution.py:111
  29.1 136.5 %reduce-scatter.5.cloned.1.call-start = ((), (), s32[]{:S(2)}) async-start(), calls=%async_computation.4 | async-start | bytes 327680 | tf_op jit(solution)/shard_map/reduce_scatter | solution.py:127
  55.3 3.5 %copy-start.2 = (bf16[16,256,2,256]{3,2,1,0:T(2,128)(2,1)S(1)}, bf16[16,256,2,256]{3,2,1,0:T(2,128)(2,1)}, u32[]{:S(2)}) copy-start(bf16[16,256,2,256]{3,2,1,0:T(2,128)(2,1)} %param.12) | copy-start | bytes 12582916
  79.5 66.7 %copy-start.6 = (bf16[256,384]{1,0:T(8,128)(2,1)S(1)}, bf16[256,384]{1,0:T(8,128)(2,1)}, u32[]{:S(2)}) copy-start(bf16[256,384]{1,0:T(8,128)(2,1)} %copy.72) | copy-start | bytes 589828
  79.5 67.0 %copy-start.5 = (bf16[256,384]{1,0:T(8,128)(2,1)S(1)}, bf16[256,384]{1,0:T(8,128)(2,1)}, u32[]{:S(2)}) copy-start(bf16[256,384]{1,0:T(8,128)(2,1)} %copy.75) | copy-start | bytes 589828
  147.6 38.4 %reduce-scatter.3.cloned.1.call-start = ((), (), s32[]{:S(2)}) async-start(), calls=%async_computation.3 | async-start | bytes 327680 | tf_op jit(solution)/shard_map/reduce_scatter | solution.py:126
  147.7 2.2 %copy-start.1 = (bf16[16,256,2,128]{3,2,1,0:T(2,128)(2,1)S(1)}, bf16[16,256,2,128]{3,2,1,0:T(2,128)(2,1)}, u32[]{:S(2)}) copy-start(bf16[16,256,2,128]{3,2,1,0:T(2,128)(2,1)} %get-tuple-element.18) | copy-start | bytes 6291460
  153.5 1.2 copy-start.8
  186.9 2.8 %copy-start.7 = (bf16[16,2,2,256]{3,2,1,0:T(2,128)(2,1)}, bf16[16,2,2,256]{3,2,1,0:T(2,128)(2,1)S(1)}, u32[]{:S(2)}) copy-start(bf16[16,2,2,256]{3,2,1,0:T(2,128)(2,1)S(1)} %reshape.168) | copy-start | bytes 98308
  187.0 2.7 %copy-start.4 = (bf16[16,256,2,128]{3,1,2,0:T(8,128)(2,1)S(1)}, bf16[16,256,2,128]{3,1,2,0:T(8,128)(2,1)}, u32[]{:S(2)}) copy-start(bf16[16,256,2,128]{3,1,2,0:T(8,128)(2,1)} %copy.93) | copy-start | bytes 6291460
Sparse Core Ops, SparseCore 0:
  147.7 17.8 reduce-scatter.4
  168.0 17.9 reduce-scatter.2
where the time goes:
time: 199 us; the launch traced here: 198 us
  blocking collectives  70.9 us (36%)
  local copies, waits for them, and re-layouts  53.9 us (27%)
  waiting for transfers between devices  31.1 us (16%)
  between operations  15 us (8%)
  Pallas kernels  8.71 us (4%)
  other arithmetic  6.98 us (4%)
  starting transfers between devices  6.36 us (3%)
  matrix products  4.77 us (2%)
    psum x1, blocking collectives, body(): lax.psum(reduced_portion, ('pool', 'tensor')).astype(jnp.bfloat16)  57.7 us
    unnamed x39, local copies, waits for them, and re-layouts  31.8 us
    reduce_scatter x1, waiting for transfers between devices, body(): lax.psum_scatter(base_part, 'pool', scatter_dimension=0, tiled=True)  20.4 us
    unnamed x1, blocking collectives  13.2 us
    reduce_scatter x1, waiting for transfers between devices, body(): lax.psum_scatter(adapter_update, 'pool', scatter_dimension=0, tiled=True)  10.7 us
    all_to_all x1, local copies, waits for them, and re-layouts, body(): lax.all_to_all(hidden, 'pool', split_axis=2, concat_axis=0, tiled=True)  9.59 us
    another operation x1, Pallas kernels  7.26 us
    all_to_all x1, starting transfers between devices, body(): lax.all_to_all(hidden, 'pool', split_axis=2, concat_axis=0, tiled=True)  6.32 us
  transfers between devices with their start and end apart: 3, of which 2 were waited for; matrix products, arithmetic and copies ran while one was open for 12% of the time, Pallas kernels for 1%

commit v1 on v0

v1 whole, which is shorter than its diff:
```python
import functools
import jax
import jax.numpy as jnp
from jax import lax
from jax.experimental import pallas as pl
from jax.experimental.pallas import tpu as pltpu
from jax.sharding import PartitionSpec as P

ADAPTER_SCALE = 0.5
LANES = 128
F32 = jnp.float32
BF16 = jnp.bfloat16
VMEM = pl.BlockSpec(memory_space=pltpu.VMEM)
SMEM = pl.BlockSpec(memory_space=pltpu.SMEM)
HIGH = 100 * 1024 * 1024 // 2


def dot(a, b):
    return jnp.dot(a, b, preferred_element_type=F32)


def dot_t(a, b):
    return lax.dot_general(a, b, (((1,), (1,)), ((), ())), preferred_element_type=F32)


def struct(shape, dtype):
    return jax.ShapeDtypeStruct(shape, dtype)


def cost(flops, moved):
    return pl.CostEstimate(flops=int(flops), bytes_accessed=int(moved), transcendentals=0)


def pack_kernel(pool, parts, place, request_adapter, adapter_storage, hidden, *outs):
    rows, steps_new, width = hidden.shape
    count = rows * steps_new
    part = width // pool
    half = part // parts
    me, side = place[0], place[1]
    row = lax.broadcasted_iota(jnp.int32, (count, LANES), 0) // steps_new
    slots = jnp.zeros((count, LANES), jnp.int32)
    for r in range(rows):
        slots = jnp.where(row == r, adapter_storage[request_adapter[r]], slots)
    slots = slots.astype(F32).astype(BF16)
    for k in range(pool):
        start = (me ^ k) * part
        mine = pl.multiple_of(start + side * half, LANES)
        outs[k][:, :half] = hidden[:, :, pl.ds(mine, half)].reshape(count, half)
        outs[k][:, half:] = slots
    if parts == 2:
        other = pl.multiple_of(me * part + (1 - side) * half, LANES)
        outs[pool][...] = hidden[:, :, pl.ds(other, half)].reshape(count, half)


def project_kernel(pool, parts, place, *refs):
    chunks, refs = refs[:pool], refs[pool:]
    if parts == 2:
        own_other, swapped, refs = refs[0], refs[1:pool], refs[pool:]
    weight, down, base, slots_out, shrink = refs
    me, side, first_slot = place[0], place[1], place[2]
    count = chunks[0].shape[0]
    half = chunks[0].shape[1] - LANES
    kv_local = weight.shape[0]
    sides = [(side * half, jnp.concatenate([c[:, :half] for c in chunks], axis=0))]
    if parts == 2:
        rest = [own_other[...]] + [c[:, :half] for c in swapped]
        sides.append(((1 - side) * half, jnp.concatenate(rest, axis=0)))
    slots = jnp.concatenate([c[:, half:] for c in chunks], axis=0)
    slots_out[...] = slots
    slots = slots.astype(F32)
    step = 2 if down.shape[0] % 2 == 0 else 1
    total = jnp.zeros((count * pool, LANES), F32)
    for a in range(0, down.shape[0], step):
        out = 0.0
        for start, x in sides:
            at = pl.ds(pl.multiple_of(start, half), half)
            out += dot(x, jnp.concatenate([down[a + i, at, :] for i in range(step)], axis=1))
        for i in range(step):
            match = slots == (first_slot + a + i).astype(F32)
            total = jnp.where(match, out[:, i * LANES:(i + 1) * LANES], total)
    total = total.astype(BF16)
    for k in range(pool):
        at = pl.ds(pl.multiple_of((me ^ k) * count, count), count)
        shrink[at, :] = total[k * count:(k + 1) * count]
    for k in range(kv_local):
        out = 0.0
        for start, x in sides:
            at = pl.ds(pl.multiple_of(start, half), half)
            out += dot(x, weight[k, at, :])
        base[:, k * weight.shape[2]:(k + 1) * weight.shape[2]] = out


def expand_kernel(pool, parts, place, *refs):
    sums, refs = refs[:parts], refs[parts:]
    slots_in, base, up_key, up_value = refs[:4]
    outs, scratch = refs[4:4 + pool], refs[4 + pool]
    me, first_slot = place[0], place[3]
    holders, rank, kv_local, size = up_key.shape
    count = base.shape[0] // pool
    total = sums[0][...]
    for s in sums[1:]:
        total = total + s[...]
    scratch[...] = total
    ordered = jnp.concatenate(
        [scratch[pl.ds(pl.multiple_of((me ^ k) * count, count), count), :] for k in range(pool)], axis=0
    ).astype(BF16)
    slots = slots_in[...].astype(F32)
    deep = rank * kv_local
    for which, up in ((0, up_key), (1, up_value)):
        row = lax.broadcasted_iota(jnp.int32, (2 * rank, deep), 0)
        col = lax.broadcasted_iota(jnp.int32, (2 * rank, deep), 1)
        wide = []
        for k in range(kv_local):
            pick = (row == which * rank + col // kv_local) & (col % kv_local == k)
            wide.append(dot(ordered, pick.astype(F32).astype(BF16)))
        acc = [jnp.zeros((base.shape[0], size), F32) for _ in range(kv_local)]
        for a in range(holders):
            match = slots == (first_slot + a).astype(F32)
            if deep != LANES:
                match = match[:, :1]
            table = up[a].reshape(deep, size)
            for k in range(kv_local):
                acc[k] = acc[k] + dot(jnp.where(match, wide[k], 0.0).astype(BF16), table)
        for k in range(kv_local):
            at = slice((2 * k + which) * size, (2 * k + which + 1) * size)
            value = base[:, at] + ADAPTER_SCALE * acc[k]
            outs[0][:, at] = value[:count]
            for j in range(1, pool):
                outs[j][:, at] = value[j * count:(j + 1) * count].astype(BF16)


def cache_kernel(rows_step, lengths, queries, cache, acc_out, stat_out):
    _, steps_new, heads, size = queries.shape
    depth, kv_local = cache.shape[1], cache.shape[2]
    count = steps_new * heads
    group = heads // kv_local
    scale = size ** -0.5
    col = lax.broadcasted_iota(jnp.int32, (count, depth * kv_local), 1)
    row = lax.broadcasted_iota(jnp.int32, (count, depth * kv_local), 0)
    same = col % kv_local == row % heads // group
    lane = lax.broadcasted_iota(jnp.int32, (count, LANES), 1)
    for i in range(rows_step):
        r = pl.program_id(0) * rows_step + i
        q = queries[i].reshape(count, size)
        both = cache[i].reshape(depth * kv_local, 2 * size)
        scores = dot_t(q, both[:, :size]) * scale
        scores = jnp.where(same & (col < lengths[r] * kv_local), scores, -1e30)
        top = jnp.max(scores, axis=1, keepdims=True)
        weights = jnp.exp(scores - top)
        total = jnp.sum(weights, axis=1, keepdims=True)
        at = pl.ds(i * count, count)
        acc_out[at, :] = dot(weights.astype(BF16), both[:, size:])
        stat_out[at, :] = jnp.where(lane == 0, top, total)


def finish_kernel(pool, own, *refs):
    parts, refs = refs[:pool - 1], refs[pool - 1:]
    queries, acc_in, stat_in, attended, fresh_out, scratch = refs
    rows, steps_new, heads, size = queries.shape
    count = rows * steps_new
    kv_local = own.shape[1] // (2 * size)
    group = heads // kv_local
    total = own[...]
    for part in parts:
        total = total + part[...].astype(F32)
    fresh = total.astype(BF16)
    fresh_out[...] = fresh
    keys = jnp.concatenate([fresh[:, 2 * k * size:(2 * k + 1) * size] for k in range(kv_local)], axis=0)
    values = jnp.concatenate([fresh[:, (2 * k + 1) * size:(2 * k + 2) * size] for k in range(kv_local)], axis=0)
    scores = dot_t(queries[...].reshape(count * heads, size), keys) * size ** -0.5
    col = lax.broadcasted_iota(jnp.int32, scores.shape, 1)
    row = lax.broadcasted_iota(jnp.int32, scores.shape, 0)
    token, other = row // heads, col % count
    valid = (
        (token // steps_new == other // steps_new)
        & (other <= token)
        & (row % heads // group == col // count)
    )
    scores = jnp.where(valid, scores, -1e30)
    stat = stat_in[...]
    top_before, total_before = stat[:, :1], stat[:, 1:2]
    top = jnp.maximum(top_before, jnp.max(scores, axis=1, keepdims=True))
    weights = jnp.exp(scores - top)
    keep = jnp.exp(top_before - top)
    norm = 1.0 / (total_before * keep + jnp.sum(weights, axis=1, keepdims=True))
    mixed = acc_in[...] * keep + dot(weights.astype(BF16), values)
    scratch[...] = mixed * norm
    for h in range(heads):
        attended[:, h * size:(h + 1) * size] = scratch[pl.ds(h, count, stride=heads), :].astype(BF16)


def body(
    hidden,
    queries,
    cache,
    key_value_weight,
    adapter_down_weight,
    adapter_up_key,
    adapter_up_value,
    request_adapter,
    adapter_storage,
    lengths,
):
    pool, tensor = lax.axis_size("pool"), lax.axis_size("tensor")
    p, t = lax.axis_index("pool"), lax.axis_index("tensor")
    rows, steps_new, width = hidden.shape
    count = rows * steps_new
    part = width // pool
    down_here, up_here = adapter_down_weight.shape[0], adapter_up_key.shape[0]
    _, kv_local, pair = key_value_weight.shape
    heads, size = queries.shape[2:]
    assert adapter_storage.shape[0] <= 256 and pool & (pool - 1) == 0 and tensor & (tensor - 1) == 0
    assert pool % tensor == 0 and down_here == up_here * (pool // tensor)
    parts = 2 if tensor % 2 == 0 else 1
    half = part // parts
    side = t % parts
    place = jnp.stack([p, side, t * down_here, p * up_here]).astype(jnp.int32)

    def over_pool(x, k):
        return lax.ppermute(x, "pool", [(i, i ^ k) for i in range(pool)])

    def over_pair(x):
        return lax.ppermute(x, "tensor", [(i, i ^ 1) for i in range(tensor)])

    chunk = struct((count, half + LANES), BF16)
    packed = pl.pallas_call(
        functools.partial(pack_kernel, pool, parts),
        out_shape=[chunk] * pool + [struct((count, half), BF16)] * (parts - 1),
        in_specs=[SMEM, SMEM, SMEM, VMEM],
        out_specs=[VMEM] * (pool + parts - 1),
        name="pack",
        cost_estimate=cost(0, 2 * hidden.size * 2),
    )(place, request_adapter, adapter_storage, hidden)
    chunks = [packed[0]] + [None] * (pool - 1)
    for k in range(pool - 1, 0, -1):
        chunks[k] = over_pool(packed[k], k)
    operands = list(chunks)
    if parts == 2:
        swapped = [None] * pool
        for k in range(pool - 1, 0, -1):
            swapped[k] = over_pair(chunks[k])
        operands += [packed[pool]] + swapped[1:]

    acc, stat = attend_cache(lengths, queries, cache)

    weight = jnp.transpose(key_value_weight, (1, 0, 2))
    all_rows = pool * count
    base, slots, shrink = pl.pallas_call(
        functools.partial(project_kernel, pool, parts),
        out_shape=[
            struct((all_rows, kv_local * pair), F32),
            struct((all_rows, LANES), BF16),
            struct((all_rows, LANES), BF16),
        ],
        in_specs=[SMEM] + [VMEM] * (len(operands) + 2),
        out_specs=[VMEM] * 3,
        name="project",
        cost_estimate=cost(2 * all_rows * part * (kv_local * pair + down_here * LANES), 6 << 20),
    )(place, *operands, weight, adapter_down_weight)

    ratio = pool // tensor
    mine = None
    for j in range(ratio):
        for m in range(0, tensor, parts):
            pairs = [
                (i * tensor + s, (s * ratio + ((i // tensor) ^ j)) * tensor + ((i % tensor) ^ m))
                for i in range(pool)
                for s in range(tensor)
            ]
            moved = lax.ppermute(shrink, ("pool", "tensor"), pairs).astype(F32)
            mine = moved if mine is None else mine + moved
    sums = [mine] + ([over_pair(mine)] if parts == 2 else [])
    expanded = pl.pallas_call(
        functools.partial(expand_kernel, pool, parts),
        out_shape=[struct((count, kv_local * pair), F32)] + [struct((count, kv_local * pair), BF16)] * (pool - 1),
        in_specs=[SMEM] + [VMEM] * (parts + 4),
        out_specs=[VMEM] * pool,
        scratch_shapes=[pltpu.VMEM((all_rows, LANES), F32)],
        name="expand",
        cost_estimate=cost(4 * all_rows * LANES * up_here * LANES, 1 << 20),
    )(place, *sums, slots, base, adapter_up_key, adapter_up_value)
    received = [None] * pool
    for k in range(pool - 1, 0, -1):
        received[k] = over_pool(expanded[k], k)
    attended, fresh = pl.pallas_call(
        functools.partial(finish_kernel, pool),
        out_shape=[struct((count, heads * size), BF16), struct((count, kv_local * pair), BF16)],
        in_specs=[VMEM] * (pool + 3),
        out_specs=[VMEM] * 2,
        scratch_shapes=[pltpu.VMEM((count * heads, size), F32)],
        name="finish",
        cost_estimate=cost(4 * count * heads * size * LANES, 1 << 20),
    )(expanded[0], *received[1:], queries, acc, stat)
    return (
        attended.reshape(rows, steps_new, heads * size),
        fresh.reshape(rows, steps_new, kv_local, pair),
    )


def attend_cache(lengths, queries, cache):
    rows, steps_new, heads, size = queries.shape
    depth, kv_local = cache.shape[1], cache.shape[2]
    rows_step = 4 if rows % 4 == 0 else 1
    block = rows_step * steps_new * heads
    return pl.pallas_call(
        functools.partial(cache_kernel, rows_step),
        out_shape=[struct((rows * steps_new * heads, size), F32), struct((rows * steps_new * heads, LANES), F32)],
        grid=(rows // rows_step,),
        in_specs=[
            SMEM,
            pl.BlockSpec((rows_step, steps_new, heads, size), lambda i: (i, 0, 0, 0)),
            pl.BlockSpec((rows_step, depth, kv_local, 2 * size), lambda i: (i, 0, 0, 0)),
        ],
        out_specs=[pl.BlockSpec((block, size), lambda i: (i, 0)), pl.BlockSpec((block, LANES), lambda i: (i, 0))],
        name="cached",
        cost_estimate=cost(8 * rows * steps_new * heads * depth * kv_local * size, cache.size * 2),
    )(lengths, queries, cache)


def solution(mesh):
    return jax.shard_map(
        body,
        mesh=mesh,
        in_specs=(
            P(("groups", "pool"), None, None),
            P(("groups", "pool"), None, "tensor", None),
            P(("groups", "pool"), None, "tensor", None),
            P("pool", "tensor", None),
            P("tensor", "pool", None),
            P("pool", None, "tensor", None),
            P("pool", None, "tensor", None),
            P(("groups", "pool")),
            P(),
            P(("groups", "pool")),
        ),
        out_specs=(
            P(("groups", "pool"), None, "tensor"),
            P(("groups", "pool"), None, "tensor", None),
        ),
        check_vma=False,
    )
```

time: 199 us -> 54.5 us (0.27)
  blocking collectives: 70.9 us -> 0 us
  local copies, waits for them, and re-layouts: 53.9 us -> 8.16 us
  waiting for transfers between devices: 31.1 us -> 11.8 us
  between operations: 15 us -> 0.78 us
  Pallas kernels: 8.71 us -> 18 us
  starting transfers between devices: 6.36 us -> 14.8 us
  other arithmetic: 6.98 us -> 0.6 us
  matrix products: 4.77 us -> 0 us
    psum x1 -> x0, blocking collectives: 57.7 us -> none  [body(): lax.psum(reduced_portion, ('pool', 'tensor')).astype(jnp.bfloat16)]
    reduce_scatter x2 -> x0, waiting for transfers between devices: 31.1 us -> none  [the longest x1 20.4 us: body(): lax.psum_scatter(base_part, 'pool', scatter_dimension=0, tiled=True)]
    unnamed x39 -> x23, local copies, waits for them, and re-layouts: 31.8 us -> 5.11 us
    pallas_call x0 -> x5, Pallas kernels: none -> 18 us  [the longest x1 6.68 us: attend_cache(): pl.pallas_call(functools.partial(cache_kernel, rows_step), out_shape=[str...]
    ppermute x0 -> x12, starting transfers between devices: none -> 14.8 us  [the longest x6 9.1 us: over_pool(): return lax.ppermute(x, 'pool', [(i, i ^ k) for i in range(pool)])]
    unnamed x1 -> x0, blocking collectives: 13.2 us -> none
    ppermute x0 -> x12, waiting for transfers between devices: none -> 11.8 us  [the longest x6 6.38 us: over_pool(): return lax.ppermute(x, 'pool', [(i, i ^ k) for i in range(pool)])]
    all_to_all x1 -> x0, local copies, waits for them, and re-layouts: 9.59 us -> none  [body(): lax.all_to_all(hidden, 'pool', split_axis=2, concat_axis=0, tiled=True)]
  transfers between devices with their start and end apart: 3 -> 12, of which waited for: 2 -> 4; matrix products, arithmetic and copies ran while one was open for 12% -> 6% of each run, Pallas kernels for 1% -> 12%
where the time goes in v1:
time: 54.5 us; the launch traced here: 54 us
  Pallas kernels  18 us (33%)
  starting transfers between devices  14.8 us (27%)
  waiting for transfers between devices  11.8 us (22%)
  local copies, waits for them, and re-layouts  8.16 us (15%)
  between operations  0.78 us (1%)
  other arithmetic  0.6 us (1%)
    ppermute x6, starting transfers between devices, over_pool(): return lax.ppermute(x, 'pool', [(i, i ^ k) for i in range(pool)])  9.1 us
    pallas_call x1, Pallas kernels, attend_cache(): pl.pallas_call(functools.partial(cache_kernel, rows_step), out_shape=[str...  6.68 us
    ppermute x6, waiting for transfers between devices, over_pool(): return lax.ppermute(x, 'pool', [(i, i ^ k) for i in range(pool)])  6.38 us
    ppermute x2, starting transfers between devices, body(): moved = lax.ppermute(shrink, ('pool', 'tensor'), pairs).astype(F32)  5.52 us
    unnamed x23, local copies, waits for them, and re-layouts  5.11 us
    pallas_call x1, Pallas kernels, body(): pl.pallas_call(functools.partial(project_kernel, pool, parts), out_shape=...  4.43 us
    ppermute x2, waiting for transfers between devices, body(): moved = lax.ppermute(shrink, ('pool', 'tensor'), pairs).astype(F32)  4.13 us
    pallas_call x1, Pallas kernels, body(): pl.pallas_call(functools.partial(finish_kernel, pool), out_shape=[struct(...  2.57 us
  transfers between devices with their start and end apart: 12, of which 4 were waited for; matrix products, arithmetic and copies ran while one was open for 6% of the time, Pallas kernels for 12%

profile of v1, /device:TPU:0, one launch (start us, length us, event | category | flops | bytes accessed | tf_op | source)
XLA Modules:
  0.0 54.0 jit_solution(6468340902985490946)
XLA Ops:
  0.6 0.6 %pad_add_fusion.place = s32[4]{0:T(128)} fusion(s32[1]{0:T(128)} %bitcast.3, s32[1]{0:T(128)} %bitcast.2, s32[1]{0:T(128)} %bitcast.1, s32[1]{0:T(128)} %bitcast), kind=kLoop, calls=%fused_computation.2 | loop fusion | flops 12 | bytes 32 | tf_op jit(solution)/shard_map/stack | solution.py:217
  1.2 1.8 %pack.1 = (bf16[32,1152]{1,0:T(8,128)(2,1)}, bf16[32,1152]{1,0:T(8,128)(2,1)}, bf16[32,1152]{1,0:T(8,128)(2,1)}, bf16[32,1152]{1,0:T(8,128)(2,1)}, bf16[32,1024]{1,0:T(8,128)(2,1)}) custom-call(s32[4]{0:T(128)} %pad_add_fusion.place, s32[16]{0:T(128)} %request_adapter.1, s32[24]{0:T(128)} %adapter_storage.1, bf16[16,2,8192]{2,1,0:T(2,128)(2,1)} %hidden.1), custom_call_target="tpu_custom_call" | custom-call | bytes 1048576 | tf_op jit(solution)/shard_map/pack/pallas_call | solution.py:226
  3.0 3.0 %collective-permute-start = (bf16[32,1152]{1,0:T(8,128)(2,1)}, bf16[32,1152]{1,0:T(8,128)(2,1)S(1)}, u32[]{:S(2)}, u32[]{:S(2)}) collective-permute-start(bf16[32,1152]{1,0:T(8,128)(2,1)} %get-tuple-element.19), channel_id=1, source_target_pairs={{0,4},{4,0},{8,12},{12,8},{1,5},{5,1},{9,13},{13,9},{2,6},{6,2},{1... | collective-permute-start | bytes 221192 | tf_op jit(solution)/shard_map/ppermute | solution.py:220
  6.0 2.6 %collective-permute-start.1 = (bf16[32,1152]{1,0:T(8,128)(2,1)}, bf16[32,1152]{1,0:T(8,128)(2,1)S(1)}, u32[]{:S(2)}, u32[]{:S(2)}) collective-permute-start(bf16[32,1152]{1,0:T(8,128)(2,1)} %get-tuple-element.20), channel_id=1, source_target_pairs={{0,8},{4,12},{8,0},{12,4},{1,9},{5,13},{9,1},{13,5},{2,10},{6,14},... | collective-permute-start | bytes 221192 | tf_op jit(solution)/shard_map/ppermute | solution.py:220
  8.6 0.1 collective-permute-start.3
  8.7 5.3 %collective-permute-done.1.refs_2_ = bf16[32,1152]{1,0:T(8,128)(2,1)S(1)} collective-permute-done((bf16[32,1152]{1,0:T(8,128)(2,1)}, bf16[32,1152]{1,0:T(8,128)(2,1)S(1)}, u32[]{:S(2)}, u32[]{:S(2)}) %collective-permute-start.1) | collective-permute-done | bytes 73760 | tf_op jit(solution)/shard_map/ppermute | solution.py:220
  14.1 1.1 %collective-permute-done.2.refs_3_ = bf16[32,1152]{1,0:T(8,128)(2,1)S(1)} collective-permute-done((bf16[32,1152]{1,0:T(8,128)(2,1)}, bf16[32,1152]{1,0:T(8,128)(2,1)S(1)}, u32[]{:S(2)}, u32[]{:S(2)}) %collective-permute-start.2) | collective-permute-done | bytes 73760 | tf_op jit(solution)/shard_map/ppermute | solution.py:220
  15.1 3.2 %copy.14 = bf16[2048,2,256]{2,0,1:T(8,128)(2,1)} copy(bf16[2048,2,256]{2,1,0:T(2,128)(2,1)} %param.13) | data formatting | bytes 4194304 | tf_op args[3]
  18.4 0.6 %copy-done.4 = bf16[32,1152]{1,0:T(8,128)(2,1)} copy-done((bf16[32,1152]{1,0:T(8,128)(2,1)}, bf16[32,1152]{1,0:T(8,128)(2,1)S(1)}, u32[]{:S(2)}) %copy-start.4) | copy-done | bytes 73752
  19.0 4.4 %project.1 = (f32[128,512]{1,0:T(8,128)}, bf16[128,128]{1,0:T(8,128)(2,1)}, bf16[128,128]{1,0:T(8,128)(2,1)}) custom-call(s32[4]{0:T(128)} %pad_add_fusion.place, bf16[32,1152]{1,0:T(8,128)(2,1)} %get-tuple-element.18.refs_0_, bf16[32,1152]{1,0:T(8,128)(2,1)} %copy-done.1, bf16[32,1152]{1,0:T(8,128)(2,1)} %copy-done.2, bf16[32,1152]{1,0:T(8,128)(2,1)} %copy-done.3, ...), custom_call_target="tpu_custom_call" | custom-call | flops 671088640 | bytes 6291456 | tf_op jit(solution)/shard_map/project/pallas_call | solution.py:248
  23.5 1.4 %collective-permute-start.6 = (bf16[128,128]{1,0:T(8,128)(2,1)}, bf16[128,128]{1,0:T(8,128)(2,1)S(1)}, u32[]{:S(2)}, u32[]{:S(2)}) collective-permute-start(bf16[128,128]{1,0:T(8,128)(2,1)} %get-tuple-element.23), channel_id=1, source_target_pairs={{0,0},{1,4},{2,8},{3,12},{4,1},{5,5},{6,9},{7,13},{8,2},{9,6},{10,... | collective-permute-start | bytes 98312 | tf_op jit(solution)/shard_map/ppermute | solution.py:270
  24.9 4.1 %collective-permute-start.7 = (bf16[128,128]{1,0:T(8,128)(2,1)}, bf16[128,128]{1,0:T(8,128)(2,1)S(1)}, u32[]{:S(2)}, u32[]{:S(2)}) collective-permute-start(bf16[128,128]{1,0:T(8,128)(2,1)} %get-tuple-element.23), channel_id=1, source_target_pairs={{0,2},{1,6},{2,10},{3,14},{4,3},{5,7},{6,11},{7,15},{8,0},{9,4},{1... | collective-permute-start | bytes 98312 | tf_op jit(solution)/shard_map/ppermute | solution.py:270
  29.0 4.1 %collective-permute-done.7 = bf16[128,128]{1,0:T(8,128)(2,1)S(1)} collective-permute-done((bf16[128,128]{1,0:T(8,128)(2,1)}, bf16[128,128]{1,0:T(8,128)(2,1)S(1)}, u32[]{:S(2)}, u32[]{:S(2)}) %collective-permute-start.7) | collective-permute-done | bytes 32800 | tf_op jit(solution)/shard_map/ppermute | solution.py:270
  33.2 1.2 %collective-permute-done.8.refs_1_ = f32[128,128]{1,0:T(8,128)S(1)} collective-permute-done((f32[128,128]{1,0:T(8,128)S(1)}, f32[128,128]{1,0:T(8,128)S(1)}, u32[]{:S(2)}, u32[]{:S(2)}) %collective-permute-start.8) | collective-permute-done | bytes 65568 | tf_op jit(solution)/shard_map/ppermute | solution.py:223
  34.5 0.6 %copy-done.7 = f32[128,128]{1,0:T(8,128)} copy-done((f32[128,128]{1,0:T(8,128)}, f32[128,128]{1,0:T(8,128)S(1)}, u32[]{:S(2)}) %copy-start.7) | copy-done | bytes 65560
  35.1 2.5 %expand.1 = (f32[32,512]{1,0:T(8,128)}, bf16[32,512]{1,0:T(8,128)(2,1)}, bf16[32,512]{1,0:T(8,128)(2,1)}, bf16[32,512]{1,0:T(8,128)(2,1)}) custom-call(s32[4]{0:T(128)} %pad_add_fusion.place, f32[128,128]{1,0:T(8,128)} %copy-done, f32[128,128]{1,0:T(8,128)} %copy-done.7, bf16[128,128]{1,0:T(8,128)(2,1)} %get-tuple-element.24.refs_2_, ...), custom_call_target="tpu_custom_call" | custom-call | flops 50331648 | bytes 1048576 | tf_op jit(solution)/shard_map/expand/pallas_call | solution.py:273
  37.6 1.0 %collective-permute-start.10 = (bf16[32,512]{1,0:T(8,128)(2,1)}, bf16[32,512]{1,0:T(8,128)(2,1)S(1)}, u32[]{:S(2)}, u32[]{:S(2)}) collective-permute-start(bf16[32,512]{1,0:T(8,128)(2,1)} %get-tuple-element.28), channel_id=1, source_target_pairs={{0,8},{4,12},{8,0},{12,4},{1,9},{5,13},{9,1},{13,5},{2,10},{6,14},... | collective-permute-start | bytes 98312 | tf_op jit(solution)/shard_map/ppermute | solution.py:220
  38.6 1.4 %collective-permute-start.11 = (bf16[32,512]{1,0:T(8,128)(2,1)}, bf16[32,512]{1,0:T(8,128)(2,1)S(1)}, u32[]{:S(2)}, u32[]{:S(2)}) collective-permute-start(bf16[32,512]{1,0:T(8,128)(2,1)} %get-tuple-element.29), channel_id=1, source_target_pairs={{0,12},{4,8},{8,4},{12,0},{1,13},{5,9},{9,5},{13,1},{2,14},{6,10},... | collective-permute-start | bytes 98312 | tf_op jit(solution)/shard_map/ppermute | solution.py:220
  39.9 1.2 %collective-permute-start.9 = (bf16[32,512]{1,0:T(8,128)(2,1)}, bf16[32,512]{1,0:T(8,128)(2,1)S(1)}, u32[]{:S(2)}, u32[]{:S(2)}) collective-permute-start(bf16[32,512]{1,0:T(8,128)(2,1)} %get-tuple-element.27), channel_id=1, source_target_pairs={{0,4},{4,0},{8,12},{12,8},{1,5},{5,1},{9,13},{13,9},{2,6},{6,2},{1... | collective-permute-start | bytes 98312 | tf_op jit(solution)/shard_map/ppermute | solution.py:220
  41.1 6.7 %cached.1 = (f32[512,128]{1,0:T(8,128)}, f32[512,128]{1,0:T(8,128)}) custom-call(s32[16]{0:T(128)} %lengths.1, bf16[16,2,16,128]{3,2,1,0:T(8,128)(2,1)} %refs_3_.1, bf16[16,256,2,256]{3,2,1,0:T(2,128)(2,1)} %cache.1), custom_call_target="tpu_custom_call" | custom-call | flops 268435456 | bytes 4194304 | tf_op jit(solution)/shard_map/cached/pallas_call | solution.py:305
  47.8 0.6 %copy-done.8 = bf16[32,512]{1,0:T(8,128)(2,1)} copy-done((bf16[32,512]{1,0:T(8,128)(2,1)}, bf16[32,512]{1,0:T(8,128)(2,1)S(1)}, u32[]{:S(2)}) %copy-start.8) | copy-done | bytes 32792
  48.4 2.6 %finish.1 = (bf16[32,2048]{1,0:T(8,128)(2,1)}, bf16[32,512]{1,0:T(8,128)(2,1)}) custom-call(f32[32,512]{1,0:T(8,128)} %get-tuple-element.26.own, bf16[32,512]{1,0:T(8,128)(2,1)} %copy-done.10, bf16[32,512]{1,0:T(8,128)(2,1)} %copy-done.8, bf16[32,512]{1,0:T(8,128)(2,1)} %copy-done.9, bf16[16,2,16,128]{3,2,1,0:T(8,128)(2,1)} %refs_3_.1, ...), custom_call_target="tpu_custom_call" | custom-call | flops 33554432 | bytes 1048576 | tf_op jit(solution)/shard_map/finish/pallas_call | solution.py:285
  51.0 1.7 %reshape.10 = bf16[16,2,2048]{2,1,0:T(2,128)(2,1)} reshape(bf16[32,2048]{1,0:T(8,128)(2,1)} %get-tuple-element.32) | data formatting | bytes 262144 | tf_op jit(solution)/shard_map/reshape | solution.py:295
  52.7 1.4 %reshape.11 = bf16[16,2,2,256]{3,2,1,0:T(2,128)(2,1)} reshape(bf16[32,512]{1,0:T(8,128)(2,1)} %get-tuple-element.33) | data formatting | bytes 65536 | tf_op jit(solution)/shard_map/reshape | solution.py:296
  (32 shorter events, 0.3 us)
Async XLA Ops:
  3.0 5.6 %collective-permute-start = (bf16[32,1152]{1,0:T(8,128)(2,1)}, bf16[32,1152]{1,0:T(8,128)(2,1)S(1)}, u32[]{:S(2)}, u32[]{:S(2)}) collective-permute-start(bf16[32,1152]{1,0:T(8,128)(2,1)} %get-tuple-element.19), channel_id=1, source_target_pairs={{0,4},{4,0},{8,12},{12,8},{1,5},{5,1},{9,13},{13,9},{2,6},{6,2},{1... | collective-permute-start | bytes 221192 | tf_op jit(solution)/shard_map/ppermute | solution.py:220
  6.0 8.0 %collective-permute-start.1 = (bf16[32,1152]{1,0:T(8,128)(2,1)}, bf16[32,1152]{1,0:T(8,128)(2,1)S(1)}, u32[]{:S(2)}, u32[]{:S(2)}) collective-permute-start(bf16[32,1152]{1,0:T(8,128)(2,1)} %get-tuple-element.20), channel_id=1, source_target_pairs={{0,8},{4,12},{8,0},{12,4},{1,9},{5,13},{9,1},{13,5},{2,10},{6,14},... | collective-permute-start | bytes 221192 | tf_op jit(solution)/shard_map/ppermute | solution.py:220
  8.6 6.5 %collective-permute-start.2 = (bf16[32,1152]{1,0:T(8,128)(2,1)}, bf16[32,1152]{1,0:T(8,128)(2,1)S(1)}, u32[]{:S(2)}, u32[]{:S(2)}) collective-permute-start(bf16[32,1152]{1,0:T(8,128)(2,1)} %get-tuple-element.21), channel_id=1, source_target_pairs={{0,12},{4,8},{8,4},{12,0},{1,13},{5,9},{9,5},{13,1},{2,14},{6,10},... | collective-permute-start | bytes 221192 | tf_op jit(solution)/shard_map/ppermute | solution.py:220
  8.6 9.7 %copy-start.1 = (bf16[32,1152]{1,0:T(8,128)(2,1)}, bf16[32,1152]{1,0:T(8,128)(2,1)S(1)}, u32[]{:S(2)}) copy-start(bf16[32,1152]{1,0:T(8,128)(2,1)S(1)} %collective-permute-done.refs_1_) | copy-start | bytes 221188
  8.6 9.7 %collective-permute-start.3 = (bf16[32,1152]{1,0:T(8,128)(2,1)S(1)}, bf16[32,1152]{1,0:T(8,128)(2,1)S(1)}, u32[]{:S(2)}, u32[]{:S(2)}) collective-permute-start(bf16[32,1152]{1,0:T(8,128)(2,1)S(1)} %collective-permute-done.refs_1_), channel_id=1, source_target_pairs={{0,1},{1,0},{2,3},{3,2},{4,5},{5,4},{6,7},{7,6},{8,9},{9,8},{10,11... | collective-permute-start | bytes 221192 | tf_op jit(solution)/shard_map/ppermute | solution.py:223
  14.0 4.3 %copy-start.2 = (bf16[32,1152]{1,0:T(8,128)(2,1)}, bf16[32,1152]{1,0:T(8,128)(2,1)S(1)}, u32[]{:S(2)}) copy-start(bf16[32,1152]{1,0:T(8,128)(2,1)S(1)} %collective-permute-done.1.refs_2_) | copy-start | bytes 221188
  14.0 4.3 %collective-permute-start.4 = (bf16[32,1152]{1,0:T(8,128)(2,1)S(1)}, bf16[32,1152]{1,0:T(8,128)(2,1)S(1)}, u32[]{:S(2)}, u32[]{:S(2)}) collective-permute-start(bf16[32,1152]{1,0:T(8,128)(2,1)S(1)} %collective-permute-done.1.refs_2_), channel_id=1, source_target_pairs={{0,1},{1,0},{2,3},{3,2},{4,5},{5,4},{6,7},{7,6},{8,9},{9,8},{10,11... | collective-permute-start | bytes 221192 | tf_op jit(solution)/shard_map/ppermute | solution.py:223
  15.1 3.3 %copy-start.3 = (bf16[32,1152]{1,0:T(8,128)(2,1)}, bf16[32,1152]{1,0:T(8,128)(2,1)S(1)}, u32[]{:S(2)}) copy-start(bf16[32,1152]{1,0:T(8,128)(2,1)S(1)} %collective-permute-done.2.refs_3_) | copy-start | bytes 221188
  15.1 3.2 %collective-permute-start.5 = (bf16[32,1152]{1,0:T(8,128)(2,1)S(1)}, bf16[32,1152]{1,0:T(8,128)(2,1)S(1)}, u32[]{:S(2)}, u32[]{:S(2)}) collective-permute-start(bf16[32,1152]{1,0:T(8,128)(2,1)S(1)} %collective-permute-done.2.refs_3_), channel_id=1, source_target_pairs={{0,1},{1,0},{2,3},{3,2},{4,5},{5,4},{6,7},{7,6},{8,9},{9,8},{10,11... | collective-permute-start | bytes 221192 | tf_op jit(solution)/shard_map/ppermute | solution.py:223
  18.3 0.6 %copy-start.4 = (bf16[32,1152]{1,0:T(8,128)(2,1)}, bf16[32,1152]{1,0:T(8,128)(2,1)S(1)}, u32[]{:S(2)}) copy-start(bf16[32,1152]{1,0:T(8,128)(2,1)S(1)} %collective-permute-done.3.refs_5_) | copy-start | bytes 221188
  18.3 0.7 %copy-start.5 = (bf16[32,1152]{1,0:T(8,128)(2,1)}, bf16[32,1152]{1,0:T(8,128)(2,1)S(1)}, u32[]{:S(2)}) copy-start(bf16[32,1152]{1,0:T(8,128)(2,1)S(1)} %collective-permute-done.4.refs_6_) | copy-start | bytes 221188
  18.4 0.7 %copy-start.6 = (bf16[32,1152]{1,0:T(8,128)(2,1)}, bf16[32,1152]{1,0:T(8,128)(2,1)S(1)}, u32[]{:S(2)}) copy-start(bf16[32,1152]{1,0:T(8,128)(2,1)S(1)} %collective-permute-done.5.refs_7_) | copy-start | bytes 221188
  23.5 5.5 %collective-permute-start.6 = (bf16[128,128]{1,0:T(8,128)(2,1)}, bf16[128,128]{1,0:T(8,128)(2,1)S(1)}, u32[]{:S(2)}, u32[]{:S(2)}) collective-permute-start(bf16[128,128]{1,0:T(8,128)(2,1)} %get-tuple-element.23), channel_id=1, source_target_pairs={{0,0},{1,4},{2,8},{3,12},{4,1},{5,5},{6,9},{7,13},{8,2},{9,6},{10,... | collective-permute-start | bytes 98312 | tf_op jit(solution)/shard_map/ppermute | solution.py:270
  24.9 8.2 %collective-permute-start.7 = (bf16[128,128]{1,0:T(8,128)(2,1)}, bf16[128,128]{1,0:T(8,128)(2,1)S(1)}, u32[]{:S(2)}, u32[]{:S(2)}) collective-permute-start(bf16[128,128]{1,0:T(8,128)(2,1)} %get-tuple-element.23), channel_id=1, source_target_pairs={{0,2},{1,6},{2,10},{3,14},{4,3},{5,7},{6,11},{7,15},{8,0},{9,4},{1... | collective-permute-start | bytes 98312 | tf_op jit(solution)/shard_map/ppermute | solution.py:270
  33.1 1.3 %copy-start = (f32[128,128]{1,0:T(8,128)}, f32[128,128]{1,0:T(8,128)S(1)}, u32[]{:S(2)}) copy-start(f32[128,128]{1,0:T(8,128)S(1)} %convert_add_fusion.refs_0_) | copy-start | bytes 196612
  33.2 1.3 %collective-permute-start.8 = (f32[128,128]{1,0:T(8,128)S(1)}, f32[128,128]{1,0:T(8,128)S(1)}, u32[]{:S(2)}, u32[]{:S(2)}) collective-permute-start(f32[128,128]{1,0:T(8,128)S(1)} %convert_add_fusion.refs_0_), channel_id=1, source_target_pairs={{0,1},{1,0},{2,3},{3,2},{4,5},{5,4},{6,7},{7,6},{8,9},{9,8},{10,11... | collective-permute-start | bytes 196616 | tf_op jit(solution)/shard_map/ppermute | solution.py:223
  34.5 0.6 %copy-start.7 = (f32[128,128]{1,0:T(8,128)}, f32[128,128]{1,0:T(8,128)S(1)}, u32[]{:S(2)}) copy-start(f32[128,128]{1,0:T(8,128)S(1)} %collective-permute-done.8.refs_1_) | copy-start | bytes 196612
  37.6 10.2 %collective-permute-start.10 = (bf16[32,512]{1,0:T(8,128)(2,1)}, bf16[32,512]{1,0:T(8,128)(2,1)S(1)}, u32[]{:S(2)}, u32[]{:S(2)}) collective-permute-start(bf16[32,512]{1,0:T(8,128)(2,1)} %get-tuple-element.28), channel_id=1, source_target_pairs={{0,8},{4,12},{8,0},{12,4},{1,9},{5,13},{9,1},{13,5},{2,10},{6,14},... | collective-permute-start | bytes 98312 | tf_op jit(solution)/shard_map/ppermute | solution.py:220
  38.6 9.2 %collective-permute-start.11 = (bf16[32,512]{1,0:T(8,128)(2,1)}, bf16[32,512]{1,0:T(8,128)(2,1)S(1)}, u32[]{:S(2)}, u32[]{:S(2)}) collective-permute-start(bf16[32,512]{1,0:T(8,128)(2,1)} %get-tuple-element.29), channel_id=1, source_target_pairs={{0,12},{4,8},{8,4},{12,0},{1,13},{5,9},{9,5},{13,1},{2,14},{6,10},... | collective-permute-start | bytes 98312 | tf_op jit(solution)/shard_map/ppermute | solution.py:220
  39.9 7.9 %collective-permute-start.9 = (bf16[32,512]{1,0:T(8,128)(2,1)}, bf16[32,512]{1,0:T(8,128)(2,1)S(1)}, u32[]{:S(2)}, u32[]{:S(2)}) collective-permute-start(bf16[32,512]{1,0:T(8,128)(2,1)} %get-tuple-element.27), channel_id=1, source_target_pairs={{0,4},{4,0},{8,12},{12,8},{1,5},{5,1},{9,13},{13,9},{2,6},{6,2},{1... | collective-permute-start | bytes 98312 | tf_op jit(solution)/shard_map/ppermute | solution.py:220
  47.8 0.6 %copy-start.8 = (bf16[32,512]{1,0:T(8,128)(2,1)}, bf16[32,512]{1,0:T(8,128)(2,1)S(1)}, u32[]{:S(2)}) copy-start(bf16[32,512]{1,0:T(8,128)(2,1)S(1)} %collective-permute-done.10.refs_1_) | copy-start | bytes 98308
  47.8 0.6 %copy-start.9 = (bf16[32,512]{1,0:T(8,128)(2,1)}, bf16[32,512]{1,0:T(8,128)(2,1)S(1)}, u32[]{:S(2)}) copy-start(bf16[32,512]{1,0:T(8,128)(2,1)S(1)} %collective-permute-done.11.refs_2_) | copy-start | bytes 98308
  47.8 0.6 %copy-start.10 = (bf16[32,512]{1,0:T(8,128)(2,1)}, bf16[32,512]{1,0:T(8,128)(2,1)S(1)}, u32[]{:S(2)}) copy-start(bf16[32,512]{1,0:T(8,128)(2,1)S(1)} %collective-permute-done.9.refs_0_) | copy-start | bytes 98308

commit v2 on v1

v2 whole, which is shorter than its diff:
```python
import functools
import jax
import jax.numpy as jnp
from jax import lax
from jax.experimental import pallas as pl
from jax.experimental.pallas import tpu as pltpu
from jax.sharding import PartitionSpec as P

ADAPTER_SCALE = 0.5
LANES = 128
F32 = jnp.float32
BF16 = jnp.bfloat16
VMEM = pl.BlockSpec(memory_space=pltpu.VMEM)
SMEM = pl.BlockSpec(memory_space=pltpu.SMEM)
HBM = pl.BlockSpec(memory_space=pltpu.HBM)
ANY = pl.BlockSpec(memory_space=pl.ANY)
LIMIT = 16 * 1024 * 1024
TOKEN = jax.ShapeDtypeStruct((8, LANES), F32)
PACK = 62 * 1024 * 1024


def dot(a, b):
    return jnp.dot(a, b, preferred_element_type=F32)


def dot_t(a, b):
    return lax.dot_general(a, b, (((1,), (1,)), ((), ())), preferred_element_type=F32)


def struct(shape, dtype):
    return jax.ShapeDtypeStruct(shape, dtype)


def cost(flops, moved):
    return pl.CostEstimate(flops=int(flops), bytes_accessed=int(moved), transcendentals=0)


def pack_kernel(pool, parts, request_adapter, adapter_storage, lengths, hidden, *refs):
    outs, (spans, pieces, ids, table, sizes, sems) = refs[:pool + parts - 1], refs[pool + parts - 1:]
    rows, steps_new, width = hidden.shape
    count = rows * steps_new
    part = width // pool
    half = part // parts
    me, side = lax.axis_index("pool"), lax.axis_index("tensor") % parts
    copies = [
        pltpu.make_async_copy(request_adapter, ids, sems.at[0]),
        pltpu.make_async_copy(adapter_storage, table, sems.at[1]),
        pltpu.make_async_copy(lengths, sizes, sems.at[2]),
    ]
    starts = [(me ^ k) * part + side * half for k in range(pool)] + [me * part + (1 - side) * half]
    for k in range(pool + parts - 1):
        at = pl.ds(pl.multiple_of(starts[k], LANES), half)
        copies.append(pltpu.make_async_copy(hidden.at[:, :, at], pieces.at[k], sems.at[3 + k]))
    for c in copies:
        c.start()
    copies[0].wait()
    copies[1].wait()
    copies[2].wait()
    row = lax.broadcasted_iota(jnp.int32, (count, LANES), 0) // steps_new
    slots = jnp.zeros((count, LANES), jnp.int32)
    for r in range(rows):
        slots = jnp.where(row == r, table[ids[r]], slots)
    slots = slots.astype(F32).astype(BF16)
    request = lax.broadcasted_iota(jnp.int32, spans.shape, 0)
    reach = jnp.zeros(spans.shape, jnp.int32)
    for r in range(rows):
        reach = jnp.where(request == r, sizes[r], reach)
    spans[...] = reach
    for k in range(pool + parts - 1):
        copies[3 + k].wait()
        outs[k][:, :half] = pieces[k].reshape(count, half)
        if k < pool:
            outs[k][:, half:] = slots


def both_sides(pool, parts, refs):
    chunks = refs[:pool]
    half = chunks[0].shape[1] - LANES
    side = lax.axis_index("tensor") % parts
    sides = [(side * half, jnp.concatenate([c[:, :half] for c in chunks], axis=0))]
    if parts == 2:
        rest = [refs[pool][...]] + [c[:, :half] for c in refs[pool + 1:2 * pool]]
        sides.append(((1 - side) * half, jnp.concatenate(rest, axis=0)))
    return [(pl.ds(pl.multiple_of(start, half), half), x) for start, x in sides]


def shrink_kernel(pool, parts, *refs):
    down, shrink, slots_out, token = refs[parts * pool:]
    token[...] = jnp.zeros_like(token)
    count = refs[0].shape[0]
    half = refs[0].shape[1] - LANES
    me = lax.axis_index("pool")
    first_slot = lax.axis_index("tensor") * down.shape[0]
    sides = both_sides(pool, parts, refs)
    slots = jnp.concatenate([c[:, half:] for c in refs[:pool]], axis=0)
    slots_out[...] = slots
    slots = slots.astype(F32)
    step = 2 if down.shape[0] % 2 == 0 else 1
    total = jnp.zeros((count * pool, LANES), F32)
    for a in range(0, down.shape[0], step):
        out = 0.0
        for at, x in sides:
            out += dot(x, jnp.concatenate([down[a + i, at, :] for i in range(step)], axis=1))
        for i in range(step):
            match = slots == (first_slot + a + i).astype(F32)
            total = jnp.where(match, out[:, i * LANES:(i + 1) * LANES], total)
    total = total.astype(BF16)
    for k in range(pool):
        at = pl.ds(pl.multiple_of((me ^ k) * count, count), count)
        shrink[at, :] = total[k * count:(k + 1) * count]


def base_kernel(pool, parts, *refs):
    weight, _, base = refs[parts * pool:]
    sides = both_sides(pool, parts, refs)
    for k in range(weight.shape[0]):
        out = 0.0
        for at, x in sides:
            out += dot(x, weight[k, at, :])
        base[:, k * weight.shape[2]:(k + 1) * weight.shape[2]] = out


def expand_kernel(pool, parts, *refs):
    sums, refs = refs[:parts], refs[parts:]
    slots_in, base, up_key, up_value = refs[:4]
    outs, token, scratch = refs[4:4 + pool], refs[4 + pool], refs[5 + pool]
    token[...] = jnp.zeros_like(token)
    holders, rank, kv_local, size = up_key.shape
    me = lax.axis_index("pool")
    first_slot = me * holders
    count = base.shape[0] // pool
    total = sums[0][...]
    for s in sums[1:]:
        total = total + s[...]
    scratch[...] = total
    ordered = jnp.concatenate(
        [scratch[pl.ds(pl.multiple_of((me ^ k) * count, count), count), :] for k in range(pool)], axis=0
    ).astype(BF16)
    slots = slots_in[...].astype(F32)
    deep = rank * kv_local
    for which, up in ((0, up_key), (1, up_value)):
        row = lax.broadcasted_iota(jnp.int32, (2 * rank, deep), 0)
        col = lax.broadcasted_iota(jnp.int32, (2 * rank, deep), 1)
        wide = []
        for k in range(kv_local):
            pick = (row == which * rank + col // kv_local) & (col % kv_local == k)
            wide.append(dot(ordered, pick.astype(F32).astype(BF16)))
        acc = [jnp.zeros((base.shape[0], size), F32) for _ in range(kv_local)]
        for a in range(holders):
            match = slots == (first_slot + a).astype(F32)
            if deep != LANES:
                match = match[:, :1]
            table = up[a].reshape(deep, size)
            for k in range(kv_local):
                acc[k] = acc[k] + dot(jnp.where(match, wide[k], 0.0).astype(BF16), table)
        for k in range(kv_local):
            at = slice((2 * k + which) * size, (2 * k + which + 1) * size)
            value = base[:, at] + ADAPTER_SCALE * acc[k]
            outs[0][:, at] = value[:count]
            for j in range(1, pool):
                outs[j][:, at] = value[j * count:(j + 1) * count].astype(BF16)


def cache_kernel(spans, queries, cache, _, acc_out, stat_out, scores_all, weights_all):
    rows, steps_new, heads, size = queries.shape
    kv_local, depth = cache.shape[1:3]
    count = steps_new * heads
    which = lax.broadcasted_iota(jnp.int32, (count, 1), 0) % heads // (heads // kv_local)
    col = lax.broadcasted_iota(jnp.int32, (1, depth), 1)
    for r in range(rows):
        q = queries[r].reshape(count, size)
        scores = dot_t(q, cache[r, 0, :, :size])
        for k in range(1, kv_local):
            scores = jnp.where(which == k, dot_t(q, cache[r, k, :, :size]), scores)
        scores = jnp.where(col < spans[r:r + 1, :], scores * size ** -0.5, -1e30)
        scores_all[r * count:(r + 1) * count, :] = scores
    scores = scores_all[...]
    top = jnp.max(scores, axis=1, keepdims=True)
    weights = jnp.exp(scores - top)
    total = jnp.sum(weights, axis=1, keepdims=True)
    lane = lax.broadcasted_iota(jnp.int32, (rows * count, LANES), 1)
    stat_out[...] = jnp.where(lane == 0, top, total)
    weights_all[...] = weights.astype(BF16)
    for r in range(rows):
        weights = weights_all[r * count:(r + 1) * count, :]
        mixed = dot(weights, cache[r, 0, :, size:])
        for k in range(1, kv_local):
            mixed = jnp.where(which == k, dot(weights, cache[r, k, :, size:]), mixed)
        acc_out[r * count:(r + 1) * count, :] = mixed


def finish_kernel(pool, own, *refs):
    parts, refs = refs[:pool - 1], refs[pool - 1:]
    queries, acc, stat, attended, fresh_out, scratch = refs
    rows, steps_new, heads, size = queries.shape
    count = rows * steps_new
    kv_local = own.shape[1] // (2 * size)
    group = heads // kv_local
    total = own[...]
    for part in parts:
        total = total + part[...].astype(F32)
    fresh = total.astype(BF16)
    wide = 2 * size
    fresh_out[...] = jnp.stack([fresh[:, k * wide:(k + 1) * wide] for k in range(kv_local)], axis=1).reshape(fresh_out.shape)
    keys = jnp.concatenate([fresh[:, 2 * k * size:(2 * k + 1) * size] for k in range(kv_local)], axis=0)
    values = jnp.concatenate([fresh[:, (2 * k + 1) * size:(2 * k + 2) * size] for k in range(kv_local)], axis=0)
    scores = dot_t(queries[...].reshape(count * heads, size), keys) * size ** -0.5
    col = lax.broadcasted_iota(jnp.int32, scores.shape, 1)
    row = lax.broadcasted_iota(jnp.int32, scores.shape, 0)
    token, other = row // heads, col % count
    valid = (
        (token // steps_new == other // steps_new)
        & (other <= token)
        & (row % heads // group == col // count)
    )
    scores = jnp.where(valid, scores, -1e30)
    stat = stat[...]
    top_before, total_before = stat[:, :1], stat[:, 1:2]
    top = jnp.maximum(top_before, jnp.max(scores, axis=1, keepdims=True))
    weights = jnp.exp(scores - top)
    keep = jnp.exp(top_before - top)
    norm = 1.0 / (total_before * keep + jnp.sum(weights, axis=1, keepdims=True))
    mixed = acc[...] * keep + dot(weights.astype(BF16), values)
    scratch[...] = mixed * norm
    for h in range(heads):
        out = scratch[pl.ds(h, count, stride=heads), :].astype(BF16)
        attended[:, :, h * size:(h + 1) * size] = out.reshape(rows, steps_new, size)


def body(
    hidden,
    queries,
    cache,
    key_value_weight,
    adapter_down_weight,
    adapter_up_key,
    adapter_up_value,
    request_adapter,
    adapter_storage,
    lengths,
):
    pool, tensor = lax.axis_size("pool"), lax.axis_size("tensor")
    rows, steps_new, width = hidden.shape
    count = rows * steps_new
    part = width // pool
    down_here, up_here = adapter_down_weight.shape[0], adapter_up_key.shape[0]
    _, kv_local, pair = key_value_weight.shape
    heads, size = queries.shape[2:]
    assert adapter_storage.shape[0] <= 256 and pool & (pool - 1) == 0 and tensor & (tensor - 1) == 0
    assert pool % tensor == 0 and down_here == up_here * (pool // tensor)
    parts = 2 if tensor % 2 == 0 else 1
    half = part // parts

    def over_pool(x, k):
        return lax.ppermute(x, "pool", [(i, i ^ k) for i in range(pool)])

    def over_pair(x):
        return lax.ppermute(x, "tensor", [(i, i ^ 1) for i in range(tensor)])

    def call(name, kernel, operands, in_specs, outs, scratch=(), work=0, moved=1 << 20, limit=LIMIT):
        return pl.pallas_call(
            kernel,
            out_shape=outs,
            in_specs=in_specs,
            out_specs=[VMEM] * len(outs),
            scratch_shapes=scratch,
            name=name,
            compiler_params=pltpu.CompilerParams(vmem_limit_bytes=limit),
            cost_estimate=cost(work, moved),
        )(*operands)

    chunk = struct((count, half + LANES), BF16)
    packed = call(
        "pack",
        functools.partial(pack_kernel, pool, parts),
        (request_adapter, adapter_storage, lengths, hidden),
        [HBM] * 4,
        [chunk] * pool + [struct((count, half), BF16)] * (parts - 1) + [struct((rows, cache.shape[1]), jnp.int32)],
        [
            pltpu.VMEM((pool + parts - 1, rows, steps_new, half), BF16),
            pltpu.SMEM(request_adapter.shape, jnp.int32),
            pltpu.SMEM(adapter_storage.shape, jnp.int32),
            pltpu.SMEM(lengths.shape, jnp.int32),
            pltpu.SemaphoreType.DMA((pool + parts + 2,)),
        ],
        limit=PACK,
    )
    operands = [packed[0]] + [None] * (pool - 1)
    for k in range(pool - 1, 0, -1):
        operands[k] = over_pool(packed[k], k)
    stored, _ = lax.optimization_barrier((cache, packed[0]))
    stored = jnp.transpose(stored, (0, 2, 1, 3))
    if parts == 2:
        swapped = [None] * pool
        for k in range(pool - 1, 0, -1):
            operands[k], stored = lax.optimization_barrier((operands[k], stored))
            swapped[k] = over_pair(operands[k])
        operands += [packed[pool]] + swapped[1:]

    all_rows = pool * count
    chunks_in = [VMEM] * len(operands)
    shrink, slots, token = call(
        "shrink",
        functools.partial(shrink_kernel, pool, parts),
        (*operands, adapter_down_weight),
        chunks_in + [VMEM],
        [struct((all_rows, LANES), BF16)] * 2 + [TOKEN],
        work=2 * all_rows * part * down_here * LANES,
        moved=4 << 20,
    )
    weight, marked = lax.optimization_barrier((key_value_weight, token))
    (base,) = call(
        "base",
        functools.partial(base_kernel, pool, parts),
        (*operands, jnp.transpose(weight, (1, 0, 2)), marked),
        chunks_in + [VMEM, ANY],
        [struct((all_rows, kv_local * pair), F32)],
        work=2 * all_rows * part * kv_local * pair,
        moved=3 << 20,
    )

    ratio = pool // tensor
    mine = None
    for j in range(ratio):
        for m in range(0, tensor, parts):
            pairs = [
                (i * tensor + s, (s * ratio + ((i // tensor) ^ j)) * tensor + ((i % tensor) ^ m))
                for i in range(pool)
                for s in range(tensor)
            ]
            moved = lax.ppermute(shrink, ("pool", "tensor"), pairs).astype(F32)
            mine = moved if mine is None else mine + moved
    sums = [mine] + ([over_pair(mine)] if parts == 2 else [])
    expanded = call(
        "expand",
        functools.partial(expand_kernel, pool, parts),
        (*sums, slots, base, adapter_up_key, adapter_up_value),
        [VMEM] * (parts + 4),
        [struct((count, kv_local * pair), F32)] + [struct((count, kv_local * pair), BF16)] * (pool - 1) + [TOKEN],
        [pltpu.VMEM((all_rows, LANES), F32)],
        work=4 * all_rows * LANES * up_here * LANES,
    )
    received = [None] * pool
    for k in range(pool - 1, 0, -1):
        received[k] = over_pool(expanded[k], k)
    acc, stat = call(
        "cached",
        cache_kernel,
        (packed[-1], queries, stored, expanded[pool]),
        [VMEM] * 3 + [ANY],
        [struct((count * heads, n), F32) for n in (size, LANES)],
        [pltpu.VMEM((count * heads, cache.shape[1]), t) for t in (F32, BF16)],
        work=4 * count * heads * cache.shape[1] * kv_local * size,
        moved=cache.size * 2,
    )
    return tuple(call(
        "finish",
        functools.partial(finish_kernel, pool),
        (expanded[0], *received[1:], queries, acc, stat),
        [VMEM] * (pool + 3),
        [struct((rows, steps_new, heads * size), BF16), struct((rows, steps_new, kv_local, pair), BF16)],
        [pltpu.VMEM((count * heads, size), F32)],
        work=4 * count * heads * size * LANES,
    ))


def solution(mesh):
    return jax.shard_map(
        body,
        mesh=mesh,
        in_specs=(
            P(("groups", "pool"), None, None),
            P(("groups", "pool"), None, "tensor", None),
            P(("groups", "pool"), None, "tensor", None),
            P("pool", "tensor", None),
            P("tensor", "pool", None),
            P("pool", None, "tensor", None),
            P("pool", None, "tensor", None),
            P(("groups", "pool")),
            P(),
            P(("groups", "pool")),
        ),
        out_specs=(
            P(("groups", "pool"), None, "tensor"),
            P(("groups", "pool"), None, "tensor", None),
        ),
        check_vma=False,
    )
```

time: 54.5 us -> 36.2 us (0.66)
  Pallas kernels: 18 us -> 6.15 us
  local copies, waits for them, and re-layouts: 8.16 us -> 3.42 us
  waiting for transfers between devices: 11.8 us -> 11.2 us
  other arithmetic: 0.6 us -> 0.01 us
    pallas_call x5 -> x6, Pallas kernels: 18 us -> 6.15 us  [call(): pl.pallas_call(kernel, out_shape=outs, in_specs=in_specs, out_specs=[VMEM...]
    unnamed x23 -> x16, local copies, waits for them, and re-layouts: 5.11 us -> 0.04 us
    optimization_barrier x0 -> x2, local copies, waits for them, and re-layouts: none -> 3.38 us  [the longest x1 3.1 us: body(): stored, _ = lax.optimization_barrier((cache, packed[0]))]
    reshape x2 -> x0, local copies, waits for them, and re-layouts: 3.05 us -> none  [the longest x1 1.66 us: body(): attended.reshape(rows, steps_new, heads * size)]
    ppermute x6, waiting for transfers between devices: 6.38 us -> 5.02 us  [over_pool(): return lax.ppermute(x, 'pool', [(i, i ^ k) for i in range(pool)])]
    ppermute x2, starting transfers between devices: 5.52 us -> 4.53 us  [body(): moved = lax.ppermute(shrink, ('pool', 'tensor'), pairs).astype(F32)]
    another operation x1 -> x0, other arithmetic: 0.59 us -> none  [body(): place = jnp.stack([p, side, t * down_here, p * up_here]).astype(jnp.int32)]
  transfers between devices with their start and end apart: 12 -> 12, of which waited for: 4 -> 8; matrix products, arithmetic and copies ran while one was open for 6% -> 9% of each run, Pallas kernels for 12% -> 4%
where the time goes in v2:
time: 36.2 us; the launch traced here: 36 us
  starting transfers between devices  14.4 us (40%)
  waiting for transfers between devices  11.2 us (31%)
  Pallas kernels  6.15 us (17%)
  local copies, waits for them, and re-layouts  3.42 us (9%)
  between operations  0.77 us (2%)
    ppermute x6, starting transfers between devices, over_pool(): return lax.ppermute(x, 'pool', [(i, i ^ k) for i in range(pool)])  9.31 us
    pallas_call x6, Pallas kernels, call(): pl.pallas_call(kernel, out_shape=outs, in_specs=in_specs, out_specs=[VMEM...  6.15 us
    ppermute x6, waiting for transfers between devices, over_pool(): return lax.ppermute(x, 'pool', [(i, i ^ k) for i in range(pool)])  5.02 us
    ppermute x2, starting transfers between devices, body(): moved = lax.ppermute(shrink, ('pool', 'tensor'), pairs).astype(F32)  4.53 us
    ppermute x2, waiting for transfers between devices, body(): moved = lax.ppermute(shrink, ('pool', 'tensor'), pairs).astype(F32)  4.53 us
    optimization_barrier x1, local copies, waits for them, and re-layouts, body(): stored, _ = lax.optimization_barrier((cache, packed[0]))  3.1 us
    ppermute x4, waiting for transfers between devices, over_pair(): return lax.ppermute(x, 'tensor', [(i, i ^ 1) for i in range(tensor)])  1.69 us
  transfers between devices with their start and end apart: 12, of which 8 were waited for; matrix products, arithmetic and copies ran while one was open for 9% of the time, Pallas kernels for 4%

profile of v2, /device:TPU:0, one launch (start us, length us, event | category | flops | bytes accessed | tf_op | source)
XLA Modules:
  0.0 36.0 jit_solution(12554425622432468281)
XLA Ops:
  0.6 1.8 %pack.1 = (bf16[32,1152]{1,0:T(8,128)(2,1)}, bf16[32,1152]{1,0:T(8,128)(2,1)}, bf16[32,1152]{1,0:T(8,128)(2,1)}, bf16[32,1152]{1,0:T(8,128)(2,1)}, bf16[32,1024]{1,0:T(8,128)(2,1)}, /*index=5*/s32[16,256]{1,0:T(8,128)}) custom-call(s32[16]{0:T(128)} %request_adapter.1, s32[24]{0:T(128)} %adapter_storage.1, s32[16]{0:T(128)} %lengths.1, ...), custom_call_target="tpu_custom_call" | custom-call | bytes 1048576 | tf_op jit(solution)/shard_map/pack/pallas_call | solution.py:261
  2.4 5.1 %collective-permute-start.2 = (bf16[32,1152]{1,0:T(8,128)(2,1)}, bf16[32,1152]{1,0:T(8,128)(2,1)S(1)}, u32[]{:S(2)}, u32[]{:S(2)}) collective-permute-start(bf16[32,1152]{1,0:T(8,128)(2,1)} %get-tuple-element.30), channel_id=1, source_target_pairs={{0,12},{4,8},{8,4},{12,0},{1,13},{5,9},{9,5},{13,1},{2,14},{6,10},... | collective-permute-start | bytes 221192 | tf_op jit(solution)/shard_map/ppermute | solution.py:255
  7.5 0.6 %collective-permute-start = (bf16[32,1152]{1,0:T(8,128)(2,1)}, bf16[32,1152]{1,0:T(8,128)(2,1)S(1)}, u32[]{:S(2)}, u32[]{:S(2)}) collective-permute-start(bf16[32,1152]{1,0:T(8,128)(2,1)} %get-tuple-element.28), channel_id=1, source_target_pairs={{0,4},{4,0},{8,12},{12,8},{1,5},{5,1},{9,13},{13,9},{2,6},{6,2},{1... | collective-permute-start | bytes 221192 | tf_op jit(solution)/shard_map/ppermute | solution.py:255
  8.2 3.1 %copy.16 = bf16[16,256,2,256]{3,1,2,0:T(8,128)(2,1)S(1)} copy(bf16[16,256,2,256]{3,2,1,0:T(2,128)(2,1)} %param.12) | data formatting | bytes 8388608 | tf_op jit(solution)/shard_map/optimization_barrier | solution.py:291
  11.3 2.6 %collective-permute-done.1.refs_2_ = bf16[32,1152]{1,0:T(8,128)(2,1)S(1)} collective-permute-done((bf16[32,1152]{1,0:T(8,128)(2,1)}, bf16[32,1152]{1,0:T(8,128)(2,1)S(1)}, u32[]{:S(2)}, u32[]{:S(2)}) %collective-permute-start.1) | collective-permute-done | bytes 73760 | tf_op jit(solution)/shard_map/ppermute | solution.py:255
  14.0 0.5 %collective-permute-start.4 = (bf16[32,1152]{1,0:T(8,128)(2,1)S(1)}, bf16[32,1152]{1,0:T(8,128)(2,1)S(1)}, u32[]{:S(2)}, u32[]{:S(2)}) collective-permute-start(bf16[32,1152]{1,0:T(8,128)(2,1)S(1)} %collective-permute-done.1.refs_2_), channel_id=1, source_target_pairs={{0,1},{1,0},{2,3},{3,2},{4,5},{5,4},{6,7},{7,6},{8,9},{9,8},{10,11... | collective-permute-start | bytes 221192 | tf_op jit(solution)/shard_map/ppermute | solution.py:258
  14.5 0.8 %collective-permute-done.3.refs_5_ = bf16[32,1152]{1,0:T(8,128)(2,1)S(1)} collective-permute-done((bf16[32,1152]{1,0:T(8,128)(2,1)S(1)}, bf16[32,1152]{1,0:T(8,128)(2,1)S(1)}, u32[]{:S(2)}, u32[]{:S(2)}) %collective-permute-start.3) | collective-permute-done | bytes 73760 | tf_op jit(solution)/shard_map/ppermute | solution.py:258
  15.2 0.2 collective-permute-done.4.refs_6_
  15.4 0.4 collective-permute-done.5.refs_7_
  15.8 0.6 %shrink.1 = (bf16[128,128]{1,0:T(8,128)(2,1)S(1)}, bf16[128,128]{1,0:T(8,128)(2,1)S(1)}, f32[8,128]{1,0:T(8,128)S(1)}) custom-call(bf16[32,1152]{1,0:T(8,128)(2,1)S(1)} %copy-done.2, bf16[32,1152]{1,0:T(8,128)(2,1)S(1)} %collective-permute-done.refs_1_, bf16[32,1152]{1,0:T(8,128)(2,1)S(1)} %collective-permute-done.1.refs_2_, ...), custom_call_target="tpu_custom_call" | custom-call | flops 402653184 | bytes 4194304 | tf_op jit(solution)/shard_map/shrink/pallas_call | solution.py:261
  16.4 0.7 %collective-permute-start.6 = (bf16[128,128]{1,0:T(8,128)(2,1)S(1)}, bf16[128,128]{1,0:T(8,128)(2,1)S(1)}, u32[]{:S(2)}, u32[]{:S(2)}) collective-permute-start(bf16[128,128]{1,0:T(8,128)(2,1)S(1)} %get-tuple-element.38), channel_id=1, source_target_pairs={{0,0},{1,4},{2,8},{3,12},{4,1},{5,5},{6,9},{7,13},{8,2},{9,6},{10,... | collective-permute-start | bytes 98312 | tf_op jit(solution)/shard_map/ppermute | solution.py:331
  17.1 3.9 %collective-permute-start.7 = (bf16[128,128]{1,0:T(8,128)(2,1)S(1)}, bf16[128,128]{1,0:T(8,128)(2,1)S(1)}, u32[]{:S(2)}, u32[]{:S(2)}) collective-permute-start(bf16[128,128]{1,0:T(8,128)(2,1)S(1)} %get-tuple-element.38), channel_id=1, source_target_pairs={{0,2},{1,6},{2,10},{3,14},{4,3},{5,7},{6,11},{7,15},{8,0},{9,4},{1... | collective-permute-start | bytes 98312 | tf_op jit(solution)/shard_map/ppermute | solution.py:331
  20.9 4.5 %collective-permute-done.7 = bf16[128,128]{1,0:T(8,128)(2,1)S(1)} collective-permute-done((bf16[128,128]{1,0:T(8,128)(2,1)S(1)}, bf16[128,128]{1,0:T(8,128)(2,1)S(1)}, u32[]{:S(2)}, u32[]{:S(2)}) %collective-permute-start.7) | collective-permute-done | bytes 32800 | tf_op jit(solution)/shard_map/ppermute | solution.py:331
  25.6 0.3 copy.17
  25.9 0.5 %base.1.refs_3_ = f32[128,512]{1,0:T(8,128)S(1)} custom-call(bf16[32,1152]{1,0:T(8,128)(2,1)S(1)} %copy-done.2, bf16[32,1152]{1,0:T(8,128)(2,1)S(1)} %collective-permute-done.refs_1_, bf16[32,1152]{1,0:T(8,128)(2,1)S(1)} %collective-permute-done.1.refs_2_, bf16[32,1152]{1,0:T(8,128)(2,1)S(1)} %collective-permute-done.2.refs_3_, ...), custom_call_target="tpu_custom_call" | custom-call | flops 268435456 | bytes 3145728 | tf_op jit(solution)/shard_map/base/pallas_call | solution.py:261
  26.4 0.4 %collective-permute-done.8.refs_1_ = f32[128,128]{1,0:T(8,128)S(1)} collective-permute-done((f32[128,128]{1,0:T(8,128)S(1)}, f32[128,128]{1,0:T(8,128)S(1)}, u32[]{:S(2)}, u32[]{:S(2)}) %collective-permute-start.8) | collective-permute-done | bytes 65568 | tf_op jit(solution)/shard_map/ppermute | solution.py:258
  26.8 0.6 %expand.1 = (f32[32,512]{1,0:T(8,128)S(1)}, bf16[32,512]{1,0:T(8,128)(2,1)S(1)}, bf16[32,512]{1,0:T(8,128)(2,1)S(1)}, bf16[32,512]{1,0:T(8,128)(2,1)S(1)}, f32[8,128]{1,0:T(8,128)S(1)}) custom-call(f32[128,128]{1,0:T(8,128)S(1)} %convert_add_fusion.refs_0_, f32[128,128]{1,0:T(8,128)S(1)} %collective-permute-done.8.refs_1_, ...), custom_call_target="tpu_custom_call" | custom-call | flops 50331648 | bytes 1048576 | tf_op jit(solution)/shard_map/expand/pallas_call | solution.py:261
  27.4 1.1 %collective-permute-start.10 = (bf16[32,512]{1,0:T(8,128)(2,1)S(1)}, bf16[32,512]{1,0:T(8,128)(2,1)S(1)}, u32[]{:S(2)}, u32[]{:S(2)}) collective-permute-start(bf16[32,512]{1,0:T(8,128)(2,1)S(1)} %get-tuple-element.45), channel_id=1, source_target_pairs={{0,8},{4,12},{8,0},{12,4},{1,9},{5,13},{9,1},{13,5},{2,10},{6,14},... | collective-permute-start | bytes 98312 | tf_op jit(solution)/shard_map/ppermute | solution.py:255
  28.5 1.6 %collective-permute-start.11 = (bf16[32,512]{1,0:T(8,128)(2,1)S(1)}, bf16[32,512]{1,0:T(8,128)(2,1)S(1)}, u32[]{:S(2)}, u32[]{:S(2)}) collective-permute-start(bf16[32,512]{1,0:T(8,128)(2,1)S(1)} %get-tuple-element.46), channel_id=1, source_target_pairs={{0,12},{4,8},{8,4},{12,0},{1,13},{5,9},{9,5},{13,1},{2,14},{6,10},... | collective-permute-start | bytes 98312 | tf_op jit(solution)/shard_map/ppermute | solution.py:255
  30.1 0.9 %collective-permute-start.9 = (bf16[32,512]{1,0:T(8,128)(2,1)S(1)}, bf16[32,512]{1,0:T(8,128)(2,1)S(1)}, u32[]{:S(2)}, u32[]{:S(2)}) collective-permute-start(bf16[32,512]{1,0:T(8,128)(2,1)S(1)} %get-tuple-element.44), channel_id=1, source_target_pairs={{0,4},{4,0},{8,12},{12,8},{1,5},{5,1},{9,13},{13,9},{2,6},{6,2},{1... | collective-permute-start | bytes 98312 | tf_op jit(solution)/shard_map/ppermute | solution.py:255
  31.0 1.1 %cached.1 = (f32[512,128]{1,0:T(8,128)S(1)}, f32[512,128]{1,0:T(8,128)S(1)}) custom-call(s32[16,256]{1,0:T(8,128)S(1)} %copy-done.6, bf16[16,2,16,128]{3,2,1,0:T(8,128)(2,1)S(1)} %copy-done.1, bf16[16,2,256,256]{3,2,1,0:T(8,128)(2,1)S(1)} %bitcast.6, f32[8,128]{1,0:T(8,128)S(1)} %get-tuple-element.49._), custom_call_target="tpu_custom_call" | custom-call | flops 134217728 | bytes 4194304 | tf_op jit(solution)/shard_map/cached/pallas_call | solution.py:261
  32.2 0.4 %collective-permute-done.10.refs_1_ = bf16[32,512]{1,0:T(8,128)(2,1)S(1)} collective-permute-done((bf16[32,512]{1,0:T(8,128)(2,1)S(1)}, bf16[32,512]{1,0:T(8,128)(2,1)S(1)}, u32[]{:S(2)}, u32[]{:S(2)}) %collective-permute-start.10) | collective-permute-done | bytes 32800 | tf_op jit(solution)/shard_map/ppermute | solution.py:255
  32.6 1.9 %collective-permute-done.11.refs_2_ = bf16[32,512]{1,0:T(8,128)(2,1)S(1)} collective-permute-done((bf16[32,512]{1,0:T(8,128)(2,1)S(1)}, bf16[32,512]{1,0:T(8,128)(2,1)S(1)}, u32[]{:S(2)}, u32[]{:S(2)}) %collective-permute-start.11) | collective-permute-done | bytes 32800 | tf_op jit(solution)/shard_map/ppermute | solution.py:255
  34.5 1.5 %finish.1 = (bf16[16,2,2048]{2,1,0:T(2,128)(2,1)}, bf16[16,2,2,256]{3,2,1,0:T(2,128)(2,1)}) custom-call(f32[32,512]{1,0:T(8,128)S(1)} %get-tuple-element.43.own, bf16[32,512]{1,0:T(8,128)(2,1)S(1)} %collective-permute-done.9.refs_0_, bf16[32,512]{1,0:T(8,128)(2,1)S(1)} %collective-permute-done.10.refs_1_, ...), custom_call_target="tpu_custom_call" | custom-call | flops 33554432 | bytes 1048576 | tf_op jit(solution)/shard_map/finish/pallas_call | solution.py:261
  (25 shorter events, 0.1 us)
Async XLA Ops:
  2.4 8.9 %collective-permute-start.2 = (bf16[32,1152]{1,0:T(8,128)(2,1)}, bf16[32,1152]{1,0:T(8,128)(2,1)S(1)}, u32[]{:S(2)}, u32[]{:S(2)}) collective-permute-start(bf16[32,1152]{1,0:T(8,128)(2,1)} %get-tuple-element.30), channel_id=1, source_target_pairs={{0,12},{4,8},{8,4},{12,0},{1,13},{5,9},{9,5},{13,1},{2,14},{6,10},... | collective-permute-start | bytes 221192 | tf_op jit(solution)/shard_map/ppermute | solution.py:255
  7.5 6.4 %collective-permute-start.1 = (bf16[32,1152]{1,0:T(8,128)(2,1)}, bf16[32,1152]{1,0:T(8,128)(2,1)S(1)}, u32[]{:S(2)}, u32[]{:S(2)}) collective-permute-start(bf16[32,1152]{1,0:T(8,128)(2,1)} %get-tuple-element.29), channel_id=1, source_target_pairs={{0,8},{4,12},{8,0},{12,4},{1,9},{5,13},{9,1},{13,5},{2,10},{6,14},... | collective-permute-start | bytes 221192 | tf_op jit(solution)/shard_map/ppermute | solution.py:255
  7.5 6.4 %collective-permute-start = (bf16[32,1152]{1,0:T(8,128)(2,1)}, bf16[32,1152]{1,0:T(8,128)(2,1)S(1)}, u32[]{:S(2)}, u32[]{:S(2)}) collective-permute-start(bf16[32,1152]{1,0:T(8,128)(2,1)} %get-tuple-element.28), channel_id=1, source_target_pairs={{0,4},{4,0},{8,12},{12,8},{1,5},{5,1},{9,13},{13,9},{2,6},{6,2},{1... | collective-permute-start | bytes 221192 | tf_op jit(solution)/shard_map/ppermute | solution.py:255
  8.2 7.6 %copy-start = (bf16[6,2048,128]{2,1,0:T(8,128)(2,1)S(1)}, bf16[6,2048,128]{2,1,0:T(8,128)(2,1)}, u32[]{:S(2)}) copy-start(bf16[6,2048,128]{2,1,0:T(8,128)(2,1)} %refs_8_.1) | copy-start | bytes 9437188
  8.2 7.6 %copy-start.2 = (bf16[32,1152]{1,0:T(8,128)(2,1)S(1)}, bf16[32,1152]{1,0:T(8,128)(2,1)}, u32[]{:S(2)}) copy-start(bf16[32,1152]{1,0:T(8,128)(2,1)} %get-tuple-element.27.refs_0_) | copy-start | bytes 221188
  8.2 7.6 %copy-start.3 = (bf16[32,1024]{1,0:T(8,128)(2,1)S(1)}, bf16[32,1024]{1,0:T(8,128)(2,1)}, u32[]{:S(2)}) copy-start(bf16[32,1024]{1,0:T(8,128)(2,1)} %get-tuple-element.37.refs_4_) | copy-start | bytes 196612
  11.3 14.2 %copy-start.7 = (bf16[2048,2,256]{2,1,0:T(2,128)(2,1)S(1)}, bf16[2048,2,256]{2,1,0:T(2,128)(2,1)}, u32[]{:S(2)}) copy-start(bf16[2048,2,256]{2,1,0:T(2,128)(2,1)} %param.13) | copy-start | bytes 6291460
  14.0 1.3 %collective-permute-start.3 = (bf16[32,1152]{1,0:T(8,128)(2,1)S(1)}, bf16[32,1152]{1,0:T(8,128)(2,1)S(1)}, u32[]{:S(2)}, u32[]{:S(2)}) collective-permute-start(bf16[32,1152]{1,0:T(8,128)(2,1)S(1)} %collective-permute-done.refs_1_), channel_id=1, source_target_pairs={{0,1},{1,0},{2,3},{3,2},{4,5},{5,4},{6,7},{7,6},{8,9},{9,8},{10,11... | collective-permute-start | bytes 221192 | tf_op jit(solution)/shard_map/ppermute | solution.py:258
  14.0 1.4 %collective-permute-start.4 = (bf16[32,1152]{1,0:T(8,128)(2,1)S(1)}, bf16[32,1152]{1,0:T(8,128)(2,1)S(1)}, u32[]{:S(2)}, u32[]{:S(2)}) collective-permute-start(bf16[32,1152]{1,0:T(8,128)(2,1)S(1)} %collective-permute-done.1.refs_2_), channel_id=1, source_target_pairs={{0,1},{1,0},{2,3},{3,2},{4,5},{5,4},{6,7},{7,6},{8,9},{9,8},{10,11... | collective-permute-start | bytes 221192 | tf_op jit(solution)/shard_map/ppermute | solution.py:258
  14.5 1.3 %collective-permute-start.5 = (bf16[32,1152]{1,0:T(8,128)(2,1)S(1)}, bf16[32,1152]{1,0:T(8,128)(2,1)S(1)}, u32[]{:S(2)}, u32[]{:S(2)}) collective-permute-start(bf16[32,1152]{1,0:T(8,128)(2,1)S(1)} %collective-permute-done.2.refs_3_), channel_id=1, source_target_pairs={{0,1},{1,0},{2,3},{3,2},{4,5},{5,4},{6,7},{7,6},{8,9},{9,8},{10,11... | collective-permute-start | bytes 221192 | tf_op jit(solution)/shard_map/ppermute | solution.py:258
  16.4 4.5 %collective-permute-start.6 = (bf16[128,128]{1,0:T(8,128)(2,1)S(1)}, bf16[128,128]{1,0:T(8,128)(2,1)S(1)}, u32[]{:S(2)}, u32[]{:S(2)}) collective-permute-start(bf16[128,128]{1,0:T(8,128)(2,1)S(1)} %get-tuple-element.38), channel_id=1, source_target_pairs={{0,0},{1,4},{2,8},{3,12},{4,1},{5,5},{6,9},{7,13},{8,2},{9,6},{10,... | collective-permute-start | bytes 98312 | tf_op jit(solution)/shard_map/ppermute | solution.py:331
  17.1 8.4 %collective-permute-start.7 = (bf16[128,128]{1,0:T(8,128)(2,1)S(1)}, bf16[128,128]{1,0:T(8,128)(2,1)S(1)}, u32[]{:S(2)}, u32[]{:S(2)}) collective-permute-start(bf16[128,128]{1,0:T(8,128)(2,1)S(1)} %get-tuple-element.38), channel_id=1, source_target_pairs={{0,2},{1,6},{2,10},{3,14},{4,3},{5,7},{6,11},{7,15},{8,0},{9,4},{1... | collective-permute-start | bytes 98312 | tf_op jit(solution)/shard_map/ppermute | solution.py:331
  25.5 1.3 %collective-permute-start.8 = (f32[128,128]{1,0:T(8,128)S(1)}, f32[128,128]{1,0:T(8,128)S(1)}, u32[]{:S(2)}, u32[]{:S(2)}) collective-permute-start(f32[128,128]{1,0:T(8,128)S(1)} %convert_add_fusion.refs_0_), channel_id=1, source_target_pairs={{0,1},{1,0},{2,3},{3,2},{4,5},{5,4},{6,7},{7,6},{8,9},{9,8},{10,11... | collective-permute-start | bytes 196616 | tf_op jit(solution)/shard_map/ppermute | solution.py:258
  25.6 1.2 %copy-start.4 = (bf16[6,64,2,128]{3,2,1,0:T(2,128)(2,1)S(1)}, bf16[6,64,2,128]{3,2,1,0:T(2,128)(2,1)}, u32[]{:S(2)}) copy-start(bf16[6,64,2,128]{3,2,1,0:T(2,128)(2,1)} %refs_4_.1) | copy-start | bytes 589828
  25.6 1.2 %copy-start.5 = (bf16[6,64,2,128]{3,2,1,0:T(2,128)(2,1)S(1)}, bf16[6,64,2,128]{3,2,1,0:T(2,128)(2,1)}, u32[]{:S(2)}) copy-start(bf16[6,64,2,128]{3,2,1,0:T(2,128)(2,1)} %refs_5_.1) | copy-start | bytes 589828
  25.6 5.4 %copy-start.1 = (bf16[16,2,16,128]{3,2,1,0:T(8,128)(2,1)S(1)}, bf16[16,2,16,128]{3,2,1,0:T(8,128)(2,1)}, u32[]{:S(2)}) copy-start(bf16[16,2,16,128]{3,2,1,0:T(8,128)(2,1)} %refs_3_.1) | copy-start | bytes 393220
  25.6 5.4 %copy-start.6 = (s32[16,256]{1,0:T(8,128)S(1)}, s32[16,256]{1,0:T(8,128)}, u32[]{:S(2)}) copy-start(s32[16,256]{1,0:T(8,128)} %get-tuple-element.47.spans) | copy-start | bytes 49156
  27.4 5.1 %collective-permute-start.10 = (bf16[32,512]{1,0:T(8,128)(2,1)S(1)}, bf16[32,512]{1,0:T(8,128)(2,1)S(1)}, u32[]{:S(2)}, u32[]{:S(2)}) collective-permute-start(bf16[32,512]{1,0:T(8,128)(2,1)S(1)} %get-tuple-element.45), channel_id=1, source_target_pairs={{0,8},{4,12},{8,0},{12,4},{1,9},{5,13},{9,1},{13,5},{2,10},{6,14},... | collective-permute-start | bytes 98312 | tf_op jit(solution)/shard_map/ppermute | solution.py:255
  28.5 6.0 %collective-permute-start.11 = (bf16[32,512]{1,0:T(8,128)(2,1)S(1)}, bf16[32,512]{1,0:T(8,128)(2,1)S(1)}, u32[]{:S(2)}, u32[]{:S(2)}) collective-permute-start(bf16[32,512]{1,0:T(8,128)(2,1)S(1)} %get-tuple-element.46), channel_id=1, source_target_pairs={{0,12},{4,8},{8,4},{12,0},{1,13},{5,9},{9,5},{13,1},{2,14},{6,10},... | collective-permute-start | bytes 98312 | tf_op jit(solution)/shard_map/ppermute | solution.py:255
  30.1 4.4 %collective-permute-start.9 = (bf16[32,512]{1,0:T(8,128)(2,1)S(1)}, bf16[32,512]{1,0:T(8,128)(2,1)S(1)}, u32[]{:S(2)}, u32[]{:S(2)}) collective-permute-start(bf16[32,512]{1,0:T(8,128)(2,1)S(1)} %get-tuple-element.44), channel_id=1, source_target_pairs={{0,4},{4,0},{8,12},{12,8},{1,5},{5,1},{9,13},{13,9},{2,6},{6,2},{1... | collective-permute-start | bytes 98312 | tf_op jit(solution)/shard_map/ppermute | solution.py:255

commit v3 on v2

--- a/solution.py
+++ b/solution.py
@@ -15,6 +15,8 @@
 HBM = pl.BlockSpec(memory_space=pltpu.HBM)
 ANY = pl.BlockSpec(memory_space=pl.ANY)
 LIMIT = 16 * 1024 * 1024
+WHOLE = (0, 1)
+TAIL = 16
 TOKEN = jax.ShapeDtypeStruct((8, LANES), F32)
 PACK = 62 * 1024 * 1024
 
@@ -36,7 +38,7 @@
 
 
 def pack_kernel(pool, parts, request_adapter, adapter_storage, lengths, hidden, *refs):
-    outs, (spans, pieces, ids, table, sizes, sems) = refs[:pool + parts - 1], refs[pool + parts - 1:]
+    outs, (spans, pieces, ids, table, sizes, sems) = refs[:pool], refs[pool:]
     rows, steps_new, width = hidden.shape
     count = rows * steps_new
     part = width // pool
@@ -47,54 +49,65 @@
         pltpu.make_async_copy(adapter_storage, table, sems.at[1]),
         pltpu.make_async_copy(lengths, sizes, sems.at[2]),
     ]
-    starts = [(me ^ k) * part + side * half for k in range(pool)] + [me * part + (1 - side) * half]
-    for k in range(pool + parts - 1):
-        at = pl.ds(pl.multiple_of(starts[k], LANES), half)
-        copies.append(pltpu.make_async_copy(hidden.at[:, :, at], pieces.at[k], sems.at[3 + k]))
+    places = []
+    for k in reversed(range(pool)):
+        for i in range(parts if k in WHOLE else 1):
+            start = (me ^ k) * part + (side if i == 0 else 1 - side) * half
+            source = hidden.at[:, :, pl.ds(pl.multiple_of(start, LANES), half)]
+            copies.append(pltpu.make_async_copy(source, pieces.at[len(places)], sems.at[3 + len(places)]))
+            places.append((k, i * half // LANES))
     for c in copies:
         c.start()
-    copies[0].wait()
-    copies[1].wait()
-    copies[2].wait()
-    row = lax.broadcasted_iota(jnp.int32, (count, LANES), 0) // steps_new
-    slots = jnp.zeros((count, LANES), jnp.int32)
+    for c in copies[:3]:
+        c.wait()
+    lane = lax.broadcasted_iota(jnp.int32, (TAIL, LANES), 1) // steps_new
+    slots = jnp.zeros((TAIL, LANES), jnp.int32)
     for r in range(rows):
-        slots = jnp.where(row == r, table[ids[r]], slots)
+        slots = jnp.where(lane == r, table[ids[r]], slots)
     slots = slots.astype(F32).astype(BF16)
     request = lax.broadcasted_iota(jnp.int32, spans.shape, 0)
     reach = jnp.zeros(spans.shape, jnp.int32)
     for r in range(rows):
         reach = jnp.where(request == r, sizes[r], reach)
     spans[...] = reach
-    for k in range(pool + parts - 1):
-        copies[3 + k].wait()
-        outs[k][:, :half] = pieces[k].reshape(count, half)
-        if k < pool:
-            outs[k][:, half:] = slots
-
-
-def both_sides(pool, parts, refs):
-    chunks = refs[:pool]
-    half = chunks[0].shape[1] - LANES
+    for k in range(pool):
+        outs[k][-TAIL:, :] = slots
+    for n, (k, first) in enumerate(places):
+        copies[3 + n].wait()
+        piece = pieces[n].reshape(count, half)
+        for j in range(half // LANES):
+            outs[k][(first + j) * count:(first + j + 1) * count, :] = piece[:, j * LANES:(j + 1) * LANES]
+
+
+def both_sides(pool, parts, count, half, refs):
     side = lax.axis_index("tensor") % parts
-    sides = [(side * half, jnp.concatenate([c[:, :half] for c in chunks], axis=0))]
+    tiles = half // LANES
+
+    def rows(chunk, first):
+        return jnp.concatenate([chunk[j * count:(j + 1) * count, :] for j in range(first, first + tiles)], axis=1)
+
+    sides = [(side * half, jnp.concatenate([rows(c, 0) for c in refs[:pool]], axis=0))]
     if parts == 2:
-        rest = [refs[pool][...]] + [c[:, :half] for c in refs[pool + 1:2 * pool]]
+        swapped = iter(refs[pool:])
+        rest = [rows(refs[k], tiles) if k in WHOLE else rows(next(swapped), 0) for k in range(pool)]
         sides.append(((1 - side) * half, jnp.concatenate(rest, axis=0)))
     return [(pl.ds(pl.multiple_of(start, half), half), x) for start, x in sides]
 
 
-def shrink_kernel(pool, parts, *refs):
-    down, shrink, slots_out, token = refs[parts * pool:]
+def shrink_kernel(pool, parts, count, half, *refs):
+    down, shrink, slots_out, token = refs[-4:]
     token[...] = jnp.zeros_like(token)
-    count = refs[0].shape[0]
-    half = refs[0].shape[1] - LANES
     me = lax.axis_index("pool")
     first_slot = lax.axis_index("tensor") * down.shape[0]
-    sides = both_sides(pool, parts, refs)
-    slots = jnp.concatenate([c[:, half:] for c in refs[:pool]], axis=0)
+    sides = both_sides(pool, parts, count, half, refs[:-4])
+    row = lax.broadcasted_iota(jnp.int32, (count, LANES), 0)
+    lane = lax.broadcasted_iota(jnp.int32, (count, LANES), 1)
+    slots = []
+    for c in refs[:pool]:
+        line = c[-TAIL:, :].astype(F32)[:1, :]
+        slots.append(jnp.sum(jnp.where(row == lane, line, 0.0), axis=1, keepdims=True))
+    slots = jnp.broadcast_to(jnp.concatenate(slots, axis=0), (count * pool, LANES))
     slots_out[...] = slots
-    slots = slots.astype(F32)
     step = 2 if down.shape[0] % 2 == 0 else 1
     total = jnp.zeros((count * pool, LANES), F32)
     for a in range(0, down.shape[0], step):
@@ -110,9 +123,9 @@
         shrink[at, :] = total[k * count:(k + 1) * count]
 
 
-def base_kernel(pool, parts, *refs):
-    weight, _, base = refs[parts * pool:]
-    sides = both_sides(pool, parts, refs)
+def base_kernel(pool, parts, count, half, *refs):
+    weight, _, base = refs[-3:]
+    sides = both_sides(pool, parts, count, half, refs[:-3])
     for k in range(weight.shape[0]):
         out = 0.0
         for at, x in sides:
@@ -136,7 +149,7 @@
     ordered = jnp.concatenate(
         [scratch[pl.ds(pl.multiple_of((me ^ k) * count, count), count), :] for k in range(pool)], axis=0
     ).astype(BF16)
-    slots = slots_in[...].astype(F32)
+    slots = slots_in[...]
     deep = rank * kv_local
     for which, up in ((0, up_key), (1, up_value)):
         row = lax.broadcasted_iota(jnp.int32, (2 * rank, deep), 0)
@@ -246,7 +259,7 @@
     down_here, up_here = adapter_down_weight.shape[0], adapter_up_key.shape[0]
     _, kv_local, pair = key_value_weight.shape
     heads, size = queries.shape[2:]
-    assert adapter_storage.shape[0] <= 256 and pool & (pool - 1) == 0 and tensor & (tensor - 1) == 0
+    assert adapter_storage.shape[0] <= 256 and count <= LANES and pool & (pool - 1) == 0 and tensor & (tensor - 1) == 0
     assert pool % tensor == 0 and down_here == up_here * (pool // tensor)
     parts = 2 if tensor % 2 == 0 else 1
     half = part // parts
@@ -269,19 +282,22 @@
             cost_estimate=cost(work, moved),
         )(*operands)
 
-    chunk = struct((count, half + LANES), BF16)
+    chunks = [
+        struct((count * (part if k in WHOLE else half) // LANES + TAIL, LANES), BF16) for k in range(pool)
+    ]
+    pieces = sum(parts if k in WHOLE else 1 for k in range(pool))
     packed = call(
         "pack",
         functools.partial(pack_kernel, pool, parts),
         (request_adapter, adapter_storage, lengths, hidden),
         [HBM] * 4,
-        [chunk] * pool + [struct((count, half), BF16)] * (parts - 1) + [struct((rows, cache.shape[1]), jnp.int32)],
+        chunks + [struct((rows, cache.shape[1]), jnp.int32)],
         [
-            pltpu.VMEM((pool + parts - 1, rows, steps_new, half), BF16),
+            pltpu.VMEM((pieces, rows, steps_new, half), BF16),
             pltpu.SMEM(request_adapter.shape, jnp.int32),
             pltpu.SMEM(adapter_storage.shape, jnp.int32),
             pltpu.SMEM(lengths.shape, jnp.int32),
-            pltpu.SemaphoreType.DMA((pool + parts + 2,)),
+            pltpu.SemaphoreType.DMA((3 + pieces,)),
         ],
         limit=PACK,
     )
@@ -290,28 +306,28 @@
         operands[k] = over_pool(packed[k], k)
     stored, _ = lax.optimization_barrier((cache, packed[0]))
     stored = jnp.transpose(stored, (0, 2, 1, 3))
-    if parts == 2:
-        swapped = [None] * pool
-        for k in range(pool - 1, 0, -1):
-            operands[k], stored = lax.optimization_barrier((operands[k], stored))
+    swapped = {}
+    for k in [*range(2, pool), 1]:
+        operands[k], stored = lax.optimization_barrier((operands[k], stored))
+        if parts == 2 and k not in WHOLE:
             swapped[k] = over_pair(operands[k])
-        operands += [packed[pool]] + swapped[1:]
+    operands += [swapped[k] for k in sorted(swapped)]
 
     all_rows = pool * count
     chunks_in = [VMEM] * len(operands)
     shrink, slots, token = call(
         "shrink",
-        functools.partial(shrink_kernel, pool, parts),
+        functools.partial(shrink_kernel, pool, parts, count, half),
         (*operands, adapter_down_weight),
         chunks_in + [VMEM],
-        [struct((all_rows, LANES), BF16)] * 2 + [TOKEN],
+        [struct((all_rows, LANES), BF16), struct((all_rows, LANES), F32), TOKEN],
         work=2 * all_rows * part * down_here * LANES,
         moved=4 << 20,
     )
     weight, marked = lax.optimization_barrier((key_value_weight, token))
     (base,) = call(
         "base",
-        functools.partial(base_kernel, pool, parts),
+        functools.partial(base_kernel, pool, parts, count, half),
         (*operands, jnp.transpose(weight, (1, 0, 2)), marked),
         chunks_in + [VMEM, ANY],
         [struct((all_rows, kv_local * pair), F32)],
@@ -322,7 +338,7 @@
     ratio = pool // tensor
     mine = None
     for j in range(ratio):
-        for m in range(0, tensor, parts):
+        for m in range(parts - 1, tensor, parts):
             pairs = [
                 (i * tensor + s, (s * ratio + ((i // tensor) ^ j)) * tensor + ((i % tensor) ^ m))
                 for i in range(pool)
@@ -356,7 +372,7 @@
     return tuple(call(
         "finish",
         functools.partial(finish_kernel, pool),
-        (expanded[0], *received[1:], queries, acc, stat),
+        (expanded[0], *[received[k] for k in [pool - 1, *range(1, pool - 1)]], queries, acc, stat),
         [VMEM] * (pool + 3),
         [struct((rows, steps_new, heads * size), BF16), struct((rows, steps_new, kv_local, pair), BF16)],
         [pltpu.VMEM((count * heads, size), F32)],

time: 36.2 us -> 34.1 us (0.942)
  starting transfers between devices: 14.4 us -> 13.2 us
  waiting for transfers between devices: 11.2 us -> 10.2 us
    ppermute x2, starting transfers between devices: 4.53 us -> 3.41 us  [body(): moved = lax.ppermute(shrink, ('pool', 'tensor'), pairs).astype(F32)]
    ppermute x2, waiting for transfers between devices: 4.53 us -> 3.78 us  [body(): moved = lax.ppermute(shrink, ('pool', 'tensor'), pairs).astype(F32)]
    ppermute x4 -> x3, waiting for transfers between devices: 1.69 us -> 0.96 us  [over_pair(): return lax.ppermute(x, 'tensor', [(i, i ^ 1) for i in range(tensor)])]
    ppermute x6, waiting for transfers between devices: 5.02 us -> 5.45 us  [over_pool(): return lax.ppermute(x, 'pool', [(i, i ^ k) for i in range(pool)])]
  transfers between devices with their start and end apart: 12 -> 11, of which waited for: 8 -> 9; matrix products, arithmetic and copies ran while one was open for 9% -> 10% of each run, Pallas kernels for 4% -> 5%
where the time goes in v3:
time: 34.1 us; the launch traced here: 33.9 us
  starting transfers between devices  13.2 us (39%)
  waiting for transfers between devices  10.2 us (30%)
  Pallas kernels  6.27 us (18%)
  local copies, waits for them, and re-layouts  3.42 us (10%)
  between operations  0.76 us (2%)
    ppermute x6, starting transfers between devices, over_pool(): return lax.ppermute(x, 'pool', [(i, i ^ k) for i in range(pool)])  9.23 us
    pallas_call x6, Pallas kernels, call(): pl.pallas_call(kernel, out_shape=outs, in_specs=in_specs, out_specs=[VMEM...  6.27 us
    ppermute x6, waiting for transfers between devices, over_pool(): return lax.ppermute(x, 'pool', [(i, i ^ k) for i in range(pool)])  5.45 us
    ppermute x2, waiting for transfers between devices, body(): moved = lax.ppermute(shrink, ('pool', 'tensor'), pairs).astype(F32)  3.78 us
    ppermute x2, starting transfers between devices, body(): moved = lax.ppermute(shrink, ('pool', 'tensor'), pairs).astype(F32)  3.41 us
    optimization_barrier x1, local copies, waits for them, and re-layouts, body(): stored, _ = lax.optimization_barrier((cache, packed[0]))  3.1 us
    ppermute x3, waiting for transfers between devices, over_pair(): return lax.ppermute(x, 'tensor', [(i, i ^ 1) for i in range(tensor)])  0.96 us
  transfers between devices with their start and end apart: 11, of which 9 were waited for; matrix products, arithmetic and copies ran while one was open for 10% of the time, Pallas kernels for 5%

profile of v3, /device:TPU:0, one launch (start us, length us, event | category | flops | bytes accessed | tf_op | source)
XLA Modules:
  0.0 33.9 jit_solution(4239998084265264290)
XLA Ops:
  0.6 1.9 %pack.1 = (bf16[528,128]{1,0:T(8,128)(2,1)}, bf16[528,128]{1,0:T(8,128)(2,1)}, bf16[272,128]{1,0:T(8,128)(2,1)}, bf16[272,128]{1,0:T(8,128)(2,1)}, s32[16,256]{1,0:T(8,128)}) custom-call(s32[16]{0:T(128)} %request_adapter.1, s32[24]{0:T(128)} %adapter_storage.1, s32[16]{0:T(128)} %lengths.1, bf16[16,2,8192]{2,1,0:T(2,128)(2,1)} %hidden.1), custom_call_target="tpu_custom_call" | custom-call | bytes 1048576 | tf_op jit(solution)/shard_map/pack/pallas_call | solution.py:274
  2.5 4.1 %collective-permute-start.2 = (bf16[272,128]{1,0:T(8,128)(2,1)}, bf16[272,128]{1,0:T(8,128)(2,1)S(1)}, u32[]{:S(2)}, u32[]{:S(2)}) collective-permute-start(bf16[272,128]{1,0:T(8,128)(2,1)} %get-tuple-element.29), channel_id=1, source_target_pairs={{0,8},{4,12},{8,0},{12,4},{1,9},{5,13},{9,1},{13,5},{2,10},{6,14},... | collective-permute-start | bytes 208904 | tf_op jit(solution)/shard_map/ppermute | solution.py:268
  6.6 1.3 %collective-permute-start.1 = (bf16[272,128]{1,0:T(8,128)(2,1)}, bf16[272,128]{1,0:T(8,128)(2,1)S(1)}, u32[]{:S(2)}, u32[]{:S(2)}) collective-permute-start(bf16[272,128]{1,0:T(8,128)(2,1)} %get-tuple-element.28), channel_id=1, source_target_pairs={{0,12},{4,8},{8,4},{12,0},{1,13},{5,9},{9,5},{13,1},{2,14},{6,10},... | collective-permute-start | bytes 208904 | tf_op jit(solution)/shard_map/ppermute | solution.py:268
  8.2 3.1 %copy.16 = bf16[16,256,2,256]{3,1,2,0:T(8,128)(2,1)S(1)} copy(bf16[16,256,2,256]{3,2,1,0:T(2,128)(2,1)} %param.12) | data formatting | bytes 8388608 | tf_op jit(solution)/shard_map/optimization_barrier | solution.py:307
  11.3 2.4 %collective-permute-done.1.refs_3_ = bf16[272,128]{1,0:T(8,128)(2,1)S(1)} collective-permute-done((bf16[272,128]{1,0:T(8,128)(2,1)}, bf16[272,128]{1,0:T(8,128)(2,1)S(1)}, u32[]{:S(2)}, u32[]{:S(2)}) %collective-permute-start.1) | collective-permute-done | bytes 69664 | tf_op jit(solution)/shard_map/ppermute | solution.py:268
  13.7 0.5 %collective-permute-start.3 = (bf16[272,128]{1,0:T(8,128)(2,1)S(1)}, bf16[272,128]{1,0:T(8,128)(2,1)S(1)}, u32[]{:S(2)}, u32[]{:S(2)}) collective-permute-start(bf16[272,128]{1,0:T(8,128)(2,1)S(1)} %collective-permute-done.2.refs_2_), channel_id=1, source_target_pairs={{0,1},{1,0},{2,3},{3,2},{4,5},{5,4},{6,7},{7,6},{8,9},{9,8},{10,11... | collective-permute-start | bytes 208904 | tf_op jit(solution)/shard_map/ppermute | solution.py:271
  14.2 0.4 %collective-permute-done.refs_1_ = bf16[528,128]{1,0:T(8,128)(2,1)S(1)} collective-permute-done((bf16[528,128]{1,0:T(8,128)(2,1)}, bf16[528,128]{1,0:T(8,128)(2,1)S(1)}, u32[]{:S(2)}, u32[]{:S(2)}) %collective-permute-start) | collective-permute-done | bytes 135200 | tf_op jit(solution)/shard_map/ppermute | solution.py:268
  14.6 0.4 %collective-permute-done.4.refs_5_ = bf16[272,128]{1,0:T(8,128)(2,1)S(1)} collective-permute-done((bf16[272,128]{1,0:T(8,128)(2,1)S(1)}, bf16[272,128]{1,0:T(8,128)(2,1)S(1)}, u32[]{:S(2)}, u32[]{:S(2)}) %collective-permute-start.4) | collective-permute-done | bytes 69664 | tf_op jit(solution)/shard_map/ppermute | solution.py:271
  15.1 0.7 %shrink.1 = (bf16[128,128]{1,0:T(8,128)(2,1)S(1)}, f32[128,128]{1,0:T(8,128)S(1)}, f32[8,128]{1,0:T(8,128)S(1)}) custom-call(bf16[528,128]{1,0:T(8,128)(2,1)S(1)} %copy-done.1, bf16[528,128]{1,0:T(8,128)(2,1)S(1)} %collective-permute-done.refs_1_, bf16[272,128]{1,0:T(8,128)(2,1)S(1)} %collective-permute-done.2.refs_2_, ...), custom_call_target="tpu_custom_call" | custom-call | flops 402653184 | bytes 4194304 | tf_op jit(solution)/shard_map/shrink/pallas_call | solution.py:274
  15.8 0.4 %collective-permute-start.5 = (bf16[128,128]{1,0:T(8,128)(2,1)S(1)}, bf16[128,128]{1,0:T(8,128)(2,1)S(1)}, u32[]{:S(2)}, u32[]{:S(2)}) collective-permute-start(bf16[128,128]{1,0:T(8,128)(2,1)S(1)} %get-tuple-element.36), channel_id=1, source_target_pairs={{0,1},{1,5},{2,9},{3,13},{4,0},{5,4},{6,8},{7,12},{8,3},{9,7},{10,... | collective-permute-start | bytes 98312 | tf_op jit(solution)/shard_map/ppermute | solution.py:347
  16.2 3.0 %collective-permute-start.6 = (bf16[128,128]{1,0:T(8,128)(2,1)S(1)}, bf16[128,128]{1,0:T(8,128)(2,1)S(1)}, u32[]{:S(2)}, u32[]{:S(2)}) collective-permute-start(bf16[128,128]{1,0:T(8,128)(2,1)S(1)} %get-tuple-element.36), channel_id=1, source_target_pairs={{0,3},{1,7},{2,11},{3,15},{4,2},{5,6},{6,10},{7,14},{8,1},{9,5},{1... | collective-permute-start | bytes 98312 | tf_op jit(solution)/shard_map/ppermute | solution.py:347
  19.2 0.6 %collective-permute-done.5 = bf16[128,128]{1,0:T(8,128)(2,1)S(1)} collective-permute-done((bf16[128,128]{1,0:T(8,128)(2,1)S(1)}, bf16[128,128]{1,0:T(8,128)(2,1)S(1)}, u32[]{:S(2)}, u32[]{:S(2)}) %collective-permute-start.5) | collective-permute-done | bytes 32800 | tf_op jit(solution)/shard_map/ppermute | solution.py:347
  19.8 3.2 %collective-permute-done.6 = bf16[128,128]{1,0:T(8,128)(2,1)S(1)} collective-permute-done((bf16[128,128]{1,0:T(8,128)(2,1)S(1)}, bf16[128,128]{1,0:T(8,128)(2,1)S(1)}, u32[]{:S(2)}, u32[]{:S(2)}) %collective-permute-start.6) | collective-permute-done | bytes 32800 | tf_op jit(solution)/shard_map/ppermute | solution.py:347
  23.1 0.3 copy.17
  23.4 0.5 %base.1.refs_3_ = f32[128,512]{1,0:T(8,128)S(1)} custom-call(bf16[528,128]{1,0:T(8,128)(2,1)S(1)} %copy-done.1, bf16[528,128]{1,0:T(8,128)(2,1)S(1)} %collective-permute-done.refs_1_, bf16[272,128]{1,0:T(8,128)(2,1)S(1)} %collective-permute-done.2.refs_2_, bf16[272,128]{1,0:T(8,128)(2,1)S(1)} %collective-permute-done.1.refs_3_, ...), custom_call_target="tpu_custom_call" | custom-call | flops 268435456 | bytes 3145728 | tf_op jit(solution)/shard_map/base/pallas_call | solution.py:274
  23.9 0.4 %collective-permute-done.7.refs_1_ = f32[128,128]{1,0:T(8,128)S(1)} collective-permute-done((f32[128,128]{1,0:T(8,128)S(1)}, f32[128,128]{1,0:T(8,128)S(1)}, u32[]{:S(2)}, u32[]{:S(2)}) %collective-permute-start.7) | collective-permute-done | bytes 65568 | tf_op jit(solution)/shard_map/ppermute | solution.py:271
  24.3 0.7 %expand.1 = (f32[32,512]{1,0:T(8,128)S(1)}, bf16[32,512]{1,0:T(8,128)(2,1)S(1)}, bf16[32,512]{1,0:T(8,128)(2,1)S(1)}, bf16[32,512]{1,0:T(8,128)(2,1)S(1)}, f32[8,128]{1,0:T(8,128)S(1)}) custom-call(f32[128,128]{1,0:T(8,128)S(1)} %convert_add_fusion.refs_0_, f32[128,128]{1,0:T(8,128)S(1)} %collective-permute-done.7.refs_1_, ...), custom_call_target="tpu_custom_call" | custom-call | flops 50331648 | bytes 1048576 | tf_op jit(solution)/shard_map/expand/pallas_call | solution.py:274
  25.0 1.7 %collective-permute-start.10 = (bf16[32,512]{1,0:T(8,128)(2,1)S(1)}, bf16[32,512]{1,0:T(8,128)(2,1)S(1)}, u32[]{:S(2)}, u32[]{:S(2)}) collective-permute-start(bf16[32,512]{1,0:T(8,128)(2,1)S(1)} %get-tuple-element.44), channel_id=1, source_target_pairs={{0,8},{4,12},{8,0},{12,4},{1,9},{5,13},{9,1},{13,5},{2,10},{6,14},... | collective-permute-start | bytes 98312 | tf_op jit(solution)/shard_map/ppermute | solution.py:268
  26.7 0.6 %collective-permute-start.8 = (bf16[32,512]{1,0:T(8,128)(2,1)S(1)}, bf16[32,512]{1,0:T(8,128)(2,1)S(1)}, u32[]{:S(2)}, u32[]{:S(2)}) collective-permute-start(bf16[32,512]{1,0:T(8,128)(2,1)S(1)} %get-tuple-element.42), channel_id=1, source_target_pairs={{0,12},{4,8},{8,4},{12,0},{1,13},{5,9},{9,5},{13,1},{2,14},{6,10},... | collective-permute-start | bytes 98312 | tf_op jit(solution)/shard_map/ppermute | solution.py:268
  27.3 1.2 %collective-permute-start.9 = (bf16[32,512]{1,0:T(8,128)(2,1)S(1)}, bf16[32,512]{1,0:T(8,128)(2,1)S(1)}, u32[]{:S(2)}, u32[]{:S(2)}) collective-permute-start(bf16[32,512]{1,0:T(8,128)(2,1)S(1)} %get-tuple-element.43), channel_id=1, source_target_pairs={{0,4},{4,0},{8,12},{12,8},{1,5},{5,1},{9,13},{13,9},{2,6},{6,2},{1... | collective-permute-start | bytes 98312 | tf_op jit(solution)/shard_map/ppermute | solution.py:268
  28.6 1.1 %cached.1 = (f32[512,128]{1,0:T(8,128)S(1)}, f32[512,128]{1,0:T(8,128)S(1)}) custom-call(s32[16,256]{1,0:T(8,128)S(1)} %copy-done.5, bf16[16,2,16,128]{3,2,1,0:T(8,128)(2,1)S(1)} %copy-done.2, bf16[16,2,256,256]{3,2,1,0:T(8,128)(2,1)S(1)} %bitcast.6, f32[8,128]{1,0:T(8,128)S(1)} %get-tuple-element.47._), custom_call_target="tpu_custom_call" | custom-call | flops 134217728 | bytes 4194304 | tf_op jit(solution)/shard_map/cached/pallas_call | solution.py:274
  29.7 0.5 %collective-permute-done.10.refs_2_ = bf16[32,512]{1,0:T(8,128)(2,1)S(1)} collective-permute-done((bf16[32,512]{1,0:T(8,128)(2,1)S(1)}, bf16[32,512]{1,0:T(8,128)(2,1)S(1)}, u32[]{:S(2)}, u32[]{:S(2)}) %collective-permute-start.10) | collective-permute-done | bytes 32800 | tf_op jit(solution)/shard_map/ppermute | solution.py:268
  30.2 2.2 %collective-permute-done.8.refs_0_ = bf16[32,512]{1,0:T(8,128)(2,1)S(1)} collective-permute-done((bf16[32,512]{1,0:T(8,128)(2,1)S(1)}, bf16[32,512]{1,0:T(8,128)(2,1)S(1)}, u32[]{:S(2)}, u32[]{:S(2)}) %collective-permute-start.8) | collective-permute-done | bytes 32800 | tf_op jit(solution)/shard_map/ppermute | solution.py:268
  32.4 1.5 %finish.1 = (bf16[16,2,2048]{2,1,0:T(2,128)(2,1)}, bf16[16,2,2,256]{3,2,1,0:T(2,128)(2,1)}) custom-call(f32[32,512]{1,0:T(8,128)S(1)} %get-tuple-element.41.own, bf16[32,512]{1,0:T(8,128)(2,1)S(1)} %collective-permute-done.8.refs_0_, bf16[32,512]{1,0:T(8,128)(2,1)S(1)} %collective-permute-done.9.refs_1_, ...), custom_call_target="tpu_custom_call" | custom-call | flops 33554432 | bytes 1048576 | tf_op jit(solution)/shard_map/finish/pallas_call | solution.py:274
  (21 shorter events, 0.5 us)
Async XLA Ops:
  2.5 8.8 %collective-permute-start.2 = (bf16[272,128]{1,0:T(8,128)(2,1)}, bf16[272,128]{1,0:T(8,128)(2,1)S(1)}, u32[]{:S(2)}, u32[]{:S(2)}) collective-permute-start(bf16[272,128]{1,0:T(8,128)(2,1)} %get-tuple-element.29), channel_id=1, source_target_pairs={{0,8},{4,12},{8,0},{12,4},{1,9},{5,13},{9,1},{13,5},{2,10},{6,14},... | collective-permute-start | bytes 208904 | tf_op jit(solution)/shard_map/ppermute | solution.py:268
  6.6 7.1 %collective-permute-start.1 = (bf16[272,128]{1,0:T(8,128)(2,1)}, bf16[272,128]{1,0:T(8,128)(2,1)S(1)}, u32[]{:S(2)}, u32[]{:S(2)}) collective-permute-start(bf16[272,128]{1,0:T(8,128)(2,1)} %get-tuple-element.28), channel_id=1, source_target_pairs={{0,12},{4,8},{8,4},{12,0},{1,13},{5,9},{9,5},{13,1},{2,14},{6,10},... | collective-permute-start | bytes 208904 | tf_op jit(solution)/shard_map/ppermute | solution.py:268
  7.9 6.6 %collective-permute-start = (bf16[528,128]{1,0:T(8,128)(2,1)}, bf16[528,128]{1,0:T(8,128)(2,1)S(1)}, u32[]{:S(2)}, u32[]{:S(2)}) collective-permute-start(bf16[528,128]{1,0:T(8,128)(2,1)} %get-tuple-element.27), channel_id=1, source_target_pairs={{0,4},{4,0},{8,12},{12,8},{1,5},{5,1},{9,13},{13,9},{2,6},{6,2},{1... | collective-permute-start | bytes 405512 | tf_op jit(solution)/shard_map/ppermute | solution.py:268
  8.2 6.9 %copy-start = (bf16[6,2048,128]{2,1,0:T(8,128)(2,1)S(1)}, bf16[6,2048,128]{2,1,0:T(8,128)(2,1)}, u32[]{:S(2)}) copy-start(bf16[6,2048,128]{2,1,0:T(8,128)(2,1)} %refs_6_.1) | copy-start | bytes 9437188
  8.2 6.9 %copy-start.1 = (bf16[528,128]{1,0:T(8,128)(2,1)S(1)}, bf16[528,128]{1,0:T(8,128)(2,1)}, u32[]{:S(2)}) copy-start(bf16[528,128]{1,0:T(8,128)(2,1)} %get-tuple-element.26.refs_0_) | copy-start | bytes 405508
  11.3 11.8 %copy-start.6 = (bf16[2048,2,256]{2,1,0:T(2,128)(2,1)S(1)}, bf16[2048,2,256]{2,1,0:T(2,128)(2,1)}, u32[]{:S(2)}) copy-start(bf16[2048,2,256]{2,1,0:T(2,128)(2,1)} %param.13) | copy-start | bytes 6291460
  13.7 1.3 %collective-permute-start.4 = (bf16[272,128]{1,0:T(8,128)(2,1)S(1)}, bf16[272,128]{1,0:T(8,128)(2,1)S(1)}, u32[]{:S(2)}, u32[]{:S(2)}) collective-permute-start(bf16[272,128]{1,0:T(8,128)(2,1)S(1)} %collective-permute-done.1.refs_3_), channel_id=1, source_target_pairs={{0,1},{1,0},{2,3},{3,2},{4,5},{5,4},{6,7},{7,6},{8,9},{9,8},{10,11... | collective-permute-start | bytes 208904 | tf_op jit(solution)/shard_map/ppermute | solution.py:271
  13.7 1.4 %collective-permute-start.3 = (bf16[272,128]{1,0:T(8,128)(2,1)S(1)}, bf16[272,128]{1,0:T(8,128)(2,1)S(1)}, u32[]{:S(2)}, u32[]{:S(2)}) collective-permute-start(bf16[272,128]{1,0:T(8,128)(2,1)S(1)} %collective-permute-done.2.refs_2_), channel_id=1, source_target_pairs={{0,1},{1,0},{2,3},{3,2},{4,5},{5,4},{6,7},{7,6},{8,9},{9,8},{10,11... | collective-permute-start | bytes 208904 | tf_op jit(solution)/shard_map/ppermute | solution.py:271
  15.8 4.0 %collective-permute-start.5 = (bf16[128,128]{1,0:T(8,128)(2,1)S(1)}, bf16[128,128]{1,0:T(8,128)(2,1)S(1)}, u32[]{:S(2)}, u32[]{:S(2)}) collective-permute-start(bf16[128,128]{1,0:T(8,128)(2,1)S(1)} %get-tuple-element.36), channel_id=1, source_target_pairs={{0,1},{1,5},{2,9},{3,13},{4,0},{5,4},{6,8},{7,12},{8,3},{9,7},{10,... | collective-permute-start | bytes 98312 | tf_op jit(solution)/shard_map/ppermute | solution.py:347
  16.2 6.8 %collective-permute-start.6 = (bf16[128,128]{1,0:T(8,128)(2,1)S(1)}, bf16[128,128]{1,0:T(8,128)(2,1)S(1)}, u32[]{:S(2)}, u32[]{:S(2)}) collective-permute-start(bf16[128,128]{1,0:T(8,128)(2,1)S(1)} %get-tuple-element.36), channel_id=1, source_target_pairs={{0,3},{1,7},{2,11},{3,15},{4,2},{5,6},{6,10},{7,14},{8,1},{9,5},{1... | collective-permute-start | bytes 98312 | tf_op jit(solution)/shard_map/ppermute | solution.py:347
  23.0 1.3 %collective-permute-start.7 = (f32[128,128]{1,0:T(8,128)S(1)}, f32[128,128]{1,0:T(8,128)S(1)}, u32[]{:S(2)}, u32[]{:S(2)}) collective-permute-start(f32[128,128]{1,0:T(8,128)S(1)} %convert_add_fusion.refs_0_), channel_id=1, source_target_pairs={{0,1},{1,0},{2,3},{3,2},{4,5},{5,4},{6,7},{7,6},{8,9},{9,8},{10,11... | collective-permute-start | bytes 196616 | tf_op jit(solution)/shard_map/ppermute | solution.py:271
  23.1 1.2 %copy-start.3 = (bf16[6,64,2,128]{3,2,1,0:T(2,128)(2,1)S(1)}, bf16[6,64,2,128]{3,2,1,0:T(2,128)(2,1)}, u32[]{:S(2)}) copy-start(bf16[6,64,2,128]{3,2,1,0:T(2,128)(2,1)} %refs_4_.1) | copy-start | bytes 589828
  23.1 1.2 %copy-start.4 = (bf16[6,64,2,128]{3,2,1,0:T(2,128)(2,1)S(1)}, bf16[6,64,2,128]{3,2,1,0:T(2,128)(2,1)}, u32[]{:S(2)}) copy-start(bf16[6,64,2,128]{3,2,1,0:T(2,128)(2,1)} %refs_5_.1) | copy-start | bytes 589828
  23.1 5.4 %copy-start.2 = (bf16[16,2,16,128]{3,2,1,0:T(8,128)(2,1)S(1)}, bf16[16,2,16,128]{3,2,1,0:T(8,128)(2,1)}, u32[]{:S(2)}) copy-start(bf16[16,2,16,128]{3,2,1,0:T(8,128)(2,1)} %refs_3_.1) | copy-start | bytes 393220
  23.1 5.4 %copy-start.5 = (s32[16,256]{1,0:T(8,128)S(1)}, s32[16,256]{1,0:T(8,128)}, u32[]{:S(2)}) copy-start(s32[16,256]{1,0:T(8,128)} %get-tuple-element.45.spans) | copy-start | bytes 49156
  25.0 5.2 %collective-permute-start.10 = (bf16[32,512]{1,0:T(8,128)(2,1)S(1)}, bf16[32,512]{1,0:T(8,128)(2,1)S(1)}, u32[]{:S(2)}, u32[]{:S(2)}) collective-permute-start(bf16[32,512]{1,0:T(8,128)(2,1)S(1)} %get-tuple-element.44), channel_id=1, source_target_pairs={{0,8},{4,12},{8,0},{12,4},{1,9},{5,13},{9,1},{13,5},{2,10},{6,14},... | collective-permute-start | bytes 98312 | tf_op jit(solution)/shard_map/ppermute | solution.py:268
  26.7 5.7 %collective-permute-start.8 = (bf16[32,512]{1,0:T(8,128)(2,1)S(1)}, bf16[32,512]{1,0:T(8,128)(2,1)S(1)}, u32[]{:S(2)}, u32[]{:S(2)}) collective-permute-start(bf16[32,512]{1,0:T(8,128)(2,1)S(1)} %get-tuple-element.42), channel_id=1, source_target_pairs={{0,12},{4,8},{8,4},{12,0},{1,13},{5,9},{9,5},{13,1},{2,14},{6,10},... | collective-permute-start | bytes 98312 | tf_op jit(solution)/shard_map/ppermute | solution.py:268
  27.3 5.1 %collective-permute-start.9 = (bf16[32,512]{1,0:T(8,128)(2,1)S(1)}, bf16[32,512]{1,0:T(8,128)(2,1)S(1)}, u32[]{:S(2)}, u32[]{:S(2)}) collective-permute-start(bf16[32,512]{1,0:T(8,128)(2,1)S(1)} %get-tuple-element.43), channel_id=1, source_target_pairs={{0,4},{4,0},{8,12},{12,8},{1,5},{5,1},{9,13},{13,9},{2,6},{6,2},{1... | collective-permute-start | bytes 98312 | tf_op jit(solution)/shard_map/ppermute | solution.py:268

commit v4 on v3

--- a/solution.py
+++ b/solution.py
@@ -124,8 +124,14 @@
 
 
 def base_kernel(pool, parts, count, half, *refs):
-    weight, _, base = refs[-3:]
-    sides = both_sides(pool, parts, count, half, refs[:-3])
+    weight, up_key, up_value, _, base, key_table, value_table, token = refs[-8:]
+    token[...] = jnp.zeros_like(token)
+    sides = both_sides(pool, parts, count, half, refs[:-8])
+    holders, rank, kv_local, size = up_key.shape
+    for a in range(holders):
+        at = slice(a * rank * kv_local, (a + 1) * rank * kv_local)
+        key_table[at, :] = up_key[a].reshape(rank * kv_local, size)
+        value_table[at, :] = up_value[a].reshape(rank * kv_local, size)
     for k in range(weight.shape[0]):
         out = 0.0
         for at, x in sides:
@@ -133,15 +139,16 @@
         base[:, k * weight.shape[2]:(k + 1) * weight.shape[2]] = out
 
 
-def expand_kernel(pool, parts, *refs):
+def expand_kernel(pool, parts, rank, kv_local, *refs):
     sums, refs = refs[:parts], refs[parts:]
-    slots_in, base, up_key, up_value = refs[:4]
-    outs, token, scratch = refs[4:4 + pool], refs[4 + pool], refs[5 + pool]
+    slots_in, base = refs[:2]
+    tables, (outs, token, scratch) = refs[2:4], (refs[4:4 + pool], refs[4 + pool], refs[5 + pool])
     token[...] = jnp.zeros_like(token)
-    holders, rank, kv_local, size = up_key.shape
+    count = base.shape[0] // pool
+    deep, size = rank * kv_local, tables[0].shape[1]
+    holders = tables[0].shape[0] // deep
     me = lax.axis_index("pool")
     first_slot = me * holders
-    count = base.shape[0] // pool
     total = sums[0][...]
     for s in sums[1:]:
         total = total + s[...]
@@ -149,32 +156,28 @@
     ordered = jnp.concatenate(
         [scratch[pl.ds(pl.multiple_of((me ^ k) * count, count), count), :] for k in range(pool)], axis=0
     ).astype(BF16)
-    slots = slots_in[...]
-    deep = rank * kv_local
-    for which, up in ((0, up_key), (1, up_value)):
-        row = lax.broadcasted_iota(jnp.int32, (2 * rank, deep), 0)
-        col = lax.broadcasted_iota(jnp.int32, (2 * rank, deep), 1)
+    slots = jnp.concatenate([slots_in[:, :deep]] * kv_local, axis=0)
+    row = lax.broadcasted_iota(jnp.int32, (2 * rank, deep), 0)
+    col = lax.broadcasted_iota(jnp.int32, (2 * rank, deep), 1)
+    for which, table in enumerate(tables):
         wide = []
         for k in range(kv_local):
             pick = (row == which * rank + col // kv_local) & (col % kv_local == k)
             wide.append(dot(ordered, pick.astype(F32).astype(BF16)))
-        acc = [jnp.zeros((base.shape[0], size), F32) for _ in range(kv_local)]
-        for a in range(holders):
-            match = slots == (first_slot + a).astype(F32)
-            if deep != LANES:
-                match = match[:, :1]
-            table = up[a].reshape(deep, size)
-            for k in range(kv_local):
-                acc[k] = acc[k] + dot(jnp.where(match, wide[k], 0.0).astype(BF16), table)
+        wide = jnp.concatenate(wide, axis=0)
+        spread = [
+            jnp.where(slots == (first_slot + a).astype(F32), wide, 0.0).astype(BF16) for a in range(holders)
+        ]
+        delta = dot(jnp.concatenate(spread, axis=1), table[...])
         for k in range(kv_local):
             at = slice((2 * k + which) * size, (2 * k + which + 1) * size)
-            value = base[:, at] + ADAPTER_SCALE * acc[k]
+            value = base[:, at] + ADAPTER_SCALE * delta[k * base.shape[0]:(k + 1) * base.shape[0]]
             outs[0][:, at] = value[:count]
             for j in range(1, pool):
                 outs[j][:, at] = value[j * count:(j + 1) * count].astype(BF16)
 
 
-def cache_kernel(spans, queries, cache, _, acc_out, stat_out, scores_all, weights_all):
+def cache_kernel(spans, queries, cache, _, acc_out, top_out, total_out, bias_out, scores_all, weights_all):
     rows, steps_new, heads, size = queries.shape
     kv_local, depth = cache.shape[1:3]
     count = steps_new * heads
@@ -191,8 +194,18 @@
     top = jnp.max(scores, axis=1, keepdims=True)
     weights = jnp.exp(scores - top)
     total = jnp.sum(weights, axis=1, keepdims=True)
-    lane = lax.broadcasted_iota(jnp.int32, (rows * count, LANES), 1)
-    stat_out[...] = jnp.where(lane == 0, top, total)
+    top_out[...] = jnp.broadcast_to(top, top_out.shape)
+    total_out[...] = jnp.broadcast_to(total, total_out.shape)
+    fresh = rows * steps_new
+    column = lax.broadcasted_iota(jnp.int32, bias_out.shape, 1)
+    line = lax.broadcasted_iota(jnp.int32, bias_out.shape, 0)
+    token, other = line // heads, column % fresh
+    valid = (
+        (token // steps_new == other // steps_new)
+        & (other <= token)
+        & (line % heads // (heads // kv_local) == column // fresh)
+    )
+    bias_out[...] = jnp.where(valid, 0.0, -1e30)
     weights_all[...] = weights.astype(BF16)
     for r in range(rows):
         weights = weights_all[r * count:(r + 1) * count, :]
@@ -204,11 +217,10 @@
 
 def finish_kernel(pool, own, *refs):
     parts, refs = refs[:pool - 1], refs[pool - 1:]
-    queries, acc, stat, attended, fresh_out, scratch = refs
+    queries, acc, top_before, total_before, bias, attended, fresh_out, scratch = refs
     rows, steps_new, heads, size = queries.shape
     count = rows * steps_new
     kv_local = own.shape[1] // (2 * size)
-    group = heads // kv_local
     total = own[...]
     for part in parts:
         total = total + part[...].astype(F32)
@@ -217,24 +229,12 @@
     fresh_out[...] = jnp.stack([fresh[:, k * wide:(k + 1) * wide] for k in range(kv_local)], axis=1).reshape(fresh_out.shape)
     keys = jnp.concatenate([fresh[:, 2 * k * size:(2 * k + 1) * size] for k in range(kv_local)], axis=0)
     values = jnp.concatenate([fresh[:, (2 * k + 1) * size:(2 * k + 2) * size] for k in range(kv_local)], axis=0)
-    scores = dot_t(queries[...].reshape(count * heads, size), keys) * size ** -0.5
-    col = lax.broadcasted_iota(jnp.int32, scores.shape, 1)
-    row = lax.broadcasted_iota(jnp.int32, scores.shape, 0)
-    token, other = row // heads, col % count
-    valid = (
-        (token // steps_new == other // steps_new)
-        & (other <= token)
-        & (row % heads // group == col // count)
-    )
-    scores = jnp.where(valid, scores, -1e30)
-    stat = stat[...]
-    top_before, total_before = stat[:, :1], stat[:, 1:2]
-    top = jnp.maximum(top_before, jnp.max(scores, axis=1, keepdims=True))
-    weights = jnp.exp(scores - top)
-    keep = jnp.exp(top_before - top)
-    norm = 1.0 / (total_before * keep + jnp.sum(weights, axis=1, keepdims=True))
-    mixed = acc[...] * keep + dot(weights.astype(BF16), values)
-    scratch[...] = mixed * norm
+    scores = dot_t(queries[...].reshape(count * heads, size), keys) * size ** -0.5 + bias[...]
+    top = jnp.maximum(top_before[...], jnp.max(scores, axis=1, keepdims=True))
+    weights = jnp.exp(scores - top[:, :scores.shape[1]])
+    keep = jnp.exp(top_before[...] - top)
+    norm = 1.0 / (total_before[...] * keep + jnp.sum(weights, axis=1, keepdims=True))
+    scratch[...] = (acc[...] * keep + dot(weights.astype(BF16), values)) * norm
     for h in range(heads):
         out = scratch[pl.ds(h, count, stride=heads), :].astype(BF16)
         attended[:, :, h * size:(h + 1) * size] = out.reshape(rows, steps_new, size)
@@ -289,7 +289,7 @@
     packed = call(
         "pack",
         functools.partial(pack_kernel, pool, parts),
-        (request_adapter, adapter_storage, lengths, hidden),
+        tuple(pltpu.with_memory_space_constraint(x, pltpu.HBM) for x in (request_adapter, adapter_storage, lengths, hidden)),
         [HBM] * 4,
         chunks + [struct((rows, cache.shape[1]), jnp.int32)],
         [
@@ -299,7 +299,6 @@
             pltpu.SMEM(lengths.shape, jnp.int32),
             pltpu.SemaphoreType.DMA((3 + pieces,)),
         ],
-        limit=PACK,
     )
     operands = [packed[0]] + [None] * (pool - 1)
     for k in range(pool - 1, 0, -1):
@@ -325,12 +324,14 @@
         moved=4 << 20,
     )
     weight, marked = lax.optimization_barrier((key_value_weight, token))
-    (base,) = call(
+    _, rank, _, size = adapter_up_key.shape
+    table = struct((up_here * rank * kv_local, size), BF16)
+    base, key_table, value_table, token = call(
         "base",
         functools.partial(base_kernel, pool, parts, count, half),
-        (*operands, jnp.transpose(weight, (1, 0, 2)), marked),
-        chunks_in + [VMEM, ANY],
-        [struct((all_rows, kv_local * pair), F32)],
+        (*operands, jnp.transpose(weight, (1, 0, 2)), adapter_up_key, adapter_up_value, marked),
+        chunks_in + [VMEM] * 3 + [ANY],
+        [struct((all_rows, kv_local * pair), F32), table, table, TOKEN],
         work=2 * all_rows * part * kv_local * pair,
         moved=3 << 20,
     )
@@ -346,11 +347,12 @@
             ]
             moved = lax.ppermute(shrink, ("pool", "tensor"), pairs).astype(F32)
             mine = moved if mine is None else mine + moved
+    mine = mine + token[:1]
     sums = [mine] + ([over_pair(mine)] if parts == 2 else [])
     expanded = call(
         "expand",
-        functools.partial(expand_kernel, pool, parts),
-        (*sums, slots, base, adapter_up_key, adapter_up_value),
+        functools.partial(expand_kernel, pool, parts, rank, kv_local),
+        (*sums, slots, base, key_table, value_table),
         [VMEM] * (parts + 4),
         [struct((count, kv_local * pair), F32)] + [struct((count, kv_local * pair), BF16)] * (pool - 1) + [TOKEN],
         [pltpu.VMEM((all_rows, LANES), F32)],
@@ -359,12 +361,12 @@
     received = [None] * pool
     for k in range(pool - 1, 0, -1):
         received[k] = over_pool(expanded[k], k)
-    acc, stat = call(
+    acc, top, total, bias = call(
         "cached",
         cache_kernel,
         (packed[-1], queries, stored, expanded[pool]),
         [VMEM] * 3 + [ANY],
-        [struct((count * heads, n), F32) for n in (size, LANES)],
+        [struct((count * heads, n), F32) for n in (size, size, size, count * kv_local)],
         [pltpu.VMEM((count * heads, cache.shape[1]), t) for t in (F32, BF16)],
         work=4 * count * heads * cache.shape[1] * kv_local * size,
         moved=cache.size * 2,
@@ -372,8 +374,8 @@
     return tuple(call(
         "finish",
         functools.partial(finish_kernel, pool),
-        (expanded[0], *[received[k] for k in [pool - 1, *range(1, pool - 1)]], queries, acc, stat),
-        [VMEM] * (pool + 3),
+        (expanded[0], *[received[k] for k in [2, 1, *range(3, pool)]], queries, acc, top, total, bias),
+        [VMEM] * (pool + 5),
         [struct((rows, steps_new, heads * size), BF16), struct((rows, steps_new, kv_local, pair), BF16)],
         [pltpu.VMEM((count * heads, size), F32)],
         work=4 * count * heads * size * LANES,

time: 34.1 us -> 32.3 us (0.947)
  waiting for transfers between devices: 10.2 us -> 8.18 us
  starting transfers between devices: 13.2 us -> 14.2 us
  Pallas kernels: 6.27 us -> 5.53 us
    ppermute x6, waiting for transfers between devices: 5.45 us -> 3.68 us  [over_pool(): return lax.ppermute(x, 'pool', [(i, i ^ k) for i in range(pool)])]
    ppermute x2, waiting for transfers between devices: 3.78 us -> 2.73 us  [body(): moved = lax.ppermute(shrink, ('pool', 'tensor'), pairs).astype(F32)]
    ppermute x6, starting transfers between devices: 9.23 us -> 10.1 us  [over_pool(): return lax.ppermute(x, 'pool', [(i, i ^ k) for i in range(pool)])]
    ppermute x3, waiting for transfers between devices: 0.96 us -> 1.77 us  [over_pair(): return lax.ppermute(x, 'tensor', [(i, i ^ 1) for i in range(tensor)])]
    pallas_call x6, Pallas kernels: 6.27 us -> 5.53 us  [call(): pl.pallas_call(kernel, out_shape=outs, in_specs=in_specs, out_specs=[VMEM...]
  transfers between devices with their start and end apart: 11 -> 11, of which waited for: 9 -> 8; matrix products, arithmetic and copies ran while one was open for 10% -> 11% of each run, Pallas kernels for 5% -> 6%
where the time goes in v4:
time: 32.3 us; the launch traced here: 32.1 us
  starting transfers between devices  14.2 us (44%)
  waiting for transfers between devices  8.18 us (25%)
  Pallas kernels  5.53 us (17%)
  local copies, waits for them, and re-layouts  3.41 us (11%)
  between operations  0.76 us (2%)
    ppermute x6, starting transfers between devices, over_pool(): return lax.ppermute(x, 'pool', [(i, i ^ k) for i in range(pool)])  10.1 us
    pallas_call x6, Pallas kernels, call(): pl.pallas_call(kernel, out_shape=outs, in_specs=in_specs, out_specs=[VMEM...  5.53 us
    ppermute x6, waiting for transfers between devices, over_pool(): return lax.ppermute(x, 'pool', [(i, i ^ k) for i in range(pool)])  3.68 us
    ppermute x2, starting transfers between devices, body(): moved = lax.ppermute(shrink, ('pool', 'tensor'), pairs).astype(F32)  3.47 us
    optimization_barrier x1, local copies, waits for them, and re-layouts, body(): stored, _ = lax.optimization_barrier((cache, packed[0]))  3.1 us
    ppermute x2, waiting for transfers between devices, body(): moved = lax.ppermute(shrink, ('pool', 'tensor'), pairs).astype(F32)  2.73 us
    ppermute x3, waiting for transfers between devices, over_pair(): return lax.ppermute(x, 'tensor', [(i, i ^ 1) for i in range(tensor)])  1.77 us
  transfers between devices with their start and end apart: 11, of which 8 were waited for; matrix products, arithmetic and copies ran while one was open for 11% of the time, Pallas kernels for 6%

profile of v4, /device:TPU:0, one launch (start us, length us, event | category | flops | bytes accessed | tf_op | source)
XLA Modules:
  0.0 32.1 jit_solution(13912179665520997925)
XLA Ops:
  0.6 1.1 %pack.1 = (bf16[528,128]{1,0:T(8,128)(2,1)S(1)}, bf16[528,128]{1,0:T(8,128)(2,1)S(1)}, bf16[272,128]{1,0:T(8,128)(2,1)S(1)}, bf16[272,128]{1,0:T(8,128)(2,1)S(1)}, s32[16,256]{1,0:T(8,128)S(1)}) custom-call(s32[16]{0:T(128)} %request_adapter.1, s32[24]{0:T(128)} %adapter_storage.1, s32[16]{0:T(128)} %lengths.1, bf16[16,2,8192]{2,1,0:T(2,128)(2,1)} %hidden.1), custom_call_target="tpu_custom_call" | custom-call | bytes 1048576 | tf_op jit(solution)/shard_map/pack/pallas_call | solution.py:274
  1.8 4.1 %collective-permute-start.2 = (bf16[272,128]{1,0:T(8,128)(2,1)S(1)}, bf16[272,128]{1,0:T(8,128)(2,1)S(1)}, u32[]{:S(2)}, u32[]{:S(2)}) collective-permute-start(bf16[272,128]{1,0:T(8,128)(2,1)S(1)} %get-tuple-element.35), channel_id=1, source_target_pairs={{0,8},{4,12},{8,0},{12,4},{1,9},{5,13},{9,1},{13,5},{2,10},{6,14},... | collective-permute-start | bytes 208904 | tf_op jit(solution)/shard_map/ppermute | solution.py:268
  5.9 1.3 %collective-permute-start.1 = (bf16[272,128]{1,0:T(8,128)(2,1)S(1)}, bf16[272,128]{1,0:T(8,128)(2,1)S(1)}, u32[]{:S(2)}, u32[]{:S(2)}) collective-permute-start(bf16[272,128]{1,0:T(8,128)(2,1)S(1)} %get-tuple-element.34), channel_id=1, source_target_pairs={{0,12},{4,8},{8,4},{12,0},{1,13},{5,9},{9,5},{13,1},{2,14},{6,10},... | collective-permute-start | bytes 208904 | tf_op jit(solution)/shard_map/ppermute | solution.py:268
  7.2 0.2 collective-permute-start
  7.4 3.1 %copy.16 = bf16[16,256,2,256]{3,1,2,0:T(8,128)(2,1)S(1)} copy(bf16[16,256,2,256]{3,2,1,0:T(2,128)(2,1)} %param.12) | data formatting | bytes 8388608 | tf_op jit(solution)/shard_map/optimization_barrier | solution.py:306
  10.6 2.1 %collective-permute-done.1.refs_3_ = bf16[272,128]{1,0:T(8,128)(2,1)S(1)} collective-permute-done((bf16[272,128]{1,0:T(8,128)(2,1)S(1)}, bf16[272,128]{1,0:T(8,128)(2,1)S(1)}, u32[]{:S(2)}, u32[]{:S(2)}) %collective-permute-start.1) | collective-permute-done | bytes 69664 | tf_op jit(solution)/shard_map/ppermute | solution.py:268
  12.7 0.5 %collective-permute-start.3 = (bf16[272,128]{1,0:T(8,128)(2,1)S(1)}, bf16[272,128]{1,0:T(8,128)(2,1)S(1)}, u32[]{:S(2)}, u32[]{:S(2)}) collective-permute-start(bf16[272,128]{1,0:T(8,128)(2,1)S(1)} %collective-permute-done.2.refs_2_), channel_id=1, source_target_pairs={{0,1},{1,0},{2,3},{3,2},{4,5},{5,4},{6,7},{7,6},{8,9},{9,8},{10,11... | collective-permute-start | bytes 208904 | tf_op jit(solution)/shard_map/ppermute | solution.py:271
  13.3 0.4 %collective-permute-done.refs_1_ = bf16[528,128]{1,0:T(8,128)(2,1)S(1)} collective-permute-done((bf16[528,128]{1,0:T(8,128)(2,1)S(1)}, bf16[528,128]{1,0:T(8,128)(2,1)S(1)}, u32[]{:S(2)}, u32[]{:S(2)}) %collective-permute-start) | collective-permute-done | bytes 135200 | tf_op jit(solution)/shard_map/ppermute | solution.py:268
  13.6 0.4 %collective-permute-done.4.refs_5_ = bf16[272,128]{1,0:T(8,128)(2,1)S(1)} collective-permute-done((bf16[272,128]{1,0:T(8,128)(2,1)S(1)}, bf16[272,128]{1,0:T(8,128)(2,1)S(1)}, u32[]{:S(2)}, u32[]{:S(2)}) %collective-permute-start.4) | collective-permute-done | bytes 69664 | tf_op jit(solution)/shard_map/ppermute | solution.py:271
  14.0 0.2 collective-permute-done.3.refs_4_
  14.2 0.7 %shrink.1 = (bf16[128,128]{1,0:T(8,128)(2,1)S(1)}, f32[128,128]{1,0:T(8,128)S(1)}, f32[8,128]{1,0:T(8,128)S(1)}) custom-call(bf16[528,128]{1,0:T(8,128)(2,1)S(1)} %get-tuple-element.32.refs_0_, bf16[528,128]{1,0:T(8,128)(2,1)S(1)} %collective-permute-done.refs_1_, bf16[272,128]{1,0:T(8,128)(2,1)S(1)} %collective-permute-done.2.refs_2_, ...), custom_call_target="tpu_custom_call" | custom-call | flops 402653184 | bytes 4194304 | tf_op jit(solution)/shard_map/shrink/pallas_call | solution.py:274
  14.8 0.4 %collective-permute-start.5 = (bf16[128,128]{1,0:T(8,128)(2,1)S(1)}, bf16[128,128]{1,0:T(8,128)(2,1)S(1)}, u32[]{:S(2)}, u32[]{:S(2)}) collective-permute-start(bf16[128,128]{1,0:T(8,128)(2,1)S(1)} %get-tuple-element.42), channel_id=1, source_target_pairs={{0,1},{1,5},{2,9},{3,13},{4,0},{5,4},{6,8},{7,12},{8,3},{9,7},{10,... | collective-permute-start | bytes 98312 | tf_op jit(solution)/shard_map/ppermute | solution.py:348
  15.3 3.1 %collective-permute-start.6 = (bf16[128,128]{1,0:T(8,128)(2,1)S(1)}, bf16[128,128]{1,0:T(8,128)(2,1)S(1)}, u32[]{:S(2)}, u32[]{:S(2)}) collective-permute-start(bf16[128,128]{1,0:T(8,128)(2,1)S(1)} %get-tuple-element.42), channel_id=1, source_target_pairs={{0,3},{1,7},{2,11},{3,15},{4,2},{5,6},{6,10},{7,14},{8,1},{9,5},{1... | collective-permute-start | bytes 98312 | tf_op jit(solution)/shard_map/ppermute | solution.py:348
  18.3 0.3 copy.17
  18.6 0.7 %base.1 = (f32[128,512]{1,0:T(8,128)S(1)}, bf16[768,128]{1,0:T(8,128)(2,1)S(1)}, bf16[768,128]{1,0:T(8,128)(2,1)S(1)}, f32[8,128]{1,0:T(8,128)S(1)}) custom-call(bf16[528,128]{1,0:T(8,128)(2,1)S(1)} %get-tuple-element.32.refs_0_, bf16[528,128]{1,0:T(8,128)(2,1)S(1)} %collective-permute-done.refs_1_, bf16[272,128]{1,0:T(8,128)(2,1)S(1)} %collective-permute-done.2.refs_2_, ...), custom_call_target="tpu_custom_call" | custom-call | flops 268435456 | bytes 3145728 | tf_op jit(solution)/shard_map/base/pallas_call | solution.py:274
  19.3 2.7 %collective-permute-done.6 = bf16[128,128]{1,0:T(8,128)(2,1)S(1)} collective-permute-done((bf16[128,128]{1,0:T(8,128)(2,1)S(1)}, bf16[128,128]{1,0:T(8,128)(2,1)S(1)}, u32[]{:S(2)}, u32[]{:S(2)}) %collective-permute-start.6) | collective-permute-done | bytes 32800 | tf_op jit(solution)/shard_map/ppermute | solution.py:348
  22.1 1.2 %collective-permute-done.7.refs_1_ = f32[128,128]{1,0:T(8,128)S(1)} collective-permute-done((f32[128,128]{1,0:T(8,128)S(1)}, f32[128,128]{1,0:T(8,128)S(1)}, u32[]{:S(2)}, u32[]{:S(2)}) %collective-permute-start.7) | collective-permute-done | bytes 65568 | tf_op jit(solution)/shard_map/ppermute | solution.py:271
  23.4 0.6 %expand.1 = (f32[32,512]{1,0:T(8,128)S(1)}, bf16[32,512]{1,0:T(8,128)(2,1)S(1)}, bf16[32,512]{1,0:T(8,128)(2,1)S(1)}, bf16[32,512]{1,0:T(8,128)(2,1)S(1)}, f32[8,128]{1,0:T(8,128)S(1)}) custom-call(f32[128,128]{1,0:T(8,128)S(1)} %add_add_fusion.refs_0_, f32[128,128]{1,0:T(8,128)S(1)} %collective-permute-done.7.refs_1_, ...), custom_call_target="tpu_custom_call" | custom-call | flops 50331648 | bytes 1048576 | tf_op jit(solution)/shard_map/expand/pallas_call | solution.py:274
  24.0 1.9 %collective-permute-start.10 = (bf16[32,512]{1,0:T(8,128)(2,1)S(1)}, bf16[32,512]{1,0:T(8,128)(2,1)S(1)}, u32[]{:S(2)}, u32[]{:S(2)}) collective-permute-start(bf16[32,512]{1,0:T(8,128)(2,1)S(1)} %get-tuple-element.54), channel_id=1, source_target_pairs={{0,12},{4,8},{8,4},{12,0},{1,13},{5,9},{9,5},{13,1},{2,14},{6,10},... | collective-permute-start | bytes 98312 | tf_op jit(solution)/shard_map/ppermute | solution.py:268
  25.9 2.6 %collective-permute-start.9 = (bf16[32,512]{1,0:T(8,128)(2,1)S(1)}, bf16[32,512]{1,0:T(8,128)(2,1)S(1)}, u32[]{:S(2)}, u32[]{:S(2)}) collective-permute-start(bf16[32,512]{1,0:T(8,128)(2,1)S(1)} %get-tuple-element.53), channel_id=1, source_target_pairs={{0,4},{4,0},{8,12},{12,8},{1,5},{5,1},{9,13},{13,9},{2,6},{6,2},{1... | collective-permute-start | bytes 98312 | tf_op jit(solution)/shard_map/ppermute | solution.py:268
  28.4 1.2 %cached.1 = (f32[512,128]{1,0:T(8,128)S(1)}, f32[512,128]{1,0:T(8,128)S(1)}, f32[512,128]{1,0:T(8,128)S(1)}, f32[512,64]{1,0:T(8,128)S(1)}) custom-call(s32[16,256]{1,0:T(8,128)S(1)} %get-tuple-element.55.spans, bf16[16,2,16,128]{3,2,1,0:T(8,128)(2,1)S(1)} %copy-done.1, bf16[16,2,256,256]{3,2,1,0:T(8,128)(2,1)S(1)} %bitcast.8, f32[8,128]{1,0:T(8,128)S(1)} %get-tuple-element.57._), custom_call_target="tpu_custom_call" | custom-call | flops 134217728 | bytes 4194304 | tf_op jit(solution)/shard_map/cached/pallas_call | solution.py:274
  29.7 0.1 collective-permute-done.10.refs_2_
  29.8 1.0 %collective-permute-done.8.refs_0_ = bf16[32,512]{1,0:T(8,128)(2,1)S(1)} collective-permute-done((bf16[32,512]{1,0:T(8,128)(2,1)S(1)}, bf16[32,512]{1,0:T(8,128)(2,1)S(1)}, u32[]{:S(2)}, u32[]{:S(2)}) %collective-permute-start.8) | collective-permute-done | bytes 32800 | tf_op jit(solution)/shard_map/ppermute | solution.py:268
  30.8 1.2 %finish.1 = (bf16[16,2,2048]{2,1,0:T(2,128)(2,1)}, bf16[16,2,2,256]{3,2,1,0:T(2,128)(2,1)}) custom-call(f32[32,512]{1,0:T(8,128)S(1)} %get-tuple-element.51.own, bf16[32,512]{1,0:T(8,128)(2,1)S(1)} %collective-permute-done.8.refs_0_, bf16[32,512]{1,0:T(8,128)(2,1)S(1)} %collective-permute-done.9.refs_1_, ...), custom_call_target="tpu_custom_call" | custom-call | flops 33554432 | bytes 1048576 | tf_op jit(solution)/shard_map/finish/pallas_call | solution.py:274
  (18 shorter events, 0.1 us)
Async XLA Ops:
  1.8 8.8 %collective-permute-start.2 = (bf16[272,128]{1,0:T(8,128)(2,1)S(1)}, bf16[272,128]{1,0:T(8,128)(2,1)S(1)}, u32[]{:S(2)}, u32[]{:S(2)}) collective-permute-start(bf16[272,128]{1,0:T(8,128)(2,1)S(1)} %get-tuple-element.35), channel_id=1, source_target_pairs={{0,8},{4,12},{8,0},{12,4},{1,9},{5,13},{9,1},{13,5},{2,10},{6,14},... | collective-permute-start | bytes 208904 | tf_op jit(solution)/shard_map/ppermute | solution.py:268
  5.9 6.9 %collective-permute-start.1 = (bf16[272,128]{1,0:T(8,128)(2,1)S(1)}, bf16[272,128]{1,0:T(8,128)(2,1)S(1)}, u32[]{:S(2)}, u32[]{:S(2)}) collective-permute-start(bf16[272,128]{1,0:T(8,128)(2,1)S(1)} %get-tuple-element.34), channel_id=1, source_target_pairs={{0,12},{4,8},{8,4},{12,0},{1,13},{5,9},{9,5},{13,1},{2,14},{6,10},... | collective-permute-start | bytes 208904 | tf_op jit(solution)/shard_map/ppermute | solution.py:268
  7.2 6.4 %collective-permute-start = (bf16[528,128]{1,0:T(8,128)(2,1)S(1)}, bf16[528,128]{1,0:T(8,128)(2,1)S(1)}, u32[]{:S(2)}, u32[]{:S(2)}) collective-permute-start(bf16[528,128]{1,0:T(8,128)(2,1)S(1)} %get-tuple-element.33), channel_id=1, source_target_pairs={{0,4},{4,0},{8,12},{12,8},{1,5},{5,1},{9,13},{13,9},{2,6},{6,2},{1... | collective-permute-start | bytes 405512 | tf_op jit(solution)/shard_map/ppermute | solution.py:268
  7.4 6.7 %copy-start = (bf16[6,2048,128]{2,1,0:T(8,128)(2,1)S(1)}, bf16[6,2048,128]{2,1,0:T(8,128)(2,1)}, u32[]{:S(2)}) copy-start(bf16[6,2048,128]{2,1,0:T(8,128)(2,1)} %refs_6_.1) | copy-start | bytes 9437188
  10.5 7.8 %copy-start.4 = (bf16[2048,2,256]{2,1,0:T(2,128)(2,1)S(1)}, bf16[2048,2,256]{2,1,0:T(2,128)(2,1)}, u32[]{:S(2)}) copy-start(bf16[2048,2,256]{2,1,0:T(2,128)(2,1)} %param.13) | copy-start | bytes 6291460
  10.6 8.0 %copy-start.2 = (bf16[6,64,2,128]{3,2,1,0:T(2,128)(2,1)S(1)}, bf16[6,64,2,128]{3,2,1,0:T(2,128)(2,1)}, u32[]{:S(2)}) copy-start(bf16[6,64,2,128]{3,2,1,0:T(2,128)(2,1)} %refs_7_.1) | copy-start | bytes 589828
  10.6 8.0 %copy-start.3 = (bf16[6,64,2,128]{3,2,1,0:T(2,128)(2,1)S(1)}, bf16[6,64,2,128]{3,2,1,0:T(2,128)(2,1)}, u32[]{:S(2)}) copy-start(bf16[6,64,2,128]{3,2,1,0:T(2,128)(2,1)} %refs_8_.1) | copy-start | bytes 589828
  12.7 1.3 %collective-permute-start.4 = (bf16[272,128]{1,0:T(8,128)(2,1)S(1)}, bf16[272,128]{1,0:T(8,128)(2,1)S(1)}, u32[]{:S(2)}, u32[]{:S(2)}) collective-permute-start(bf16[272,128]{1,0:T(8,128)(2,1)S(1)} %collective-permute-done.1.refs_3_), channel_id=1, source_target_pairs={{0,1},{1,0},{2,3},{3,2},{4,5},{5,4},{6,7},{7,6},{8,9},{9,8},{10,11... | collective-permute-start | bytes 208904 | tf_op jit(solution)/shard_map/ppermute | solution.py:271
  12.7 1.4 %collective-permute-start.3 = (bf16[272,128]{1,0:T(8,128)(2,1)S(1)}, bf16[272,128]{1,0:T(8,128)(2,1)S(1)}, u32[]{:S(2)}, u32[]{:S(2)}) collective-permute-start(bf16[272,128]{1,0:T(8,128)(2,1)S(1)} %collective-permute-done.2.refs_2_), channel_id=1, source_target_pairs={{0,1},{1,0},{2,3},{3,2},{4,5},{5,4},{6,7},{7,6},{8,9},{9,8},{10,11... | collective-permute-start | bytes 208904 | tf_op jit(solution)/shard_map/ppermute | solution.py:271
  14.8 4.5 %collective-permute-start.5 = (bf16[128,128]{1,0:T(8,128)(2,1)S(1)}, bf16[128,128]{1,0:T(8,128)(2,1)S(1)}, u32[]{:S(2)}, u32[]{:S(2)}) collective-permute-start(bf16[128,128]{1,0:T(8,128)(2,1)S(1)} %get-tuple-element.42), channel_id=1, source_target_pairs={{0,1},{1,5},{2,9},{3,13},{4,0},{5,4},{6,8},{7,12},{8,3},{9,7},{10,... | collective-permute-start | bytes 98312 | tf_op jit(solution)/shard_map/ppermute | solution.py:348
  15.3 6.8 %collective-permute-start.6 = (bf16[128,128]{1,0:T(8,128)(2,1)S(1)}, bf16[128,128]{1,0:T(8,128)(2,1)S(1)}, u32[]{:S(2)}, u32[]{:S(2)}) collective-permute-start(bf16[128,128]{1,0:T(8,128)(2,1)S(1)} %get-tuple-element.42), channel_id=1, source_target_pairs={{0,3},{1,7},{2,11},{3,15},{4,2},{5,6},{6,10},{7,14},{8,1},{9,5},{1... | collective-permute-start | bytes 98312 | tf_op jit(solution)/shard_map/ppermute | solution.py:348
  18.3 10.1 %copy-start.1 = (bf16[16,2,16,128]{3,2,1,0:T(8,128)(2,1)S(1)}, bf16[16,2,16,128]{3,2,1,0:T(8,128)(2,1)}, u32[]{:S(2)}) copy-start(bf16[16,2,16,128]{3,2,1,0:T(8,128)(2,1)} %refs_3_.1) | copy-start | bytes 393220
  22.1 1.3 %collective-permute-start.7 = (f32[128,128]{1,0:T(8,128)S(1)}, f32[128,128]{1,0:T(8,128)S(1)}, u32[]{:S(2)}, u32[]{:S(2)}) collective-permute-start(f32[128,128]{1,0:T(8,128)S(1)} %add_add_fusion.refs_0_), channel_id=1, source_target_pairs={{0,1},{1,0},{2,3},{3,2},{4,5},{5,4},{6,7},{7,6},{8,9},{9,8},{10,11... | collective-permute-start | bytes 196616 | tf_op jit(solution)/shard_map/ppermute | solution.py:271
  24.0 5.8 %collective-permute-start.10 = (bf16[32,512]{1,0:T(8,128)(2,1)S(1)}, bf16[32,512]{1,0:T(8,128)(2,1)S(1)}, u32[]{:S(2)}, u32[]{:S(2)}) collective-permute-start(bf16[32,512]{1,0:T(8,128)(2,1)S(1)} %get-tuple-element.54), channel_id=1, source_target_pairs={{0,12},{4,8},{8,4},{12,0},{1,13},{5,9},{9,5},{13,1},{2,14},{6,10},... | collective-permute-start | bytes 98312 | tf_op jit(solution)/shard_map/ppermute | solution.py:268
  25.9 5.0 %collective-permute-start.8 = (bf16[32,512]{1,0:T(8,128)(2,1)S(1)}, bf16[32,512]{1,0:T(8,128)(2,1)S(1)}, u32[]{:S(2)}, u32[]{:S(2)}) collective-permute-start(bf16[32,512]{1,0:T(8,128)(2,1)S(1)} %get-tuple-element.52), channel_id=1, source_target_pairs={{0,8},{4,12},{8,0},{12,4},{1,9},{5,13},{9,1},{13,5},{2,10},{6,14},... | collective-permute-start | bytes 98312 | tf_op jit(solution)/shard_map/ppermute | solution.py:268
  25.9 5.0 %collective-permute-start.9 = (bf16[32,512]{1,0:T(8,128)(2,1)S(1)}, bf16[32,512]{1,0:T(8,128)(2,1)S(1)}, u32[]{:S(2)}, u32[]{:S(2)}) collective-permute-start(bf16[32,512]{1,0:T(8,128)(2,1)S(1)} %get-tuple-element.53), channel_id=1, source_target_pairs={{0,4},{4,0},{8,12},{12,8},{1,5},{5,1},{9,13},{13,9},{2,6},{6,2},{1... | collective-permute-start | bytes 98312 | tf_op jit(solution)/shard_map/ppermute | solution.py:268

commit v5 on v4

--- a/solution.py
+++ b/solution.py
@@ -124,14 +124,23 @@
 
 
 def base_kernel(pool, parts, count, half, *refs):
-    weight, up_key, up_value, _, base, key_table, value_table, token = refs[-8:]
+    weight, up_key, up_value, _, base, table, token = refs[-7:]
     token[...] = jnp.zeros_like(token)
-    sides = both_sides(pool, parts, count, half, refs[:-8])
+    sides = both_sides(pool, parts, count, half, refs[:-7])
     holders, rank, kv_local, size = up_key.shape
+    row = lax.broadcasted_iota(jnp.int32, (kv_local * rank, rank * kv_local), 0)
+    col = lax.broadcasted_iota(jnp.int32, (kv_local * rank, rank * kv_local), 1)
+    pick = (row // rank == col % kv_local) & (row % rank == col // kv_local)
+    pick = pick.astype(F32).astype(BF16)
+    nothing = jnp.zeros((rank, size), BF16)
     for a in range(holders):
-        at = slice(a * rank * kv_local, (a + 1) * rank * kv_local)
-        key_table[at, :] = up_key[a].reshape(rank * kv_local, size)
-        value_table[at, :] = up_value[a].reshape(rank * kv_local, size)
+        for which, up in enumerate((up_key, up_value)):
+            heads = dot(pick, up[a].reshape(rank * kv_local, size)).astype(BF16)
+            at = slice((2 * a + which) * rank, (2 * a + which + 1) * rank)
+            for k in range(kv_local):
+                for i in range(2):
+                    value = heads[k * rank:(k + 1) * rank] if i == which else nothing
+                    table[at, (2 * k + i) * size:(2 * k + i + 1) * size] = value
     for k in range(weight.shape[0]):
         out = 0.0
         for at, x in sides:
@@ -139,42 +148,26 @@
         base[:, k * weight.shape[2]:(k + 1) * weight.shape[2]] = out
 
 
-def expand_kernel(pool, parts, rank, kv_local, *refs):
-    sums, refs = refs[:parts], refs[parts:]
-    slots_in, base = refs[:2]
-    tables, (outs, token, scratch) = refs[2:4], (refs[4:4 + pool], refs[4 + pool], refs[5 + pool])
+def expand_kernel(pool, parts, *refs):
+    sums, (slots_in, base, table), refs = refs[:parts], refs[parts:parts + 3], refs[parts + 3:]
+    outs, token, scratch = refs[:pool], refs[pool], refs[pool + 1]
     token[...] = jnp.zeros_like(token)
-    count = base.shape[0] // pool
-    deep, size = rank * kv_local, tables[0].shape[1]
-    holders = tables[0].shape[0] // deep
+    count, wide = base.shape[0] // pool, slots_in.shape[1]
+    holders = table.shape[0] // wide
     me = lax.axis_index("pool")
-    first_slot = me * holders
     total = sums[0][...]
     for s in sums[1:]:
         total = total + s[...]
     scratch[...] = total
     ordered = jnp.concatenate(
         [scratch[pl.ds(pl.multiple_of((me ^ k) * count, count), count), :] for k in range(pool)], axis=0
-    ).astype(BF16)
-    slots = jnp.concatenate([slots_in[:, :deep]] * kv_local, axis=0)
-    row = lax.broadcasted_iota(jnp.int32, (2 * rank, deep), 0)
-    col = lax.broadcasted_iota(jnp.int32, (2 * rank, deep), 1)
-    for which, table in enumerate(tables):
-        wide = []
-        for k in range(kv_local):
-            pick = (row == which * rank + col // kv_local) & (col % kv_local == k)
-            wide.append(dot(ordered, pick.astype(F32).astype(BF16)))
-        wide = jnp.concatenate(wide, axis=0)
-        spread = [
-            jnp.where(slots == (first_slot + a).astype(F32), wide, 0.0).astype(BF16) for a in range(holders)
-        ]
-        delta = dot(jnp.concatenate(spread, axis=1), table[...])
-        for k in range(kv_local):
-            at = slice((2 * k + which) * size, (2 * k + which + 1) * size)
-            value = base[:, at] + ADAPTER_SCALE * delta[k * base.shape[0]:(k + 1) * base.shape[0]]
-            outs[0][:, at] = value[:count]
-            for j in range(1, pool):
-                outs[j][:, at] = value[j * count:(j + 1) * count].astype(BF16)
+    )
+    slots = slots_in[...] - (me * holders).astype(F32)
+    spread = [jnp.where(slots == float(a), ordered, 0.0).astype(BF16) for a in range(holders)]
+    value = base[...] + ADAPTER_SCALE * dot(jnp.concatenate(spread, axis=1), table[...])
+    outs[0][...] = value[:count]
+    for j in range(1, pool):
+        outs[j][...] = value[j * count:(j + 1) * count].astype(BF16)
 
 
 def cache_kernel(spans, queries, cache, _, acc_out, top_out, total_out, bias_out, scores_all, weights_all):
@@ -324,14 +317,17 @@
         moved=4 << 20,
     )
     weight, marked = lax.optimization_barrier((key_value_weight, token))
-    _, rank, _, size = adapter_up_key.shape
-    table = struct((up_here * rank * kv_local, size), BF16)
-    base, key_table, value_table, token = call(
+    rank = adapter_up_key.shape[1]
+    base, table, token = call(
         "base",
         functools.partial(base_kernel, pool, parts, count, half),
         (*operands, jnp.transpose(weight, (1, 0, 2)), adapter_up_key, adapter_up_value, marked),
         chunks_in + [VMEM] * 3 + [ANY],
-        [struct((all_rows, kv_local * pair), F32), table, table, TOKEN],
+        [
+            struct((all_rows, kv_local * pair), F32),
+            struct((up_here * 2 * rank, kv_local * pair), BF16),
+            TOKEN,
+        ],
         work=2 * all_rows * part * kv_local * pair,
         moved=3 << 20,
     )
@@ -351,9 +347,9 @@
     sums = [mine] + ([over_pair(mine)] if parts == 2 else [])
     expanded = call(
         "expand",
-        functools.partial(expand_kernel, pool, parts, rank, kv_local),
-        (*sums, slots, base, key_table, value_table),
-        [VMEM] * (parts + 4),
+        functools.partial(expand_kernel, pool, parts),
+        (*sums, slots, base, table),
+        [VMEM] * (parts + 3),
         [struct((count, kv_local * pair), F32)] + [struct((count, kv_local * pair), BF16)] * (pool - 1) + [TOKEN],
         [pltpu.VMEM((all_rows, LANES), F32)],
         work=4 * all_rows * LANES * up_here * LANES,

time: 32.3 us -> 31.9 us (0.988)
  no operation moved by 1% of the time
where the time goes in v5:
time: 31.9 us; the launch traced here: 31.7 us
  starting transfers between devices  14.2 us (45%)
  waiting for transfers between devices  8.09 us (25%)
  Pallas kernels  5.28 us (17%)
  local copies, waits for them, and re-layouts  3.41 us (11%)
  between operations  0.77 us (2%)
    ppermute x6, starting transfers between devices, over_pool(): return lax.ppermute(x, 'pool', [(i, i ^ k) for i in range(pool)])  10.1 us
    pallas_call x6, Pallas kernels, call(): pl.pallas_call(kernel, out_shape=outs, in_specs=in_specs, out_specs=[VMEM...  5.28 us
    ppermute x6, waiting for transfers between devices, over_pool(): return lax.ppermute(x, 'pool', [(i, i ^ k) for i in range(pool)])  3.68 us
    ppermute x2, starting transfers between devices, body(): moved = lax.ppermute(shrink, ('pool', 'tensor'), pairs).astype(F32)  3.47 us
    optimization_barrier x1, local copies, waits for them, and re-layouts, body(): stored, _ = lax.optimization_barrier((cache, packed[0]))  3.1 us
    ppermute x2, waiting for transfers between devices, body(): moved = lax.ppermute(shrink, ('pool', 'tensor'), pairs).astype(F32)  2.64 us
    ppermute x3, waiting for transfers between devices, over_pair(): return lax.ppermute(x, 'tensor', [(i, i ^ 1) for i in range(tensor)])  1.77 us
  transfers between devices with their start and end apart: 11, of which 8 were waited for; matrix products, arithmetic and copies ran while one was open for 11% of the time, Pallas kernels for 6%

profile of v5, /device:TPU:0, one launch (start us, length us, event | category | flops | bytes accessed | tf_op | source)
XLA Modules:
  0.0 31.7 jit_solution(183995177962950740)
XLA Ops:
  0.6 1.1 %pack.1 = (bf16[528,128]{1,0:T(8,128)(2,1)S(1)}, bf16[528,128]{1,0:T(8,128)(2,1)S(1)}, bf16[272,128]{1,0:T(8,128)(2,1)S(1)}, bf16[272,128]{1,0:T(8,128)(2,1)S(1)}, s32[16,256]{1,0:T(8,128)S(1)}) custom-call(s32[16]{0:T(128)} %request_adapter.1, s32[24]{0:T(128)} %adapter_storage.1, s32[16]{0:T(128)} %lengths.1, bf16[16,2,8192]{2,1,0:T(2,128)(2,1)} %hidden.1), custom_call_target="tpu_custom_call" | custom-call | bytes 1048576 | tf_op jit(solution)/shard_map/pack/pallas_call | solution.py:267
  1.8 4.1 %collective-permute-start.2 = (bf16[272,128]{1,0:T(8,128)(2,1)S(1)}, bf16[272,128]{1,0:T(8,128)(2,1)S(1)}, u32[]{:S(2)}, u32[]{:S(2)}) collective-permute-start(bf16[272,128]{1,0:T(8,128)(2,1)S(1)} %get-tuple-element.34), channel_id=1, source_target_pairs={{0,8},{4,12},{8,0},{12,4},{1,9},{5,13},{9,1},{13,5},{2,10},{6,14},... | collective-permute-start | bytes 208904 | tf_op jit(solution)/shard_map/ppermute | solution.py:261
  5.9 1.3 %collective-permute-start.1 = (bf16[272,128]{1,0:T(8,128)(2,1)S(1)}, bf16[272,128]{1,0:T(8,128)(2,1)S(1)}, u32[]{:S(2)}, u32[]{:S(2)}) collective-permute-start(bf16[272,128]{1,0:T(8,128)(2,1)S(1)} %get-tuple-element.33), channel_id=1, source_target_pairs={{0,12},{4,8},{8,4},{12,0},{1,13},{5,9},{9,5},{13,1},{2,14},{6,10},... | collective-permute-start | bytes 208904 | tf_op jit(solution)/shard_map/ppermute | solution.py:261
  7.2 0.2 collective-permute-start
  7.4 3.1 %copy.16 = bf16[16,256,2,256]{3,1,2,0:T(8,128)(2,1)S(1)} copy(bf16[16,256,2,256]{3,2,1,0:T(2,128)(2,1)} %param.12) | data formatting | bytes 8388608 | tf_op jit(solution)/shard_map/optimization_barrier | solution.py:299
  10.6 2.1 %collective-permute-done.1.refs_3_ = bf16[272,128]{1,0:T(8,128)(2,1)S(1)} collective-permute-done((bf16[272,128]{1,0:T(8,128)(2,1)S(1)}, bf16[272,128]{1,0:T(8,128)(2,1)S(1)}, u32[]{:S(2)}, u32[]{:S(2)}) %collective-permute-start.1) | collective-permute-done | bytes 69664 | tf_op jit(solution)/shard_map/ppermute | solution.py:261
  12.7 0.5 %collective-permute-start.3 = (bf16[272,128]{1,0:T(8,128)(2,1)S(1)}, bf16[272,128]{1,0:T(8,128)(2,1)S(1)}, u32[]{:S(2)}, u32[]{:S(2)}) collective-permute-start(bf16[272,128]{1,0:T(8,128)(2,1)S(1)} %collective-permute-done.2.refs_2_), channel_id=1, source_target_pairs={{0,1},{1,0},{2,3},{3,2},{4,5},{5,4},{6,7},{7,6},{8,9},{9,8},{10,11... | collective-permute-start | bytes 208904 | tf_op jit(solution)/shard_map/ppermute | solution.py:264
  13.3 0.4 %collective-permute-done.refs_1_ = bf16[528,128]{1,0:T(8,128)(2,1)S(1)} collective-permute-done((bf16[528,128]{1,0:T(8,128)(2,1)S(1)}, bf16[528,128]{1,0:T(8,128)(2,1)S(1)}, u32[]{:S(2)}, u32[]{:S(2)}) %collective-permute-start) | collective-permute-done | bytes 135200 | tf_op jit(solution)/shard_map/ppermute | solution.py:261
  13.6 0.4 %collective-permute-done.4.refs_5_ = bf16[272,128]{1,0:T(8,128)(2,1)S(1)} collective-permute-done((bf16[272,128]{1,0:T(8,128)(2,1)S(1)}, bf16[272,128]{1,0:T(8,128)(2,1)S(1)}, u32[]{:S(2)}, u32[]{:S(2)}) %collective-permute-start.4) | collective-permute-done | bytes 69664 | tf_op jit(solution)/shard_map/ppermute | solution.py:264
  14.0 0.2 collective-permute-done.3.refs_4_
  14.2 0.7 %shrink.1 = (bf16[128,128]{1,0:T(8,128)(2,1)S(1)}, f32[128,128]{1,0:T(8,128)S(1)}, f32[8,128]{1,0:T(8,128)S(1)}) custom-call(bf16[528,128]{1,0:T(8,128)(2,1)S(1)} %get-tuple-element.31.refs_0_, bf16[528,128]{1,0:T(8,128)(2,1)S(1)} %collective-permute-done.refs_1_, bf16[272,128]{1,0:T(8,128)(2,1)S(1)} %collective-permute-done.2.refs_2_, ...), custom_call_target="tpu_custom_call" | custom-call | flops 402653184 | bytes 4194304 | tf_op jit(solution)/shard_map/shrink/pallas_call | solution.py:267
  14.8 0.4 %collective-permute-start.5 = (bf16[128,128]{1,0:T(8,128)(2,1)S(1)}, bf16[128,128]{1,0:T(8,128)(2,1)S(1)}, u32[]{:S(2)}, u32[]{:S(2)}) collective-permute-start(bf16[128,128]{1,0:T(8,128)(2,1)S(1)} %get-tuple-element.41), channel_id=1, source_target_pairs={{0,1},{1,5},{2,9},{3,13},{4,0},{5,4},{6,8},{7,12},{8,3},{9,7},{10,... | collective-permute-start | bytes 98312 | tf_op jit(solution)/shard_map/ppermute | solution.py:344
  15.3 3.1 %collective-permute-start.6 = (bf16[128,128]{1,0:T(8,128)(2,1)S(1)}, bf16[128,128]{1,0:T(8,128)(2,1)S(1)}, u32[]{:S(2)}, u32[]{:S(2)}) collective-permute-start(bf16[128,128]{1,0:T(8,128)(2,1)S(1)} %get-tuple-element.41), channel_id=1, source_target_pairs={{0,3},{1,7},{2,11},{3,15},{4,2},{5,6},{6,10},{7,14},{8,1},{9,5},{1... | collective-permute-start | bytes 98312 | tf_op jit(solution)/shard_map/ppermute | solution.py:344
  18.3 0.3 copy.17
  18.6 0.7 %base.1 = (f32[128,512]{1,0:T(8,128)S(1)}, bf16[768,512]{1,0:T(8,128)(2,1)S(1)}, f32[8,128]{1,0:T(8,128)S(1)}) custom-call(bf16[528,128]{1,0:T(8,128)(2,1)S(1)} %get-tuple-element.31.refs_0_, bf16[528,128]{1,0:T(8,128)(2,1)S(1)} %collective-permute-done.refs_1_, bf16[272,128]{1,0:T(8,128)(2,1)S(1)} %collective-permute-done.2.refs_2_, ...), custom_call_target="tpu_custom_call" | custom-call | flops 268435456 | bytes 3145728 | tf_op jit(solution)/shard_map/base/pallas_call | solution.py:267
  19.4 2.6 %collective-permute-done.6 = bf16[128,128]{1,0:T(8,128)(2,1)S(1)} collective-permute-done((bf16[128,128]{1,0:T(8,128)(2,1)S(1)}, bf16[128,128]{1,0:T(8,128)(2,1)S(1)}, u32[]{:S(2)}, u32[]{:S(2)}) %collective-permute-start.6) | collective-permute-done | bytes 32800 | tf_op jit(solution)/shard_map/ppermute | solution.py:344
  22.1 1.2 %collective-permute-done.7.refs_1_ = f32[128,128]{1,0:T(8,128)S(1)} collective-permute-done((f32[128,128]{1,0:T(8,128)S(1)}, f32[128,128]{1,0:T(8,128)S(1)}, u32[]{:S(2)}, u32[]{:S(2)}) %collective-permute-start.7) | collective-permute-done | bytes 65568 | tf_op jit(solution)/shard_map/ppermute | solution.py:264
  23.4 0.3 expand.1
  23.7 1.9 %collective-permute-start.10 = (bf16[32,512]{1,0:T(8,128)(2,1)S(1)}, bf16[32,512]{1,0:T(8,128)(2,1)S(1)}, u32[]{:S(2)}, u32[]{:S(2)}) collective-permute-start(bf16[32,512]{1,0:T(8,128)(2,1)S(1)} %get-tuple-element.52), channel_id=1, source_target_pairs={{0,12},{4,8},{8,4},{12,0},{1,13},{5,9},{9,5},{13,1},{2,14},{6,10},... | collective-permute-start | bytes 98312 | tf_op jit(solution)/shard_map/ppermute | solution.py:261
  25.5 2.6 %collective-permute-start.9 = (bf16[32,512]{1,0:T(8,128)(2,1)S(1)}, bf16[32,512]{1,0:T(8,128)(2,1)S(1)}, u32[]{:S(2)}, u32[]{:S(2)}) collective-permute-start(bf16[32,512]{1,0:T(8,128)(2,1)S(1)} %get-tuple-element.51), channel_id=1, source_target_pairs={{0,4},{4,0},{8,12},{12,8},{1,5},{5,1},{9,13},{13,9},{2,6},{6,2},{1... | collective-permute-start | bytes 98312 | tf_op jit(solution)/shard_map/ppermute | solution.py:261
  28.1 1.2 %cached.1 = (f32[512,128]{1,0:T(8,128)S(1)}, f32[512,128]{1,0:T(8,128)S(1)}, f32[512,128]{1,0:T(8,128)S(1)}, f32[512,64]{1,0:T(8,128)S(1)}) custom-call(s32[16,256]{1,0:T(8,128)S(1)} %get-tuple-element.53.spans, bf16[16,2,16,128]{3,2,1,0:T(8,128)(2,1)S(1)} %copy-done.1, bf16[16,2,256,256]{3,2,1,0:T(8,128)(2,1)S(1)} %bitcast.8, f32[8,128]{1,0:T(8,128)S(1)} %get-tuple-element.55._), custom_call_target="tpu_custom_call" | custom-call | flops 134217728 | bytes 4194304 | tf_op jit(solution)/shard_map/cached/pallas_call | solution.py:267
  29.3 0.1 collective-permute-done.10.refs_2_
  29.5 1.0 %collective-permute-done.8.refs_0_ = bf16[32,512]{1,0:T(8,128)(2,1)S(1)} collective-permute-done((bf16[32,512]{1,0:T(8,128)(2,1)S(1)}, bf16[32,512]{1,0:T(8,128)(2,1)S(1)}, u32[]{:S(2)}, u32[]{:S(2)}) %collective-permute-start.8) | collective-permute-done | bytes 32800 | tf_op jit(solution)/shard_map/ppermute | solution.py:261
  30.5 1.2 %finish.1 = (bf16[16,2,2048]{2,1,0:T(2,128)(2,1)}, bf16[16,2,2,256]{3,2,1,0:T(2,128)(2,1)}) custom-call(f32[32,512]{1,0:T(8,128)S(1)} %get-tuple-element.49.own, bf16[32,512]{1,0:T(8,128)(2,1)S(1)} %collective-permute-done.8.refs_0_, bf16[32,512]{1,0:T(8,128)(2,1)S(1)} %collective-permute-done.9.refs_1_, ...), custom_call_target="tpu_custom_call" | custom-call | flops 33554432 | bytes 1048576 | tf_op jit(solution)/shard_map/finish/pallas_call | solution.py:267
  (18 shorter events, 0.1 us)
Async XLA Ops:
  1.8 8.8 %collective-permute-start.2 = (bf16[272,128]{1,0:T(8,128)(2,1)S(1)}, bf16[272,128]{1,0:T(8,128)(2,1)S(1)}, u32[]{:S(2)}, u32[]{:S(2)}) collective-permute-start(bf16[272,128]{1,0:T(8,128)(2,1)S(1)} %get-tuple-element.34), channel_id=1, source_target_pairs={{0,8},{4,12},{8,0},{12,4},{1,9},{5,13},{9,1},{13,5},{2,10},{6,14},... | collective-permute-start | bytes 208904 | tf_op jit(solution)/shard_map/ppermute | solution.py:261
  5.9 6.9 %collective-permute-start.1 = (bf16[272,128]{1,0:T(8,128)(2,1)S(1)}, bf16[272,128]{1,0:T(8,128)(2,1)S(1)}, u32[]{:S(2)}, u32[]{:S(2)}) collective-permute-start(bf16[272,128]{1,0:T(8,128)(2,1)S(1)} %get-tuple-element.33), channel_id=1, source_target_pairs={{0,12},{4,8},{8,4},{12,0},{1,13},{5,9},{9,5},{13,1},{2,14},{6,10},... | collective-permute-start | bytes 208904 | tf_op jit(solution)/shard_map/ppermute | solution.py:261
  7.2 6.4 %collective-permute-start = (bf16[528,128]{1,0:T(8,128)(2,1)S(1)}, bf16[528,128]{1,0:T(8,128)(2,1)S(1)}, u32[]{:S(2)}, u32[]{:S(2)}) collective-permute-start(bf16[528,128]{1,0:T(8,128)(2,1)S(1)} %get-tuple-element.32), channel_id=1, source_target_pairs={{0,4},{4,0},{8,12},{12,8},{1,5},{5,1},{9,13},{13,9},{2,6},{6,2},{1... | collective-permute-start | bytes 405512 | tf_op jit(solution)/shard_map/ppermute | solution.py:261
  7.4 6.7 %copy-start = (bf16[6,2048,128]{2,1,0:T(8,128)(2,1)S(1)}, bf16[6,2048,128]{2,1,0:T(8,128)(2,1)}, u32[]{:S(2)}) copy-start(bf16[6,2048,128]{2,1,0:T(8,128)(2,1)} %refs_6_.1) | copy-start | bytes 9437188
  10.5 7.8 %copy-start.4 = (bf16[2048,2,256]{2,1,0:T(2,128)(2,1)S(1)}, bf16[2048,2,256]{2,1,0:T(2,128)(2,1)}, u32[]{:S(2)}) copy-start(bf16[2048,2,256]{2,1,0:T(2,128)(2,1)} %param.13) | copy-start | bytes 6291460
  10.6 8.0 %copy-start.2 = (bf16[6,64,2,128]{3,2,1,0:T(2,128)(2,1)S(1)}, bf16[6,64,2,128]{3,2,1,0:T(2,128)(2,1)}, u32[]{:S(2)}) copy-start(bf16[6,64,2,128]{3,2,1,0:T(2,128)(2,1)} %refs_7_.1) | copy-start | bytes 589828
  10.6 8.0 %copy-start.3 = (bf16[6,64,2,128]{3,2,1,0:T(2,128)(2,1)S(1)}, bf16[6,64,2,128]{3,2,1,0:T(2,128)(2,1)}, u32[]{:S(2)}) copy-start(bf16[6,64,2,128]{3,2,1,0:T(2,128)(2,1)} %refs_8_.1) | copy-start | bytes 589828
  12.7 1.3 %collective-permute-start.4 = (bf16[272,128]{1,0:T(8,128)(2,1)S(1)}, bf16[272,128]{1,0:T(8,128)(2,1)S(1)}, u32[]{:S(2)}, u32[]{:S(2)}) collective-permute-start(bf16[272,128]{1,0:T(8,128)(2,1)S(1)} %collective-permute-done.1.refs_3_), channel_id=1, source_target_pairs={{0,1},{1,0},{2,3},{3,2},{4,5},{5,4},{6,7},{7,6},{8,9},{9,8},{10,11... | collective-permute-start | bytes 208904 | tf_op jit(solution)/shard_map/ppermute | solution.py:264
  12.7 1.4 %collective-permute-start.3 = (bf16[272,128]{1,0:T(8,128)(2,1)S(1)}, bf16[272,128]{1,0:T(8,128)(2,1)S(1)}, u32[]{:S(2)}, u32[]{:S(2)}) collective-permute-start(bf16[272,128]{1,0:T(8,128)(2,1)S(1)} %collective-permute-done.2.refs_2_), channel_id=1, source_target_pairs={{0,1},{1,0},{2,3},{3,2},{4,5},{5,4},{6,7},{7,6},{8,9},{9,8},{10,11... | collective-permute-start | bytes 208904 | tf_op jit(solution)/shard_map/ppermute | solution.py:264
  14.8 4.5 %collective-permute-start.5 = (bf16[128,128]{1,0:T(8,128)(2,1)S(1)}, bf16[128,128]{1,0:T(8,128)(2,1)S(1)}, u32[]{:S(2)}, u32[]{:S(2)}) collective-permute-start(bf16[128,128]{1,0:T(8,128)(2,1)S(1)} %get-tuple-element.41), channel_id=1, source_target_pairs={{0,1},{1,5},{2,9},{3,13},{4,0},{5,4},{6,8},{7,12},{8,3},{9,7},{10,... | collective-permute-start | bytes 98312 | tf_op jit(solution)/shard_map/ppermute | solution.py:344
  15.3 6.8 %collective-permute-start.6 = (bf16[128,128]{1,0:T(8,128)(2,1)S(1)}, bf16[128,128]{1,0:T(8,128)(2,1)S(1)}, u32[]{:S(2)}, u32[]{:S(2)}) collective-permute-start(bf16[128,128]{1,0:T(8,128)(2,1)S(1)} %get-tuple-element.41), channel_id=1, source_target_pairs={{0,3},{1,7},{2,11},{3,15},{4,2},{5,6},{6,10},{7,14},{8,1},{9,5},{1... | collective-permute-start | bytes 98312 | tf_op jit(solution)/shard_map/ppermute | solution.py:344
  18.6 9.5 %copy-start.1 = (bf16[16,2,16,128]{3,2,1,0:T(8,128)(2,1)S(1)}, bf16[16,2,16,128]{3,2,1,0:T(8,128)(2,1)}, u32[]{:S(2)}) copy-start(bf16[16,2,16,128]{3,2,1,0:T(8,128)(2,1)} %refs_3_.1) | copy-start | bytes 393220
  22.1 1.3 %collective-permute-start.7 = (f32[128,128]{1,0:T(8,128)S(1)}, f32[128,128]{1,0:T(8,128)S(1)}, u32[]{:S(2)}, u32[]{:S(2)}) collective-permute-start(f32[128,128]{1,0:T(8,128)S(1)} %add_add_fusion.refs_0_), channel_id=1, source_target_pairs={{0,1},{1,0},{2,3},{3,2},{4,5},{5,4},{6,7},{7,6},{8,9},{9,8},{10,11... | collective-permute-start | bytes 196616 | tf_op jit(solution)/shard_map/ppermute | solution.py:264
  23.7 5.8 %collective-permute-start.10 = (bf16[32,512]{1,0:T(8,128)(2,1)S(1)}, bf16[32,512]{1,0:T(8,128)(2,1)S(1)}, u32[]{:S(2)}, u32[]{:S(2)}) collective-permute-start(bf16[32,512]{1,0:T(8,128)(2,1)S(1)} %get-tuple-element.52), channel_id=1, source_target_pairs={{0,12},{4,8},{8,4},{12,0},{1,13},{5,9},{9,5},{13,1},{2,14},{6,10},... | collective-permute-start | bytes 98312 | tf_op jit(solution)/shard_map/ppermute | solution.py:261
  25.5 5.0 %collective-permute-start.8 = (bf16[32,512]{1,0:T(8,128)(2,1)S(1)}, bf16[32,512]{1,0:T(8,128)(2,1)S(1)}, u32[]{:S(2)}, u32[]{:S(2)}) collective-permute-start(bf16[32,512]{1,0:T(8,128)(2,1)S(1)} %get-tuple-element.50), channel_id=1, source_target_pairs={{0,8},{4,12},{8,0},{12,4},{1,9},{5,13},{9,1},{13,5},{2,10},{6,14},... | collective-permute-start | bytes 98312 | tf_op jit(solution)/shard_map/ppermute | solution.py:261
  25.5 5.0 %collective-permute-start.9 = (bf16[32,512]{1,0:T(8,128)(2,1)S(1)}, bf16[32,512]{1,0:T(8,128)(2,1)S(1)}, u32[]{:S(2)}, u32[]{:S(2)}) collective-permute-start(bf16[32,512]{1,0:T(8,128)(2,1)S(1)} %get-tuple-element.51), channel_id=1, source_target_pairs={{0,4},{4,0},{8,12},{12,8},{1,5},{5,1},{9,13},{13,9},{2,6},{6,2},{1... | collective-permute-start | bytes 98312 | tf_op jit(solution)/shard_map/ppermute | solution.py:261

commit v6 on v5

--- a/solution.py
+++ b/solution.py
@@ -150,7 +150,7 @@
 
 def expand_kernel(pool, parts, *refs):
     sums, (slots_in, base, table), refs = refs[:parts], refs[parts:parts + 3], refs[parts + 3:]
-    outs, token, scratch = refs[:pool], refs[pool], refs[pool + 1]
+    outs, token, scratch, values = refs[:pool], *refs[pool:]
     token[...] = jnp.zeros_like(token)
     count, wide = base.shape[0] // pool, slots_in.shape[1]
     holders = table.shape[0] // wide
@@ -166,8 +166,10 @@
     spread = [jnp.where(slots == float(a), ordered, 0.0).astype(BF16) for a in range(holders)]
     value = base[...] + ADAPTER_SCALE * dot(jnp.concatenate(spread, axis=1), table[...])
     outs[0][...] = value[:count]
+    values[...] = value
     for j in range(1, pool):
-        outs[j][...] = value[j * count:(j + 1) * count].astype(BF16)
+        k = me ^ ((me + j) % pool)
+        outs[j][...] = values[pl.ds(pl.multiple_of(k * count, count), count), :].astype(BF16)
 
 
 def cache_kernel(spans, queries, cache, _, acc_out, top_out, total_out, bias_out, scores_all, weights_all):
@@ -351,12 +353,12 @@
         (*sums, slots, base, table),
         [VMEM] * (parts + 3),
         [struct((count, kv_local * pair), F32)] + [struct((count, kv_local * pair), BF16)] * (pool - 1) + [TOKEN],
-        [pltpu.VMEM((all_rows, LANES), F32)],
+        [pltpu.VMEM((all_rows, LANES), F32), pltpu.VMEM((all_rows, kv_local * pair), F32)],
         work=4 * all_rows * LANES * up_here * LANES,
     )
     received = [None] * pool
     for k in range(pool - 1, 0, -1):
-        received[k] = over_pool(expanded[k], k)
+        received[k] = lax.ppermute(expanded[k], "pool", [(i, (i + k) % pool) for i in range(pool)])
     acc, top, total, bias = call(
         "cached",
         cache_kernel,
@@ -370,7 +372,7 @@
     return tuple(call(
         "finish",
         functools.partial(finish_kernel, pool),
-        (expanded[0], *[received[k] for k in [2, 1, *range(3, pool)]], queries, acc, top, total, bias),
+        (expanded[0], *[received[k] for k in [*range(2, pool), 1]], queries, acc, top, total, bias),
         [VMEM] * (pool + 5),
         [struct((rows, steps_new, heads * size), BF16), struct((rows, steps_new, kv_local, pair), BF16)],
         [pltpu.VMEM((count * heads, size), F32)],

time: 31.9 us -> 31.4 us (0.984)
  waiting for transfers between devices: 8.09 us -> 7.46 us
    ppermute x0 -> x3, starting transfers between devices: none -> 4.58 us  [body(): lax.ppermute(expanded[k], 'pool', [(i, (i + k) % pool) for i in range(poo...]
    ppermute x6 -> x3, starting transfers between devices: 10.1 us -> 5.68 us  [over_pool(): return lax.ppermute(x, 'pool', [(i, i ^ k) for i in range(pool)])]
    ppermute x6 -> x3, waiting for transfers between devices: 3.68 us -> 2.53 us  [over_pool(): return lax.ppermute(x, 'pool', [(i, i ^ k) for i in range(pool)])]
    ppermute x0 -> x3, waiting for transfers between devices: none -> 0.53 us  [body(): lax.ppermute(expanded[k], 'pool', [(i, (i + k) % pool) for i in range(poo...]
where the time goes in v6:
time: 31.4 us; the launch traced here: 31.3 us
  starting transfers between devices  14.3 us (46%)
  waiting for transfers between devices  7.46 us (24%)
  Pallas kernels  5.29 us (17%)
  local copies, waits for them, and re-layouts  3.41 us (11%)
  between operations  0.78 us (2%)
    ppermute x3, starting transfers between devices, over_pool(): return lax.ppermute(x, 'pool', [(i, i ^ k) for i in range(pool)])  5.68 us
    pallas_call x6, Pallas kernels, call(): pl.pallas_call(kernel, out_shape=outs, in_specs=in_specs, out_specs=[VMEM...  5.29 us
    ppermute x3, starting transfers between devices, body(): lax.ppermute(expanded[k], 'pool', [(i, (i + k) % pool) for i in range(poo...  4.58 us
    ppermute x2, starting transfers between devices, body(): moved = lax.ppermute(shrink, ('pool', 'tensor'), pairs).astype(F32)  3.47 us
    optimization_barrier x1, local copies, waits for them, and re-layouts, body(): stored, _ = lax.optimization_barrier((cache, packed[0]))  3.1 us
    ppermute x2, waiting for transfers between devices, body(): moved = lax.ppermute(shrink, ('pool', 'tensor'), pairs).astype(F32)  2.64 us
    ppermute x3, waiting for transfers between devices, over_pool(): return lax.ppermute(x, 'pool', [(i, i ^ k) for i in range(pool)])  2.53 us
    ppermute x3, waiting for transfers between devices, over_pair(): return lax.ppermute(x, 'tensor', [(i, i ^ 1) for i in range(tensor)])  1.77 us
  transfers between devices with their start and end apart: 11, of which 8 were waited for; matrix products, arithmetic and copies ran while one was open for 11% of the time, Pallas kernels for 6%

profile of v6, /device:TPU:0, one launch (start us, length us, event | category | flops | bytes accessed | tf_op | source)
XLA Modules:
  0.0 31.3 jit_solution(18415744992948089570)
XLA Ops:
  0.6 1.1 %pack.1 = (bf16[528,128]{1,0:T(8,128)(2,1)S(1)}, bf16[528,128]{1,0:T(8,128)(2,1)S(1)}, bf16[272,128]{1,0:T(8,128)(2,1)S(1)}, bf16[272,128]{1,0:T(8,128)(2,1)S(1)}, s32[16,256]{1,0:T(8,128)S(1)}) custom-call(s32[16]{0:T(128)} %request_adapter.1, s32[24]{0:T(128)} %adapter_storage.1, s32[16]{0:T(128)} %lengths.1, bf16[16,2,8192]{2,1,0:T(2,128)(2,1)} %hidden.1), custom_call_target="tpu_custom_call" | custom-call | bytes 1048576 | tf_op jit(solution)/shard_map/pack/pallas_call | solution.py:269
  1.8 4.1 %collective-permute-start.2 = (bf16[272,128]{1,0:T(8,128)(2,1)S(1)}, bf16[272,128]{1,0:T(8,128)(2,1)S(1)}, u32[]{:S(2)}, u32[]{:S(2)}) collective-permute-start(bf16[272,128]{1,0:T(8,128)(2,1)S(1)} %get-tuple-element.34), channel_id=1, source_target_pairs={{0,8},{4,12},{8,0},{12,4},{1,9},{5,13},{9,1},{13,5},{2,10},{6,14},... | collective-permute-start | bytes 208904 | tf_op jit(solution)/shard_map/ppermute | solution.py:263
  5.9 1.3 %collective-permute-start.1 = (bf16[272,128]{1,0:T(8,128)(2,1)S(1)}, bf16[272,128]{1,0:T(8,128)(2,1)S(1)}, u32[]{:S(2)}, u32[]{:S(2)}) collective-permute-start(bf16[272,128]{1,0:T(8,128)(2,1)S(1)} %get-tuple-element.33), channel_id=1, source_target_pairs={{0,12},{4,8},{8,4},{12,0},{1,13},{5,9},{9,5},{13,1},{2,14},{6,10},... | collective-permute-start | bytes 208904 | tf_op jit(solution)/shard_map/ppermute | solution.py:263
  7.2 0.2 collective-permute-start
  7.4 3.1 %copy.16 = bf16[16,256,2,256]{3,1,2,0:T(8,128)(2,1)S(1)} copy(bf16[16,256,2,256]{3,2,1,0:T(2,128)(2,1)} %param.12) | data formatting | bytes 8388608 | tf_op jit(solution)/shard_map/optimization_barrier | solution.py:301
  10.6 2.1 %collective-permute-done.1.refs_3_ = bf16[272,128]{1,0:T(8,128)(2,1)S(1)} collective-permute-done((bf16[272,128]{1,0:T(8,128)(2,1)S(1)}, bf16[272,128]{1,0:T(8,128)(2,1)S(1)}, u32[]{:S(2)}, u32[]{:S(2)}) %collective-permute-start.1) | collective-permute-done | bytes 69664 | tf_op jit(solution)/shard_map/ppermute | solution.py:263
  12.7 0.5 %collective-permute-start.3 = (bf16[272,128]{1,0:T(8,128)(2,1)S(1)}, bf16[272,128]{1,0:T(8,128)(2,1)S(1)}, u32[]{:S(2)}, u32[]{:S(2)}) collective-permute-start(bf16[272,128]{1,0:T(8,128)(2,1)S(1)} %collective-permute-done.2.refs_2_), channel_id=1, source_target_pairs={{0,1},{1,0},{2,3},{3,2},{4,5},{5,4},{6,7},{7,6},{8,9},{9,8},{10,11... | collective-permute-start | bytes 208904 | tf_op jit(solution)/shard_map/ppermute | solution.py:266
  13.3 0.4 %collective-permute-done.refs_1_ = bf16[528,128]{1,0:T(8,128)(2,1)S(1)} collective-permute-done((bf16[528,128]{1,0:T(8,128)(2,1)S(1)}, bf16[528,128]{1,0:T(8,128)(2,1)S(1)}, u32[]{:S(2)}, u32[]{:S(2)}) %collective-permute-start) | collective-permute-done | bytes 135200 | tf_op jit(solution)/shard_map/ppermute | solution.py:263
  13.6 0.4 %collective-permute-done.4.refs_5_ = bf16[272,128]{1,0:T(8,128)(2,1)S(1)} collective-permute-done((bf16[272,128]{1,0:T(8,128)(2,1)S(1)}, bf16[272,128]{1,0:T(8,128)(2,1)S(1)}, u32[]{:S(2)}, u32[]{:S(2)}) %collective-permute-start.4) | collective-permute-done | bytes 69664 | tf_op jit(solution)/shard_map/ppermute | solution.py:266
  14.0 0.2 collective-permute-done.3.refs_4_
  14.2 0.7 %shrink.1 = (bf16[128,128]{1,0:T(8,128)(2,1)S(1)}, f32[128,128]{1,0:T(8,128)S(1)}, f32[8,128]{1,0:T(8,128)S(1)}) custom-call(bf16[528,128]{1,0:T(8,128)(2,1)S(1)} %get-tuple-element.31.refs_0_, bf16[528,128]{1,0:T(8,128)(2,1)S(1)} %collective-permute-done.refs_1_, bf16[272,128]{1,0:T(8,128)(2,1)S(1)} %collective-permute-done.2.refs_2_, ...), custom_call_target="tpu_custom_call" | custom-call | flops 402653184 | bytes 4194304 | tf_op jit(solution)/shard_map/shrink/pallas_call | solution.py:269
  14.8 0.4 %collective-permute-start.5 = (bf16[128,128]{1,0:T(8,128)(2,1)S(1)}, bf16[128,128]{1,0:T(8,128)(2,1)S(1)}, u32[]{:S(2)}, u32[]{:S(2)}) collective-permute-start(bf16[128,128]{1,0:T(8,128)(2,1)S(1)} %get-tuple-element.41), channel_id=1, source_target_pairs={{0,1},{1,5},{2,9},{3,13},{4,0},{5,4},{6,8},{7,12},{8,3},{9,7},{10,... | collective-permute-start | bytes 98312 | tf_op jit(solution)/shard_map/ppermute | solution.py:346
  15.3 3.1 %collective-permute-start.6 = (bf16[128,128]{1,0:T(8,128)(2,1)S(1)}, bf16[128,128]{1,0:T(8,128)(2,1)S(1)}, u32[]{:S(2)}, u32[]{:S(2)}) collective-permute-start(bf16[128,128]{1,0:T(8,128)(2,1)S(1)} %get-tuple-element.41), channel_id=1, source_target_pairs={{0,3},{1,7},{2,11},{3,15},{4,2},{5,6},{6,10},{7,14},{8,1},{9,5},{1... | collective-permute-start | bytes 98312 | tf_op jit(solution)/shard_map/ppermute | solution.py:346
  18.3 0.3 copy.17
  18.6 0.7 %base.1 = (f32[128,512]{1,0:T(8,128)S(1)}, bf16[768,512]{1,0:T(8,128)(2,1)S(1)}, f32[8,128]{1,0:T(8,128)S(1)}) custom-call(bf16[528,128]{1,0:T(8,128)(2,1)S(1)} %get-tuple-element.31.refs_0_, bf16[528,128]{1,0:T(8,128)(2,1)S(1)} %collective-permute-done.refs_1_, bf16[272,128]{1,0:T(8,128)(2,1)S(1)} %collective-permute-done.2.refs_2_, ...), custom_call_target="tpu_custom_call" | custom-call | flops 268435456 | bytes 3145728 | tf_op jit(solution)/shard_map/base/pallas_call | solution.py:269
  19.4 2.6 %collective-permute-done.6 = bf16[128,128]{1,0:T(8,128)(2,1)S(1)} collective-permute-done((bf16[128,128]{1,0:T(8,128)(2,1)S(1)}, bf16[128,128]{1,0:T(8,128)(2,1)S(1)}, u32[]{:S(2)}, u32[]{:S(2)}) %collective-permute-start.6) | collective-permute-done | bytes 32800 | tf_op jit(solution)/shard_map/ppermute | solution.py:346
  22.1 1.2 %collective-permute-done.7.refs_1_ = f32[128,128]{1,0:T(8,128)S(1)} collective-permute-done((f32[128,128]{1,0:T(8,128)S(1)}, f32[128,128]{1,0:T(8,128)S(1)}, u32[]{:S(2)}, u32[]{:S(2)}) %collective-permute-start.7) | collective-permute-done | bytes 65568 | tf_op jit(solution)/shard_map/ppermute | solution.py:266
  23.4 0.3 expand.1
  23.7 2.4 %collective-permute-start.8 = (bf16[32,512]{1,0:T(8,128)(2,1)S(1)}, bf16[32,512]{1,0:T(8,128)(2,1)S(1)}, u32[]{:S(2)}, u32[]{:S(2)}) collective-permute-start(bf16[32,512]{1,0:T(8,128)(2,1)S(1)} %get-tuple-element.50), channel_id=1, source_target_pairs={{0,8},{4,12},{8,0},{12,4},{1,9},{5,13},{9,1},{13,5},{2,10},{6,14},... | collective-permute-start | bytes 98312 | tf_op jit(solution)/shard_map/ppermute | solution.py:361
  26.1 2.2 %collective-permute-start.9 = (bf16[32,512]{1,0:T(8,128)(2,1)S(1)}, bf16[32,512]{1,0:T(8,128)(2,1)S(1)}, u32[]{:S(2)}, u32[]{:S(2)}) collective-permute-start(bf16[32,512]{1,0:T(8,128)(2,1)S(1)} %get-tuple-element.51), channel_id=1, source_target_pairs={{0,12},{4,0},{8,4},{12,8},{1,13},{5,1},{9,5},{13,9},{2,14},{6,2},{... | collective-permute-start | bytes 98312 | tf_op jit(solution)/shard_map/ppermute | solution.py:361
  28.3 1.2 %cached.1 = (f32[512,128]{1,0:T(8,128)S(1)}, f32[512,128]{1,0:T(8,128)S(1)}, f32[512,128]{1,0:T(8,128)S(1)}, f32[512,64]{1,0:T(8,128)S(1)}) custom-call(s32[16,256]{1,0:T(8,128)S(1)} %get-tuple-element.53.spans, bf16[16,2,16,128]{3,2,1,0:T(8,128)(2,1)S(1)} %copy-done.1, bf16[16,2,256,256]{3,2,1,0:T(8,128)(2,1)S(1)} %bitcast.8, f32[8,128]{1,0:T(8,128)S(1)} %get-tuple-element.55._), custom_call_target="tpu_custom_call" | custom-call | flops 134217728 | bytes 4194304 | tf_op jit(solution)/shard_map/cached/pallas_call | solution.py:269
  29.5 0.2 collective-permute-done.10.refs_2_
  29.7 0.3 %collective-permute-done.9.refs_1_ = bf16[32,512]{1,0:T(8,128)(2,1)S(1)} collective-permute-done((bf16[32,512]{1,0:T(8,128)(2,1)S(1)}, bf16[32,512]{1,0:T(8,128)(2,1)S(1)}, u32[]{:S(2)}, u32[]{:S(2)}) %collective-permute-start.9) | collective-permute-done | bytes 32800 | tf_op jit(solution)/shard_map/ppermute | solution.py:361
  30.0 1.2 %finish.1 = (bf16[16,2,2048]{2,1,0:T(2,128)(2,1)}, bf16[16,2,2,256]{3,2,1,0:T(2,128)(2,1)}) custom-call(f32[32,512]{1,0:T(8,128)S(1)} %get-tuple-element.49.own, bf16[32,512]{1,0:T(8,128)(2,1)S(1)} %collective-permute-done.8.refs_0_, bf16[32,512]{1,0:T(8,128)(2,1)S(1)} %collective-permute-done.9.refs_1_, ...), custom_call_target="tpu_custom_call" | custom-call | flops 33554432 | bytes 1048576 | tf_op jit(solution)/shard_map/finish/pallas_call | solution.py:269
  (18 shorter events, 0.2 us)
Async XLA Ops:
  1.8 8.8 %collective-permute-start.2 = (bf16[272,128]{1,0:T(8,128)(2,1)S(1)}, bf16[272,128]{1,0:T(8,128)(2,1)S(1)}, u32[]{:S(2)}, u32[]{:S(2)}) collective-permute-start(bf16[272,128]{1,0:T(8,128)(2,1)S(1)} %get-tuple-element.34), channel_id=1, source_target_pairs={{0,8},{4,12},{8,0},{12,4},{1,9},{5,13},{9,1},{13,5},{2,10},{6,14},... | collective-permute-start | bytes 208904 | tf_op jit(solution)/shard_map/ppermute | solution.py:263
  5.9 6.9 %collective-permute-start.1 = (bf16[272,128]{1,0:T(8,128)(2,1)S(1)}, bf16[272,128]{1,0:T(8,128)(2,1)S(1)}, u32[]{:S(2)}, u32[]{:S(2)}) collective-permute-start(bf16[272,128]{1,0:T(8,128)(2,1)S(1)} %get-tuple-element.33), channel_id=1, source_target_pairs={{0,12},{4,8},{8,4},{12,0},{1,13},{5,9},{9,5},{13,1},{2,14},{6,10},... | collective-permute-start | bytes 208904 | tf_op jit(solution)/shard_map/ppermute | solution.py:263
  7.2 6.4 %collective-permute-start = (bf16[528,128]{1,0:T(8,128)(2,1)S(1)}, bf16[528,128]{1,0:T(8,128)(2,1)S(1)}, u32[]{:S(2)}, u32[]{:S(2)}) collective-permute-start(bf16[528,128]{1,0:T(8,128)(2,1)S(1)} %get-tuple-element.32), channel_id=1, source_target_pairs={{0,4},{4,0},{8,12},{12,8},{1,5},{5,1},{9,13},{13,9},{2,6},{6,2},{1... | collective-permute-start | bytes 405512 | tf_op jit(solution)/shard_map/ppermute | solution.py:263
  7.4 6.7 %copy-start = (bf16[6,2048,128]{2,1,0:T(8,128)(2,1)S(1)}, bf16[6,2048,128]{2,1,0:T(8,128)(2,1)}, u32[]{:S(2)}) copy-start(bf16[6,2048,128]{2,1,0:T(8,128)(2,1)} %refs_6_.1) | copy-start | bytes 9437188
  10.5 7.8 %copy-start.4 = (bf16[2048,2,256]{2,1,0:T(2,128)(2,1)S(1)}, bf16[2048,2,256]{2,1,0:T(2,128)(2,1)}, u32[]{:S(2)}) copy-start(bf16[2048,2,256]{2,1,0:T(2,128)(2,1)} %param.13) | copy-start | bytes 6291460
  10.6 8.0 %copy-start.2 = (bf16[6,64,2,128]{3,2,1,0:T(2,128)(2,1)S(1)}, bf16[6,64,2,128]{3,2,1,0:T(2,128)(2,1)}, u32[]{:S(2)}) copy-start(bf16[6,64,2,128]{3,2,1,0:T(2,128)(2,1)} %refs_7_.1) | copy-start | bytes 589828
  10.6 8.0 %copy-start.3 = (bf16[6,64,2,128]{3,2,1,0:T(2,128)(2,1)S(1)}, bf16[6,64,2,128]{3,2,1,0:T(2,128)(2,1)}, u32[]{:S(2)}) copy-start(bf16[6,64,2,128]{3,2,1,0:T(2,128)(2,1)} %refs_8_.1) | copy-start | bytes 589828
  12.7 1.3 %collective-permute-start.4 = (bf16[272,128]{1,0:T(8,128)(2,1)S(1)}, bf16[272,128]{1,0:T(8,128)(2,1)S(1)}, u32[]{:S(2)}, u32[]{:S(2)}) collective-permute-start(bf16[272,128]{1,0:T(8,128)(2,1)S(1)} %collective-permute-done.1.refs_3_), channel_id=1, source_target_pairs={{0,1},{1,0},{2,3},{3,2},{4,5},{5,4},{6,7},{7,6},{8,9},{9,8},{10,11... | collective-permute-start | bytes 208904 | tf_op jit(solution)/shard_map/ppermute | solution.py:266
  12.7 1.4 %collective-permute-start.3 = (bf16[272,128]{1,0:T(8,128)(2,1)S(1)}, bf16[272,128]{1,0:T(8,128)(2,1)S(1)}, u32[]{:S(2)}, u32[]{:S(2)}) collective-permute-start(bf16[272,128]{1,0:T(8,128)(2,1)S(1)} %collective-permute-done.2.refs_2_), channel_id=1, source_target_pairs={{0,1},{1,0},{2,3},{3,2},{4,5},{5,4},{6,7},{7,6},{8,9},{9,8},{10,11... | collective-permute-start | bytes 208904 | tf_op jit(solution)/shard_map/ppermute | solution.py:266
  14.8 4.5 %collective-permute-start.5 = (bf16[128,128]{1,0:T(8,128)(2,1)S(1)}, bf16[128,128]{1,0:T(8,128)(2,1)S(1)}, u32[]{:S(2)}, u32[]{:S(2)}) collective-permute-start(bf16[128,128]{1,0:T(8,128)(2,1)S(1)} %get-tuple-element.41), channel_id=1, source_target_pairs={{0,1},{1,5},{2,9},{3,13},{4,0},{5,4},{6,8},{7,12},{8,3},{9,7},{10,... | collective-permute-start | bytes 98312 | tf_op jit(solution)/shard_map/ppermute | solution.py:346
  15.3 6.8 %collective-permute-start.6 = (bf16[128,128]{1,0:T(8,128)(2,1)S(1)}, bf16[128,128]{1,0:T(8,128)(2,1)S(1)}, u32[]{:S(2)}, u32[]{:S(2)}) collective-permute-start(bf16[128,128]{1,0:T(8,128)(2,1)S(1)} %get-tuple-element.41), channel_id=1, source_target_pairs={{0,3},{1,7},{2,11},{3,15},{4,2},{5,6},{6,10},{7,14},{8,1},{9,5},{1... | collective-permute-start | bytes 98312 | tf_op jit(solution)/shard_map/ppermute | solution.py:346
  18.6 9.7 %copy-start.1 = (bf16[16,2,16,128]{3,2,1,0:T(8,128)(2,1)S(1)}, bf16[16,2,16,128]{3,2,1,0:T(8,128)(2,1)}, u32[]{:S(2)}) copy-start(bf16[16,2,16,128]{3,2,1,0:T(8,128)(2,1)} %refs_3_.1) | copy-start | bytes 393220
  22.1 1.3 %collective-permute-start.7 = (f32[128,128]{1,0:T(8,128)S(1)}, f32[128,128]{1,0:T(8,128)S(1)}, u32[]{:S(2)}, u32[]{:S(2)}) collective-permute-start(f32[128,128]{1,0:T(8,128)S(1)} %add_add_fusion.refs_0_), channel_id=1, source_target_pairs={{0,1},{1,0},{2,3},{3,2},{4,5},{5,4},{6,7},{7,6},{8,9},{9,8},{10,11... | collective-permute-start | bytes 196616 | tf_op jit(solution)/shard_map/ppermute | solution.py:266
  23.7 6.0 %collective-permute-start.10 = (bf16[32,512]{1,0:T(8,128)(2,1)S(1)}, bf16[32,512]{1,0:T(8,128)(2,1)S(1)}, u32[]{:S(2)}, u32[]{:S(2)}) collective-permute-start(bf16[32,512]{1,0:T(8,128)(2,1)S(1)} %get-tuple-element.52), channel_id=1, source_target_pairs={{0,4},{4,8},{8,12},{12,0},{1,5},{5,9},{9,13},{13,1},{2,6},{6,10},{... | collective-permute-start | bytes 98312 | tf_op jit(solution)/shard_map/ppermute | solution.py:361
  23.7 6.0 %collective-permute-start.8 = (bf16[32,512]{1,0:T(8,128)(2,1)S(1)}, bf16[32,512]{1,0:T(8,128)(2,1)S(1)}, u32[]{:S(2)}, u32[]{:S(2)}) collective-permute-start(bf16[32,512]{1,0:T(8,128)(2,1)S(1)} %get-tuple-element.50), channel_id=1, source_target_pairs={{0,8},{4,12},{8,0},{12,4},{1,9},{5,13},{9,1},{13,5},{2,10},{6,14},... | collective-permute-start | bytes 98312 | tf_op jit(solution)/shard_map/ppermute | solution.py:361
  26.1 3.9 %collective-permute-start.9 = (bf16[32,512]{1,0:T(8,128)(2,1)S(1)}, bf16[32,512]{1,0:T(8,128)(2,1)S(1)}, u32[]{:S(2)}, u32[]{:S(2)}) collective-permute-start(bf16[32,512]{1,0:T(8,128)(2,1)S(1)} %get-tuple-element.51), channel_id=1, source_target_pairs={{0,12},{4,0},{8,4},{12,8},{1,13},{5,1},{9,5},{13,9},{2,14},{6,2},{... | collective-permute-start | bytes 98312 | tf_op jit(solution)/shard_map/ppermute | solution.py:361
